TPU v7x, 32 devices: a whole 2x2x4 slice. The times are simulated.
32 devices in a mesh: rows: 16 (over z, y, x), heads: 2 (over core).
Axes of the slice: x: 2, y: 2, z: 4, core: 2. Of those that a mesh axis runs over, the one named last changes fastest.
Arguments:
- tokens_in: bfloat16 [32768, 384], P('rows')
- neighbours: int32 [32768, 27], P('rows'), may hold values from -129 to 128, as said below
- scene_lengths: int32 [4], replicated, may hold values from 1 to 768, 1024 in all
- window_mask: int32 [32768], P('rows'), may hold values from 0 to 1, as said below
- small_params: float32 [41, 384], replicated
- qkv_weight: bfloat16 [3, 384, 384], P(None, 'heads'), may hold values from -0.3125 to 0.3125
- proj_weight: bfloat16 [384, 384], P('heads'), may hold values from -0.875 to 0.875
- fc1_weight: bfloat16 [1536, 384], P('heads'), may hold values from -0.3125 to 0.3125
- fc2_weight: bfloat16 [1536, 384], P('heads'), may hold values from -0.15625 to 0.15625
- cotangent: float32 [32768, 384], P('rows')
- owners: int32 [144], replicated, may hold values from 0 to 15, as said below
- small_first: float32 [41, 384], replicated
- small_second: float32 [41, 384], replicated
- tile_first: float32 [2, 224, 16, 384], P('heads', 'rows')
- tile_second: float32 [2, 224, 16, 384], P('heads', 'rows')
Outputs:
- output: float32 [32768, 384], P('rows')
- input_grad: float32 [32768, 384], P('rows')
- tile_weight: float32 [2, 224, 16, 384], P('heads', 'rows')
- tile_first_new: float32 [2, 224, 16, 384], P('heads', 'rows')
- tile_second_new: float32 [2, 224, 16, 384], P('heads', 'rows')
- tile_weight_low: bfloat16 [2, 224, 16, 384], P('heads', 'rows')
- small_new: float32 [41, 384], replicated
- small_first_new: float32 [41, 384], replicated
- small_second_new: float32 [41, 384], replicated
Inputs may be any that keep to these rules, and one draw needn't show every extreme that they name: `neighbours`: each entry is -128 - 1 (no neighbour) or an offset of -128 to 128 whose row r plus the offset lies among the nodes; entry 13 is 0; entries 0 and 26 are -128 and 128 where those rows exist. `scene_lengths`: lengths count windows of 32 rows and sum to 1024. `window_mask`: the first row of every window is 1. `owners`: no index of rows owns more than 14 tiles; some index owns exactly 14.
All inputs are finite; a program needn't handle non-finite values.
Results may differ from a plain program's by a relative error of at most 0.0049.
Values may be sent and summed in bfloat16 or wider, within the bound.
A program may use at most 192 MiB of HBM per device.

v0:
```python
import jax
import jax.numpy as jnp
from jax import lax
from jax.sharding import PartitionSpec as P

HEAD_DIM = 32
WIN = 32
HALO = 128
BR = 16
STEP = 3


norm_eps = 1e-05
adam_rate = 0.05
beta_one = 0.5
beta_two = 0.5
adam_eps = 1e-08
decay_rate = 0.05
masked_score = -1e30


def extended_2(x, sides, width):
    for axis, dim in sides:
        size, length = (lax.axis_size(axis), x.shape[dim])
        up = [(i, (i + 1) % size) for i in range(size - 1)]
        down = [(j, i) for i, j in up]
        last = lax.slice_in_dim(x, length - width, length, axis=dim)
        first = lax.slice_in_dim(x, 0, width, axis=dim)
        before = lax.ppermute(last, axis, up)
        after = lax.ppermute(first, axis, down)
        x = jnp.concatenate([before, x, after], axis=dim)
    return x


def scene_index(positions, scene_ends):
    return jnp.sum((positions[..., None] >= scene_ends).astype(jnp.int32), axis=-1)


def layer_norm(values, norm_gain, norm_shift):
    centre = values - jnp.mean(values, axis=1, keepdims=True)
    factor = lax.rsqrt(jnp.mean(centre * centre, axis=1, keepdims=True) + norm_eps)
    unit_part = centre * factor
    return (unit_part * norm_gain + norm_shift, unit_part, factor)


def norm_back(upstream, unit_part, factor, norm_gain):
    scaled = upstream * norm_gain
    return factor * (
        scaled
        - jnp.mean(scaled, axis=1, keepdims=True)
        - unit_part * jnp.mean(scaled * unit_part, axis=1, keepdims=True)
    )


def gelu_value(hidden):
    return 0.5 * hidden * (1.0 + lax.erf(hidden * 0.5**0.5))


def gelu_slope(hidden):
    cumulative = 0.5 * (1.0 + lax.erf(hidden * 0.5**0.5))
    density = jnp.exp(-0.5 * hidden * hidden) * (2.0 * jnp.pi) ** (-0.5)
    return cumulative + hidden * density


def adam_step(weight, gradient, first_moment, second_moment, decay_factor):
    first_new = beta_one * first_moment + (1.0 - beta_one) * gradient
    second_new = beta_two * second_moment + (1.0 - beta_two) * gradient * gradient
    first_hat = first_new / (1.0 - beta_one**STEP)
    second_hat = second_new / (1.0 - beta_two**STEP)
    weight_new = weight - adam_rate * (
        first_hat / (jnp.sqrt(second_hat) + adam_eps) + decay_factor * weight
    )
    return (weight_new, first_new, second_new)


def dot_rows(left_side, right_side):
    return lax.dot_general(
        left_side, right_side, (((0,), (0,)), ((), ())), preferred_element_type=jnp.float32
    )


def dot_cols(left_side, right_side):
    return lax.dot_general(
        left_side, right_side, (((1,), (1,)), ((), ())), preferred_element_type=jnp.float32
    )


def local(
    tokens_in,
    neighbours,
    scene_lengths,
    window_mask,
    small_params,
    qkv_weight,
    proj_weight,
    fc1_weight,
    fc2_weight,
    cotangent,
    owners,
    small_first,
    small_second,
    tile_first,
    tile_second,
):
    rows_here, model_width = tokens_in.shape
    row_count = lax.axis_size("rows")
    pair_count = lax.axis_size("heads")
    row_rank = lax.axis_index("rows")
    head_rank = lax.axis_index("heads")
    half_width = model_width // pair_count
    ffn_half = fc1_weight.shape[0]
    ffn_rows = ffn_half // model_width
    node_total = rows_here * row_count
    att_scale = HEAD_DIM ** (-0.5)
    row_base = row_rank * rows_here
    lead_head = (head_rank == 0).astype(jnp.float32)
    qkv_use, proj_use, fc1_use, fc2_use = (qkv_weight, proj_weight, fc1_weight, fc2_weight)
    conv_start = head_rank * half_width
    ffn_first = 37 + head_rank * ffn_rows
    conv_lead = 1.0
    conv_width = qkv_use.shape[1]
    ffn_units = fc1_use.shape[0]
    ffn_use_rows = ffn_units // model_width
    scene_ends = jnp.cumsum(scene_lengths) * WIN
    local_rows = jnp.arange(rows_here, dtype=jnp.int32)
    own_rows = row_base + local_rows
    target = own_rows[:, None] + neighbours
    inside = (neighbours >= -HALO) & (target >= 0) & (target < node_total)
    usable = inside & (
        scene_index(target, scene_ends) == scene_index(own_rows, scene_ends)[:, None]
    )
    usable = usable.astype(jnp.float32)
    local_index = jnp.clip(neighbours + local_rows[:, None] + HALO, 0, rows_here + 2 * HALO - 1)
    tokens_part = lax.dynamic_slice_in_dim(tokens_in, conv_start, conv_width, 1)
    extended = extended_2(tokens_part, (("rows", 0),), HALO)
    conv_taps = lax.dynamic_slice_in_dim(small_params[:27], conv_start, conv_width, 1)
    filtered = jnp.zeros((rows_here, conv_width), jnp.float32)
    for position in range(27):
        picked = jnp.take(extended, local_index[:, position], axis=0).astype(jnp.float32)
        filtered = filtered + usable[:, position : position + 1] * conv_taps[position] * picked
    stat_sums = lax.psum((jnp.sum(filtered, axis=0), jnp.sum(filtered * filtered, axis=0)), "rows")
    centre = stat_sums[0] / node_total
    spread = stat_sums[1] / node_total - centre * centre
    inv_std = lax.rsqrt(spread + norm_eps)
    bn_norm = (filtered - centre) * inv_std
    bn_gain = lax.dynamic_slice_in_dim(small_params[27], conv_start, conv_width)
    bn_shift = lax.dynamic_slice_in_dim(small_params[28], conv_start, conv_width)
    cpe_part = bn_norm * bn_gain + bn_shift
    cpe_full = lax.all_gather(cpe_part, "heads", axis=1, tiled=True)
    resid = tokens_in.astype(jnp.float32) + cpe_full
    normed_one, unit_one, factor_one = layer_norm(resid, small_params[29], small_params[30])
    normed_one = normed_one.astype(jnp.bfloat16)
    query_bias = lax.dynamic_slice_in_dim(small_params[35], conv_start, conv_width)
    value_bias = lax.dynamic_slice_in_dim(small_params[36], conv_start, conv_width)
    qkv_bias = jnp.stack([query_bias, jnp.zeros_like(query_bias), value_bias])
    projected = jnp.einsum("nd,jcd->jnc", normed_one, qkv_use, preferred_element_type=jnp.float32)
    qkv_low = ((projected + qkv_bias[:, None, :]) * att_scale).astype(jnp.bfloat16)
    heads_here = conv_width // HEAD_DIM
    windows = rows_here // WIN
    shape_four = (windows, WIN, heads_here, HEAD_DIM)
    queries = qkv_low[0].reshape(shape_four)
    key_part = qkv_low[1].reshape(shape_four)
    value_part = qkv_low[2].reshape(shape_four)
    key_keep = window_mask.reshape(windows, 1, 1, WIN) > 0

    def scores_of():
        raw_scores = jnp.einsum(
            "wqhd,wkhd->whqk", queries, key_part, preferred_element_type=jnp.float32
        )
        return jnp.where(key_keep, raw_scores, masked_score)

    scores = scores_of()
    row_top = jnp.max(scores, axis=-1, keepdims=True)
    powers = jnp.exp(scores - row_top)
    row_total = jnp.sum(powers, axis=-1, keepdims=True)
    log_total = row_top + jnp.log(row_total)
    probs_low = (powers / row_total).astype(jnp.bfloat16)
    mixture = jnp.einsum(
        "whqk,wkhd->wqhd", probs_low, value_part, preferred_element_type=jnp.float32
    )
    mixture = mixture.reshape(rows_here, conv_width).astype(jnp.bfloat16)
    proj_term = jnp.dot(mixture, proj_use, preferred_element_type=jnp.float32)
    branch = lax.psum(proj_term, "heads")
    after_attn = resid + (branch + small_params[33])
    normed_two, unit_two, factor_two = layer_norm(after_attn, small_params[31], small_params[32])
    normed_two = normed_two.astype(jnp.bfloat16)
    ffn_bias = lax.dynamic_slice_in_dim(small_params, ffn_first, ffn_use_rows, 0).reshape(ffn_units)
    hidden = dot_cols(normed_two, fc1_use) + ffn_bias
    activation = gelu_value(hidden).astype(jnp.bfloat16)
    ffn_term = jnp.dot(activation, fc2_use, preferred_element_type=jnp.float32)
    ffn_out = lax.psum(ffn_term.astype(jnp.bfloat16), "heads").astype(jnp.float32)
    output_work = after_attn + (ffn_out + small_params[34])
    grad_ffn = cotangent.astype(jnp.bfloat16)
    fc2_grad = dot_rows(activation, grad_ffn)
    fc2_bias_grad = jnp.sum(grad_ffn, axis=0, dtype=jnp.float32)
    grad_hidden = (dot_cols(grad_ffn, fc2_use) * gelu_slope(hidden)).astype(jnp.bfloat16)
    fc1_grad = dot_rows(grad_hidden, normed_two)
    fc1_bias_grad = jnp.sum(grad_hidden, axis=0, dtype=jnp.float32)
    norm_two_term = jnp.dot(grad_hidden, fc1_use, preferred_element_type=jnp.float32)
    grad_normed_two = lax.psum(norm_two_term.astype(jnp.bfloat16), "heads").astype(jnp.float32)
    grad_after = cotangent + norm_back(grad_normed_two, unit_two, factor_two, small_params[31])
    ln_two_gain = jnp.sum(grad_normed_two * unit_two, axis=0)
    ln_two_shift = jnp.sum(grad_normed_two, axis=0)
    grad_branch = grad_after.astype(jnp.bfloat16)
    proj_grad = dot_rows(mixture, grad_branch)
    proj_bias_grad = jnp.sum(grad_branch, axis=0, dtype=jnp.float32)
    grad_mixture = dot_cols(grad_branch, proj_use).astype(jnp.bfloat16).reshape(shape_four)
    scores = scores_of()
    attn_probs = jnp.exp(scores - log_total)
    probs_again = attn_probs.astype(jnp.bfloat16)
    grad_probs = jnp.einsum(
        "wqhd,wkhd->whqk", grad_mixture, value_part, preferred_element_type=jnp.float32
    )
    value_grad = jnp.einsum(
        "whqk,wqhd->wkhd", probs_again, grad_mixture, preferred_element_type=jnp.float32
    )
    grad_scores = attn_probs * (
        grad_probs - jnp.sum(grad_probs * attn_probs, axis=-1, keepdims=True)
    )
    grad_scores = grad_scores.astype(jnp.bfloat16)
    query_grad = jnp.einsum(
        "whqk,wkhd->wqhd", grad_scores, key_part, preferred_element_type=jnp.float32
    )
    key_grad = jnp.einsum(
        "whqk,wqhd->wkhd", grad_scores, queries, preferred_element_type=jnp.float32
    )
    grad_qkv = (
        jnp.stack([query_grad, key_grad, value_grad])
        .reshape(3, rows_here, conv_width)
        .astype(jnp.bfloat16)
    )
    qkv_grad = att_scale * jnp.einsum(
        "jnc,nd->jcd", grad_qkv, normed_one, preferred_element_type=jnp.float32
    )
    qkv_bias_grad = att_scale * jnp.sum(grad_qkv, axis=1, dtype=jnp.float32)
    norm_one_term = att_scale * jnp.einsum(
        "jnc,jcd->nd", grad_qkv, qkv_use, preferred_element_type=jnp.float32
    )
    grad_normed_one = lax.psum(norm_one_term.astype(jnp.bfloat16), "heads").astype(jnp.float32)
    grad_resid = grad_after + norm_back(grad_normed_one, unit_one, factor_one, small_params[29])
    ln_one_gain = jnp.sum(grad_normed_one * unit_one, axis=0)
    ln_one_shift = jnp.sum(grad_normed_one, axis=0)
    grad_cpe = lax.dynamic_slice_in_dim(grad_resid, conv_start, conv_width, 1)
    local_shift = jnp.sum(grad_cpe, axis=0)
    local_gain = jnp.sum(grad_cpe * bn_norm, axis=0)
    shift_total, gain_total = lax.psum((local_shift, local_gain), "rows")
    grad_filtered = (
        bn_gain
        * inv_std
        * (grad_cpe - shift_total / node_total - bn_norm * gain_total / node_total)
    )
    spread_back = jnp.zeros((rows_here + 2 * HALO, conv_width), jnp.float32)
    tap_grads = []
    for position in range(27):
        weighted = usable[:, position : position + 1] * grad_filtered
        picked = jnp.take(extended, local_index[:, position], axis=0).astype(jnp.float32)
        tap_grads.append(jnp.sum(weighted * picked, axis=0))
        spread_back = spread_back.at[local_index[:, position]].add(weighted * conv_taps[position])
    rims = jnp.concatenate([spread_back[:HALO], spread_back[rows_here + HALO :]], axis=0)
    arrived = extended_2(rims.astype(jnp.bfloat16), (("rows", 0),), HALO).astype(rims.dtype)
    conv_back = spread_back[HALO : HALO + rows_here]
    conv_back = conv_back.at[:HALO].add(arrived[:HALO])
    conv_back = conv_back.at[rows_here - HALO :].add(arrived[3 * HALO :])
    input_grad = grad_resid + lax.all_gather(
        conv_back.astype(jnp.bfloat16), "heads", axis=1, tiled=True
    ).astype(conv_back.dtype)
    small_grad = jnp.zeros(small_params.shape, jnp.float32)
    conv_rows = (
        jnp.concatenate([jnp.stack(tap_grads), local_gain[None], local_shift[None]], axis=0)
        * conv_lead
    )
    small_grad = lax.dynamic_update_slice(small_grad, conv_rows, (0, conv_start))
    full_rows = (
        jnp.stack(
            [ln_one_gain, ln_one_shift, ln_two_gain, ln_two_shift, proj_bias_grad, fc2_bias_grad]
        )
        * lead_head
    )
    small_grad = lax.dynamic_update_slice(small_grad, full_rows, (29, 0))
    bias_rows = jnp.stack([qkv_bias_grad[0], qkv_bias_grad[2]])
    small_grad = lax.dynamic_update_slice(small_grad, bias_rows, (35, conv_start))
    small_grad = lax.dynamic_update_slice(
        small_grad, fc1_bias_grad.reshape(ffn_use_rows, model_width), (ffn_first, 0)
    )
    small_grad = lax.psum(small_grad, ("rows", "heads"))
    small_new, small_first_new, small_second_new = adam_step(
        small_params, small_grad, small_first, small_second, 0.0
    )
    tile_count = owners.shape[0]
    slot_cap = tile_first.shape[1]
    tile_order = jnp.arange(tile_count, dtype=jnp.int32)
    same_owner = (owners[:, None] == owners[None, :]) & (tile_order[None, :] < tile_order[:, None])
    rank_in = jnp.sum(same_owner.astype(jnp.int32), axis=1)
    slot_tile = (
        jnp.full((row_count * slot_cap,), -1, jnp.int32)
        .at[owners * slot_cap + rank_in]
        .set(tile_order)
    )
    own_slots = lax.dynamic_slice_in_dim(slot_tile, row_rank * slot_cap, slot_cap)
    slot_live = (own_slots >= 0).astype(jnp.float32)[:, None, None]
    chosen = jnp.clip(own_slots, 0, tile_count - 1)
    grad_stack = jnp.concatenate(
        [qkv_grad.reshape(3 * half_width, model_width), proj_grad, fc1_grad, fc2_grad], axis=0
    )
    grad_stack = grad_stack.reshape(tile_count, BR, model_width)
    summed = lax.psum(grad_stack, "rows")
    tile_grad = jnp.take(summed, chosen, axis=0) * slot_live
    weight_stack = jnp.concatenate(
        [qkv_weight.reshape(3 * half_width, model_width), proj_weight, fc1_weight, fc2_weight],
        axis=0,
    )
    weight_stack = weight_stack.reshape(tile_count, BR, model_width)
    tile_old = jnp.take(weight_stack, chosen, axis=0).astype(jnp.float32)
    new_weight, new_first, new_second = adam_step(
        tile_old, tile_grad, tile_first[0], tile_second[0], decay_rate
    )
    new_weight = new_weight * slot_live
    new_first = new_first * slot_live
    new_second = new_second * slot_live
    return (
        output_work,
        input_grad,
        new_weight[None],
        new_first[None],
        new_second[None],
        new_weight.astype(jnp.bfloat16)[None],
        small_new,
        small_first_new,
        small_second_new,
    )


def solution(mesh):
    return jax.shard_map(
        local,
        mesh=mesh,
        in_specs=(
            P("rows", None),
            P("rows", None),
            P(),
            P("rows"),
            P(),
            P(None, "heads", None),
            P("heads", None),
            P("heads", None),
            P("heads", None),
            P("rows", None),
            P(),
            P(),
            P(),
            P("heads", "rows", None, None),
            P("heads", "rows", None, None),
        ),
        out_specs=(
            P("rows", None),
            P("rows", None),
            P("heads", "rows", None, None),
            P("heads", "rows", None, None),
            P("heads", "rows", None, None),
            P("heads", "rows", None, None),
            P(),
            P(),
            P(),
        ),
        check_vma=False,
    )
```

profile of v0, /device:TPU:0, one launch (start us, length us, event | category | flops | bytes accessed | tf_op | source)
XLA Modules:
  0.0 1189.6 jit_solution(15311319207073779175)
XLA Ops:
  286.1 30.7 %fusion.292 = (f32[192]{0:T(256)}, f32[192]{0:T(256)}, f32[2048,192]{1,0:T(8,128)S(1)}) fusion(bf16[2048,192]{1,0:T(8,128)(2,1)S(1)} %gather_fusion.28, pred[2048]{0:T(1024)(128)(4,1)} %get-tuple-element.268, f32[192]{0:T(256)} %bitcast.373, f32[2048]{0:T(1024)S(1)} %bitcast.253, bf16[2048,192]{1,0:T(8,128)(2,1)} %gather_fusion.27, ...), kind=kLoop, calls=%fused_computation.612 | loop fusion | flops 53870208 | bytes 23105280 | tf_op jit(solution)/shard_map/reduce_sum | solution.py:141
  316.8 43.3 %all-reduce.1 = (f32[192]{0:T(256)S(1)}, f32[192]{0:T(256)S(1)}) all-reduce(f32[192]{0:T(256)} %get-tuple-element.68, f32[192]{0:T(256)} %get-tuple-element.67), channel_id=1, replica_groups=mesh['rows'=16,'heads'=2] {'rows'}, use_global_device_ids=true, to_apply=%region_6.8 | all-reduce | flops 384 | bytes 3072 | tf_op jit(solution)/shard_map/psum | solution.py:141
  433.0 21.4 %all-reduce.8.cloned.1.call-done = f32[2048,384]{1,0:T(8,128)} async-done(((f32[2048,384]{1,0:T(8,128)}), f32[2048,384]{1,0:T(8,128)}) %all-reduce.8.cloned.1.call-update) | async-done | bytes 3145744 | tf_op jit(solution)/shard_map/psum | solution.py:183
  609.8 43.7 %all-reduce = (f32[192]{0:T(256)S(1)}, f32[192]{0:T(256)S(1)}) all-reduce(f32[192]{0:T(256)S(1)} %get-tuple-element.39, f32[192]{0:T(256)S(1)} %get-tuple-element.38), channel_id=1, replica_groups=mesh['rows'=16,'heads'=2] {'rows'}, use_global_device_ids=true, to_apply=%region_25.27 | all-reduce | flops 384 | bytes 3072 | tf_op jit(solution)/shard_map/psum | solution.py:246
  661.3 14.2 %scatter_custom_fusion = f32[2304,192]{1,0:T(8,128)} fusion(s32[2048]{0:T(1024)} %bitcast.457, f32[2048,192]{1,0:T(8,128)S(1)} %get-tuple-element.90, f32[]{:T(128)} %constant.183.clone.1, f32[192]{0:T(256)S(1)} %bitcast.426, f32[2048]{0:T(1024)S(1)} %bitcast.251), kind=kCustom, calls=%fused_computation.297 | custom fusion | flops 1179648 | bytes 3351808 | tf_op jit(solution)/shard_map/scatter-add | solution.py:258
  675.6 15.7 %scatter_custom_fusion.1 = f32[2304,192]{1,0:T(8,128)} fusion(f32[2304,192]{1,0:T(8,128)} %scatter_custom_fusion, s32[2048]{0:T(1024)} %bitcast.456, f32[2048,192]{1,0:T(8,128)S(1)} %get-tuple-element.90, f32[192]{0:T(256)S(1)} %bitcast.424, f32[2048]{0:T(1024)S(1)} %bitcast.239), kind=kCustom, calls=%fused_computation.295 | custom fusion | flops 1179648 | bytes 3351296 | tf_op jit(solution)/shard_map/scatter-add | solution.py:258
  691.3 15.8 %scatter_custom_fusion.2 = f32[2304,192]{1,0:T(8,128)} fusion(f32[2304,192]{1,0:T(8,128)} %scatter_custom_fusion.1, s32[2048]{0:T(1024)} %bitcast.455, f32[2048,192]{1,0:T(8,128)S(1)} %get-tuple-element.90, f32[192]{0:T(256)S(1)} %bitcast.422, f32[2048]{0:T(1024)S(1)} %bitcast.248), kind=kCustom, calls=%fused_computation.293 | custom fusion | flops 1179648 | bytes 3351296 | tf_op jit(solution)/shard_map/scatter-add | solution.py:258
  707.1 15.9 %scatter_custom_fusion.3 = f32[2304,192]{1,0:T(8,128)} fusion(f32[2304,192]{1,0:T(8,128)} %scatter_custom_fusion.2, s32[2048]{0:T(1024)} %bitcast.454, f32[2048,192]{1,0:T(8,128)S(1)} %get-tuple-element.90, f32[192]{0:T(256)S(1)} %bitcast.420, f32[2048]{0:T(1024)S(1)} %bitcast.245), kind=kCustom, calls=%fused_computation.291 | custom fusion | flops 1179648 | bytes 3351296 | tf_op jit(solution)/shard_map/scatter-add | solution.py:258
  723.1 15.8 %scatter_custom_fusion.4 = f32[2304,192]{1,0:T(8,128)} fusion(f32[2304,192]{1,0:T(8,128)} %scatter_custom_fusion.3, s32[2048]{0:T(1024)} %bitcast.453, f32[2048,192]{1,0:T(8,128)S(1)} %get-tuple-element.90, f32[192]{0:T(256)S(1)} %bitcast.418, f32[2048]{0:T(1024)S(1)} %bitcast.242), kind=kCustom, calls=%fused_computation.289 | custom fusion | flops 1179648 | bytes 3351296 | tf_op jit(solution)/shard_map/scatter-add | solution.py:258
  738.9 15.8 %scatter_custom_fusion.5 = f32[2304,192]{1,0:T(8,128)} fusion(f32[2304,192]{1,0:T(8,128)} %scatter_custom_fusion.4, s32[2048]{0:T(1024)} %bitcast.452, f32[2048,192]{1,0:T(8,128)S(1)} %get-tuple-element.90, f32[192]{0:T(256)S(1)} %bitcast.414, f32[2048]{0:T(1024)S(1)} %bitcast.266), kind=kCustom, calls=%fused_computation.287 | custom fusion | flops 1179648 | bytes 3351296 | tf_op jit(solution)/shard_map/scatter-add | solution.py:258
  754.6 15.8 %scatter_custom_fusion.6 = f32[2304,192]{1,0:T(8,128)} fusion(f32[2304,192]{1,0:T(8,128)} %scatter_custom_fusion.5, s32[2048]{0:T(1024)} %bitcast.451, f32[2048,192]{1,0:T(8,128)S(1)} %get-tuple-element.90, f32[192]{0:T(256)S(1)} %bitcast.410, f32[2048]{0:T(1024)S(1)} %bitcast.263), kind=kCustom, calls=%fused_computation.285 | custom fusion | flops 1179648 | bytes 3351296 | tf_op jit(solution)/shard_map/scatter-add | solution.py:258
  770.4 16.1 %scatter_custom_fusion.7 = f32[2304,192]{1,0:T(8,128)} fusion(f32[2304,192]{1,0:T(8,128)} %scatter_custom_fusion.6, s32[2048]{0:T(1024)} %bitcast.450, f32[2048,192]{1,0:T(8,128)S(1)} %get-tuple-element.90, f32[192]{0:T(256)S(1)} %bitcast.406, f32[2048]{0:T(1024)S(1)} %bitcast.260), kind=kCustom, calls=%fused_computation.283 | custom fusion | flops 1179648 | bytes 3351296 | tf_op jit(solution)/shard_map/scatter-add | solution.py:258
  786.5 15.7 %scatter_custom_fusion.8 = f32[2304,192]{1,0:T(8,128)} fusion(f32[2304,192]{1,0:T(8,128)} %scatter_custom_fusion.7, s32[2048]{0:T(1024)} %bitcast.449, f32[2048,192]{1,0:T(8,128)S(1)} %get-tuple-element.90, f32[192]{0:T(256)S(1)} %bitcast.402, f32[2048]{0:T(1024)S(1)} %bitcast.257), kind=kCustom, calls=%fused_computation.281 | custom fusion | flops 1179648 | bytes 3351296 | tf_op jit(solution)/shard_map/scatter-add | solution.py:258
  802.3 15.7 %scatter_custom_fusion.9 = f32[2304,192]{1,0:T(8,128)} fusion(f32[2304,192]{1,0:T(8,128)} %scatter_custom_fusion.8, s32[2048]{0:T(1024)} %bitcast.448, f32[2048,192]{1,0:T(8,128)S(1)} %get-tuple-element.90, f32[192]{0:T(256)S(1)} %bitcast.416, f32[2048]{0:T(1024)S(1)} %bitcast.272), kind=kCustom, calls=%fused_computation.279 | custom fusion | flops 1179648 | bytes 3351296 | tf_op jit(solution)/shard_map/scatter-add | solution.py:258
  818.1 15.7 %scatter_custom_fusion.10 = f32[2304,192]{1,0:T(8,128)} fusion(f32[2304,192]{1,0:T(8,128)} %scatter_custom_fusion.9, s32[2048]{0:T(1024)} %bitcast.447, f32[2048,192]{1,0:T(8,128)S(1)} %get-tuple-element.90, f32[192]{0:T(256)S(1)} %bitcast.412, f32[2048]{0:T(1024)S(1)} %bitcast.290), kind=kCustom, calls=%fused_computation.277 | custom fusion | flops 1179648 | bytes 3351296 | tf_op jit(solution)/shard_map/scatter-add | solution.py:258
  833.8 15.9 %scatter_custom_fusion.11 = f32[2304,192]{1,0:T(8,128)} fusion(f32[2304,192]{1,0:T(8,128)} %scatter_custom_fusion.10, s32[2048]{0:T(1024)} %bitcast.446, f32[2048,192]{1,0:T(8,128)S(1)} %get-tuple-element.90, f32[192]{0:T(256)S(1)} %bitcast.408, f32[2048]{0:T(1024)S(1)} %bitcast.287), kind=kCustom, calls=%fused_computation.275 | custom fusion | flops 1179648 | bytes 3351296 | tf_op jit(solution)/shard_map/scatter-add | solution.py:258
  849.7 15.7 %scatter_custom_fusion.12 = f32[2304,192]{1,0:T(8,128)} fusion(f32[2304,192]{1,0:T(8,128)} %scatter_custom_fusion.11, s32[2048]{0:T(1024)} %bitcast.445, f32[2048,192]{1,0:T(8,128)S(1)} %get-tuple-element.90, f32[192]{0:T(256)S(1)} %bitcast.404, f32[2048]{0:T(1024)S(1)} %bitcast.284), kind=kCustom, calls=%fused_computation.273 | custom fusion | flops 1179648 | bytes 3351296 | tf_op jit(solution)/shard_map/scatter-add | solution.py:258
  865.5 15.7 %scatter_custom_fusion.13 = f32[2304,192]{1,0:T(8,128)} fusion(f32[2304,192]{1,0:T(8,128)} %scatter_custom_fusion.12, s32[2048]{0:T(1024)} %bitcast.444, f32[2048,192]{1,0:T(8,128)S(1)} %get-tuple-element.90, f32[192]{0:T(256)S(1)} %bitcast.400, f32[2048]{0:T(1024)S(1)} %bitcast.281), kind=kCustom, calls=%fused_computation.271 | custom fusion | flops 1179648 | bytes 3351296 | tf_op jit(solution)/shard_map/scatter-add | solution.py:258
  881.3 15.7 %scatter_custom_fusion.14 = f32[2304,192]{1,0:T(8,128)} fusion(f32[2304,192]{1,0:T(8,128)} %scatter_custom_fusion.13, s32[2048]{0:T(1024)} %bitcast.443, f32[2048,192]{1,0:T(8,128)S(1)} %get-tuple-element.90, f32[192]{0:T(256)S(1)} %bitcast.398, f32[2048]{0:T(1024)S(1)} %bitcast.278), kind=kCustom, calls=%fused_computation.269 | custom fusion | flops 1179648 | bytes 3351296 | tf_op jit(solution)/shard_map/scatter-add | solution.py:258
  897.0 15.9 %scatter_custom_fusion.15 = f32[2304,192]{1,0:T(8,128)} fusion(f32[2304,192]{1,0:T(8,128)} %scatter_custom_fusion.14, s32[2048]{0:T(1024)} %bitcast.442, f32[2048,192]{1,0:T(8,128)S(1)} %get-tuple-element.90, f32[192]{0:T(256)S(1)} %bitcast.396, f32[2048]{0:T(1024)S(1)} %bitcast.308), kind=kCustom, calls=%fused_computation.267 | custom fusion | flops 1179648 | bytes 3351296 | tf_op jit(solution)/shard_map/scatter-add | solution.py:258
  913.0 15.7 %scatter_custom_fusion.16 = f32[2304,192]{1,0:T(8,128)} fusion(f32[2304,192]{1,0:T(8,128)} %scatter_custom_fusion.15, s32[2048]{0:T(1024)} %bitcast.441, f32[2048,192]{1,0:T(8,128)S(1)} %get-tuple-element.90, f32[192]{0:T(256)S(1)} %bitcast.394, f32[2048]{0:T(1024)S(1)} %bitcast.305), kind=kCustom, calls=%fused_computation.265 | custom fusion | flops 1179648 | bytes 3351296 | tf_op jit(solution)/shard_map/scatter-add | solution.py:258
  928.7 15.7 %scatter_custom_fusion.17 = f32[2304,192]{1,0:T(8,128)} fusion(f32[2304,192]{1,0:T(8,128)} %scatter_custom_fusion.16, s32[2048]{0:T(1024)} %bitcast.440, f32[2048,192]{1,0:T(8,128)S(1)} %get-tuple-element.90, f32[192]{0:T(256)S(1)} %bitcast.392, f32[2048]{0:T(1024)S(1)} %bitcast.302), kind=kCustom, calls=%fused_computation.263 | custom fusion | flops 1179648 | bytes 3351296 | tf_op jit(solution)/shard_map/scatter-add | solution.py:258
  944.5 15.7 %scatter_custom_fusion.18 = f32[2304,192]{1,0:T(8,128)} fusion(f32[2304,192]{1,0:T(8,128)} %scatter_custom_fusion.17, s32[2048]{0:T(1024)} %bitcast.438, f32[2048,192]{1,0:T(8,128)S(1)} %get-tuple-element.90, f32[192]{0:T(256)S(1)} %bitcast.390, f32[2048]{0:T(1024)S(1)} %bitcast.299), kind=kCustom, calls=%fused_computation.261 | custom fusion | flops 1179648 | bytes 3351296 | tf_op jit(solution)/shard_map/scatter-add | solution.py:258
  960.3 16.1 %scatter_custom_fusion.19 = f32[2304,192]{1,0:T(8,128)} fusion(f32[2304,192]{1,0:T(8,128)} %scatter_custom_fusion.18, s32[2048]{0:T(1024)} %bitcast.437, f32[2048,192]{1,0:T(8,128)S(1)} %get-tuple-element.90, f32[192]{0:T(256)S(1)} %bitcast.388, f32[2048]{0:T(1024)S(1)} %bitcast.296), kind=kCustom, calls=%fused_computation.259 | custom fusion | flops 1179648 | bytes 3351296 | tf_op jit(solution)/shard_map/scatter-add | solution.py:258
  976.4 15.7 %scatter_custom_fusion.20 = f32[2304,192]{1,0:T(8,128)} fusion(f32[2304,192]{1,0:T(8,128)} %scatter_custom_fusion.19, s32[2048]{0:T(1024)} %bitcast.436, f32[2048,192]{1,0:T(8,128)S(1)} %get-tuple-element.90, f32[192]{0:T(256)S(1)} %bitcast.386, f32[2048]{0:T(1024)S(1)} %bitcast.318), kind=kCustom, calls=%fused_computation.257 | custom fusion | flops 1179648 | bytes 3351296 | tf_op jit(solution)/shard_map/scatter-add | solution.py:258
  992.1 15.7 %scatter_custom_fusion.21 = f32[2304,192]{1,0:T(8,128)} fusion(f32[2304,192]{1,0:T(8,128)} %scatter_custom_fusion.20, s32[2048]{0:T(1024)} %bitcast.435, f32[2048,192]{1,0:T(8,128)S(1)} %get-tuple-element.90, f32[192]{0:T(256)S(1)} %bitcast.384, f32[2048]{0:T(1024)S(1)} %bitcast.315), kind=kCustom, calls=%fused_computation.255 | custom fusion | flops 1179648 | bytes 3351296 | tf_op jit(solution)/shard_map/scatter-add | solution.py:258
  1007.9 15.8 %scatter_custom_fusion.22 = f32[2304,192]{1,0:T(8,128)} fusion(f32[2304,192]{1,0:T(8,128)} %scatter_custom_fusion.21, s32[2048]{0:T(1024)} %bitcast.434, f32[2048,192]{1,0:T(8,128)S(1)} %get-tuple-element.90, f32[192]{0:T(256)S(1)} %bitcast.382, f32[2048]{0:T(1024)S(1)} %bitcast.312), kind=kCustom, calls=%fused_computation.253 | custom fusion | flops 1179648 | bytes 3351296 | tf_op jit(solution)/shard_map/scatter-add | solution.py:258
  1023.6 15.9 %scatter_custom_fusion.23 = f32[2304,192]{1,0:T(8,128)} fusion(f32[2304,192]{1,0:T(8,128)} %scatter_custom_fusion.22, s32[2048]{0:T(1024)} %bitcast.433, f32[2048,192]{1,0:T(8,128)S(1)} %get-tuple-element.90, f32[192]{0:T(256)S(1)} %bitcast.380, f32[2048]{0:T(1024)S(1)} %bitcast.293), kind=kCustom, calls=%fused_computation.251 | custom fusion | flops 1179648 | bytes 3351296 | tf_op jit(solution)/shard_map/scatter-add | solution.py:258
  1039.6 15.7 %scatter_custom_fusion.24 = f32[2304,192]{1,0:T(8,128)} fusion(f32[2304,192]{1,0:T(8,128)} %scatter_custom_fusion.23, s32[2048]{0:T(1024)} %bitcast.432, f32[2048,192]{1,0:T(8,128)S(1)} %get-tuple-element.90, f32[192]{0:T(256)S(1)} %bitcast.378, f32[2048]{0:T(1024)S(1)} %bitcast.275), kind=kCustom, calls=%fused_computation.249 | custom fusion | flops 1179648 | bytes 3351296 | tf_op jit(solution)/shard_map/scatter-add | solution.py:258
  1055.3 15.7 %scatter_custom_fusion.25 = f32[2304,192]{1,0:T(8,128)} fusion(f32[2304,192]{1,0:T(8,128)} %scatter_custom_fusion.24, s32[2048]{0:T(1024)} %bitcast.431, f32[2048,192]{1,0:T(8,128)S(1)} %get-tuple-element.90, f32[192]{0:T(256)S(1)} %bitcast.376, f32[2048]{0:T(1024)S(1)} %bitcast.269), kind=kCustom, calls=%fused_computation.247 | custom fusion | flops 1179648 | bytes 3351296 | tf_op jit(solution)/shard_map/scatter-add | solution.py:258
  1071.1 15.7 %scatter_custom_fusion.26 = f32[2304,192]{1,0:T(8,128)} fusion(f32[2304,192]{1,0:T(8,128)} %scatter_custom_fusion.25, s32[2048]{0:T(1024)} %bitcast.439, f32[2048,192]{1,0:T(8,128)S(1)} %get-tuple-element.90, f32[192]{0:T(256)S(1)} %bitcast.374, f32[2048]{0:T(1024)S(1)} %bitcast.254), kind=kCustom, calls=%fused_computation.245 | custom fusion | flops 1179648 | bytes 3351296 | tf_op jit(solution)/shard_map/scatter-add | solution.py:258
  1127.3 38.7 %psum.79 = f32[41,384]{1,0:T(8,128)S(1)} all-reduce(f32[41,384]{1,0:T(8,128)S(1)} %dynamic_update_slice.15), channel_id=1, replica_groups=mesh['rows'=16,'heads'=2] {'rows','heads'}, use_global_device_ids=true, to_apply=%region_91.93 | all-reduce | flops 15744 | bytes 125952 | tf_op jit(solution)/shard_map/psum | solution.py:285
  (681 shorter events, 569.9 us)
Async XLA Ops:
  7.2 367.4 %all-gather.3.cloned.1.call-start = ((), (), s32[]{:S(2)}) async-start(), calls=%async_computation | async-start | bytes 4718592 | tf_op jit(solution)/shard_map/all_gather | solution.py:149
  8.9 34.1 %collective-permute-start = (bf16[128,192]{1,0:T(8,128)(2,1)}, bf16[128,192]{1,0:T(8,128)(2,1)S(1)}, u32[]{:S(2)}, u32[]{:S(2)}) collective-permute-start(bf16[128,192]{1,0:T(8,128)(2,1)} %get-tuple-element.104), channel_id=1, source_target_pairs={{0,2},{2,4},{4,6},{6,8},{8,10},{10,12},{12,14},{14,16},{16,18},{18... | collective-permute-start | bytes 147464 | tf_op jit(solution)/shard_map/ppermute | solution.py:29
  13.9 29.1 %collective-permute-start.1 = (bf16[128,192]{1,0:T(8,128)(2,1)S(1)}, bf16[128,192]{1,0:T(8,128)(2,1)S(1)}, u32[]{:S(2)}, u32[]{:S(2)}) collective-permute-start(bf16[128,192]{1,0:T(8,128)(2,1)S(1)} %get-tuple-element.105), channel_id=1, source_target_pairs={{2,0},{4,2},{6,4},{8,6},{10,8},{12,10},{14,12},{16,14},{18,16},{20... | collective-permute-start | bytes 147464 | tf_op jit(solution)/shard_map/ppermute | solution.py:30
  21.8 264.1 %copy-start.62 = (f32[2048,1]{0,1:T(1,128)}, f32[2048,1]{0,1:T(1,128)S(1)}, u32[]{:S(2)}) copy-start(f32[2048,1]{0,1:T(1,128)S(1)} %get-tuple-element.183) | copy-start | bytes 24580
  21.8 264.1 %copy-start.64 = (f32[2048,1]{0,1:T(1,128)}, f32[2048,1]{0,1:T(1,128)S(1)}, u32[]{:S(2)}) copy-start(f32[2048,1]{0,1:T(1,128)S(1)} %get-tuple-element.188) | copy-start | bytes 24580
  21.8 264.1 %copy-start.66 = (f32[2048,1]{0,1:T(1,128)}, f32[2048,1]{0,1:T(1,128)S(1)}, u32[]{:S(2)}) copy-start(f32[2048,1]{0,1:T(1,128)S(1)} %get-tuple-element.189) | copy-start | bytes 24580
  21.8 264.1 %copy-start.68 = (f32[2048,1]{0,1:T(1,128)}, f32[2048,1]{0,1:T(1,128)S(1)}, u32[]{:S(2)}) copy-start(f32[2048,1]{0,1:T(1,128)S(1)} %get-tuple-element.190) | copy-start | bytes 24580
  21.9 264.1 %copy-start.74 = (f32[2048,1]{0,1:T(1,128)}, f32[2048,1]{0,1:T(1,128)S(1)}, u32[]{:S(2)}) copy-start(f32[2048,1]{0,1:T(1,128)S(1)} %get-tuple-element.184) | copy-start | bytes 24580
  21.9 264.1 %copy-start.76 = (f32[2048,1]{0,1:T(1,128)}, f32[2048,1]{0,1:T(1,128)S(1)}, u32[]{:S(2)}) copy-start(f32[2048,1]{0,1:T(1,128)S(1)} %get-tuple-element.185) | copy-start | bytes 24580
  21.9 264.1 %copy-start.78 = (f32[2048,1]{0,1:T(1,128)}, f32[2048,1]{0,1:T(1,128)S(1)}, u32[]{:S(2)}) copy-start(f32[2048,1]{0,1:T(1,128)S(1)} %get-tuple-element.186) | copy-start | bytes 24580
  21.9 264.1 %copy-start.80 = (f32[2048,1]{0,1:T(1,128)}, f32[2048,1]{0,1:T(1,128)S(1)}, u32[]{:S(2)}) copy-start(f32[2048,1]{0,1:T(1,128)S(1)} %get-tuple-element.187) | copy-start | bytes 24580
  22.6 263.4 %copy-start.70 = (f32[2048,1]{0,1:T(1,128)}, f32[2048,1]{0,1:T(1,128)S(1)}, u32[]{:S(2)}) copy-start(f32[2048,1]{0,1:T(1,128)S(1)} %get-tuple-element.148) | copy-start | bytes 24580
  22.6 263.4 %copy-start.72 = (f32[2048,1]{0,1:T(1,128)}, f32[2048,1]{0,1:T(1,128)S(1)}, u32[]{:S(2)}) copy-start(f32[2048,1]{0,1:T(1,128)S(1)} %get-tuple-element.149) | copy-start | bytes 24580
  22.6 263.4 %copy-start.82 = (f32[2048,1]{0,1:T(1,128)}, f32[2048,1]{0,1:T(1,128)S(1)}, u32[]{:S(2)}) copy-start(f32[2048,1]{0,1:T(1,128)S(1)} %get-tuple-element.150) | copy-start | bytes 24580
  22.7 263.4 %copy-start.84 = (f32[2048,1]{0,1:T(1,128)}, f32[2048,1]{0,1:T(1,128)S(1)}, u32[]{:S(2)}) copy-start(f32[2048,1]{0,1:T(1,128)S(1)} %get-tuple-element.166) | copy-start | bytes 24580
  22.7 263.4 %copy-start.86 = (f32[2048,1]{0,1:T(1,128)}, f32[2048,1]{0,1:T(1,128)S(1)}, u32[]{:S(2)}) copy-start(f32[2048,1]{0,1:T(1,128)S(1)} %get-tuple-element.151) | copy-start | bytes 24580
  22.7 263.4 %copy-start.88 = (f32[2048,1]{0,1:T(1,128)}, f32[2048,1]{0,1:T(1,128)S(1)}, u32[]{:S(2)}) copy-start(f32[2048,1]{0,1:T(1,128)S(1)} %get-tuple-element.161) | copy-start | bytes 24580
  22.7 263.4 %copy-start.90 = (f32[2048,1]{0,1:T(1,128)}, f32[2048,1]{0,1:T(1,128)S(1)}, u32[]{:S(2)}) copy-start(f32[2048,1]{0,1:T(1,128)S(1)} %get-tuple-element.162) | copy-start | bytes 24580
  22.7 263.4 %copy-start.92 = (f32[2048,1]{0,1:T(1,128)}, f32[2048,1]{0,1:T(1,128)S(1)}, u32[]{:S(2)}) copy-start(f32[2048,1]{0,1:T(1,128)S(1)} %get-tuple-element.163) | copy-start | bytes 24580
  22.7 263.4 %copy-start.94 = (f32[2048,1]{0,1:T(1,128)}, f32[2048,1]{0,1:T(1,128)S(1)}, u32[]{:S(2)}) copy-start(f32[2048,1]{0,1:T(1,128)S(1)} %get-tuple-element.164) | copy-start | bytes 24580
  22.7 263.4 %copy-start.96 = (f32[2048,1]{0,1:T(1,128)}, f32[2048,1]{0,1:T(1,128)S(1)}, u32[]{:S(2)}) copy-start(f32[2048,1]{0,1:T(1,128)S(1)} %get-tuple-element.165) | copy-start | bytes 24580
  51.1 235.0 %copy-start.19 = (bf16[2048,192]{1,0:T(8,128)(2,1)}, bf16[2048,192]{1,0:T(8,128)(2,1)S(1)}, u32[]{:S(2)}) copy-start(bf16[2048,192]{1,0:T(8,128)(2,1)S(1)} %gather_fusion.28) | copy-start | bytes 2359300
  366.4 87.9 %all-reduce.8.cloned.1.call-start = ((), (), s32[]{:S(2)}) async-start(), calls=%async_computation.1 | async-start | bytes 6291456 | tf_op jit(solution)/shard_map/psum | solution.py:183
  366.6 48.3 %copy-start.59 = (pred[64,32]{1,0:T(8,128)(4,1)}, pred[64,32]{1,0:T(8,128)(4,1)S(1)}, u32[]{:S(2)}) copy-start(pred[64,32]{1,0:T(8,128)(4,1)S(1)} %gt.16) | copy-start | bytes 6148
  429.8 64.5 %all-reduce.10.cloned.1.call-start = ((), (), s32[]{:S(2)}) async-start(), calls=%async_computation.2 | async-start | bytes 3145728 | tf_op jit(solution)/shard_map/psum | solution.py:200
  472.5 130.2 %all-reduce.14.cloned.1.call-start = ((), (), s32[]{:S(2)}) async-start(), calls=%async_computation.5 | async-start | bytes 6291456 | tf_op jit(solution)/shard_map/psum | solution.py:191
  578.1 594.0 %all-reduce.12.cloned.1.call-start = ((), (), s32[]{:S(2)}) async-start(), calls=%async_computation.4 | async-start | bytes 7077888 | tf_op jit(solution)/shard_map/psum | solution.py:306
  598.3 578.2 %all-gather.5.cloned.1.call-start = ((), (), s32[]{:S(2)}) async-start(), calls=%async_computation.3 | async-start | bytes 2359296 | tf_op jit(solution)/shard_map/all_gather | solution.py:264
  1091.7 19.7 %collective-permute-start.2 = (bf16[128,192]{0,1:T(8,128)(2,1)S(1)}, bf16[128,192]{0,1:T(8,128)(2,1)S(1)}, u32[]{:S(2)}, u32[]{:S(2)}) collective-permute-start(bf16[128,192]{0,1:T(8,128)(2,1)S(1)} %get-tuple-element.106), channel_id=1, source_target_pairs={{0,2},{2,4},{4,6},{6,8},{8,10},{10,12},{12,14},{14,16},{16,18},{18... | collective-permute-start | bytes 147464 | tf_op jit(solution)/shard_map/ppermute | solution.py:29
  1093.1 18.3 %collective-permute-start.3 = (bf16[128,192]{0,1:T(8,128)(2,1)S(1)}, bf16[128,192]{0,1:T(8,128)(2,1)S(1)}, u32[]{:S(2)}, u32[]{:S(2)}) collective-permute-start(bf16[128,192]{0,1:T(8,128)(2,1)S(1)} %get-tuple-element.107), channel_id=1, source_target_pairs={{2,0},{4,2},{6,4},{8,6},{10,8},{12,10},{14,12},{16,14},{18,16},{20... | collective-permute-start | bytes 147464 | tf_op jit(solution)/shard_map/ppermute | solution.py:30
  1113.9 52.2 %copy-start.61 = (f32[41,384]{1,0:T(8,128)S(1)}, f32[41,384]{1,0:T(8,128)}, u32[]{:S(2)}) copy-start(f32[41,384]{1,0:T(8,128)} %param.25) | copy-start | bytes 188932
  1113.9 52.2 %copy-start.114 = (f32[41,384]{1,0:T(8,128)S(1)}, f32[41,384]{1,0:T(8,128)}, u32[]{:S(2)}) copy-start(f32[41,384]{1,0:T(8,128)} %param.32) | copy-start | bytes 188932
  (212 other events, 2063.4 us)
Sparse Core Ops, SparseCore 0:
  366.5 7.9 all-gather.2
  429.9 24.3 all-reduce.7
  472.7 21.5 all-reduce.9
  578.2 24.4 all-reduce.13
  609.3 156.4 all-reduce.11
  1113.9 9.0 all-gather.4
where the time goes:
time: 1200 us; the launch traced here: 1190 us
  other arithmetic  557 us (46%)
  local copies, waits for them, and re-layouts  352 us (29%)
  blocking collectives  126 us (10%)
  matrix products  82.3 us (7%)
  waiting for transfers between devices  46.6 us (4%)
  between operations  16.7 us (1%)
    scatter-add x27, other arithmetic, local(): spread_back.at[local_index[:, position]].add(weighted * conv_taps[position])  425 us
    gather x27, local copies, waits for them, and re-layouts, local(): jnp.take(extended, local_index[:, position], axis=0).astype(jnp.float32)  243 us
    psum x1, blocking collectives, local(): shift_total, gain_total = lax.psum((local_shift, local_gain), 'rows')  43.7 us
    psum x1, blocking collectives, local(): lax.psum((jnp.sum(filtered, axis=0), jnp.sum(filtered * filtered, axis=0)...  43.3 us
    psum x1, blocking collectives, local(): small_grad = lax.psum(small_grad, ('rows', 'heads'))  38.7 us
    reduce_sum x5, other arithmetic, local(): tap_grads.append(jnp.sum(weighted * picked, axis=0))  30.8 us
    reduce_sum x1, other arithmetic, local(): jnp.sum(filtered, axis=0)  30.7 us
  transfers between devices with their start and end apart: 10, of which 4 were waited for; matrix products, arithmetic and copies ran while one was open for 46% of the time, Pallas kernels for 0%

commit v1 on v0

v1 whole, which is shorter than its diff:
```python
import functools

import jax
import jax.numpy as jnp
from jax import lax
from jax.experimental import pallas as pl
from jax.experimental.pallas import tpu as pltpu
from jax.sharding import PartitionSpec as P

HEAD_DIM = 32
WIN = 32
HALO = 128
BR = 16
STEP = 3
TAPS = 27
LANES = 128

norm_eps = 1e-05
adam_rate = 0.05
beta_one = 0.5
beta_two = 0.5
adam_eps = 1e-08
decay_rate = 0.05
masked_score = -1e30

F32 = jnp.float32
BF16 = jnp.bfloat16


def adam_step(weight, gradient, first_moment, second_moment, decay_factor):
    first_new = beta_one * first_moment + (1.0 - beta_one) * gradient
    second_new = beta_two * second_moment + (1.0 - beta_two) * gradient * gradient
    first_hat = first_new / (1.0 - beta_one**STEP)
    second_hat = second_new / (1.0 - beta_two**STEP)
    weight_new = weight - adam_rate * (
        first_hat / (jnp.sqrt(second_hat) + adam_eps) + decay_factor * weight
    )
    return (weight_new, first_new, second_new)


def dot_plain(a, b):
    return jnp.dot(a, b, preferred_element_type=F32)


def dot_last(a, b):
    return lax.dot_general(a, b, (((1,), (1,)), ((), ())), preferred_element_type=F32)


def dot_first(a, b):
    return lax.dot_general(a, b, (((0,), (0,)), ((), ())), preferred_element_type=F32)


def col_sum(v):
    return jnp.sum(v, axis=0, keepdims=True)


def layer_norm(v):
    centre = v - jnp.mean(v, axis=1, keepdims=True)
    factor = lax.rsqrt(jnp.mean(centre * centre, axis=1, keepdims=True) + norm_eps)
    return centre * factor, factor


def norm_back(upstream, unit_part, factor, gain):
    scaled = upstream * gain
    return factor * (
        scaled
        - jnp.mean(scaled, axis=1, keepdims=True)
        - unit_part * jnp.mean(scaled * unit_part, axis=1, keepdims=True)
    )


def full_spec(shape):
    zeros = (0,) * len(shape)
    return pl.BlockSpec(shape, lambda i: zeros)


def filter_kernel(x_ref, near_ref, taps_ref, out_ref, stat_ref, *, block):
    i = pl.program_id(0)
    width = block + 2 * HALO

    @pl.when(i == 0)
    def _():
        stat_ref[...] = jnp.zeros_like(stat_ref)

    window = x_ref[pl.ds(pl.multiple_of(i * block, block), width), :]
    place = lax.broadcasted_iota(jnp.int32, (block, TAPS), 0) + near_ref[...] + HALO
    column = lax.broadcasted_iota(jnp.int32, (block, width), 1)
    total = jnp.zeros(out_ref.shape, F32)
    group = 3
    for first in range(0, TAPS, group):
        hot = jnp.concatenate(
            [
                (place[:, k : k + 1] == column).astype(F32).astype(BF16)
                for k in range(first, first + group)
            ],
            axis=0,
        )
        picked = dot_plain(hot, window)
        for j in range(group):
            total += picked[j * block : (j + 1) * block] * taps_ref[first + j : first + j + 1, :]
    out_ref[...] = total
    stat_ref[0:1, :] += col_sum(total)
    stat_ref[1:2, :] += col_sum(total * total)


def filter_forward(extended, near, taps, block=128):
    rows, width = near.shape[0], extended.shape[1]
    outs = [jax.ShapeDtypeStruct((rows, width), F32), jax.ShapeDtypeStruct((8, width), F32)]
    return pl.pallas_call(
        functools.partial(filter_kernel, block=block),
        grid=(rows // block,),
        in_specs=[
            full_spec(extended.shape),
            pl.BlockSpec((block, TAPS), lambda i: (i, 0)),
            full_spec(taps.shape),
        ],
        out_specs=[pl.BlockSpec((block, width), lambda i: (i, 0)), full_spec(outs[1].shape)],
        out_shape=outs,
        compiler_params=pltpu.CompilerParams(vmem_limit_bytes=40 << 20),
    )(extended, near, taps)


def filter_back_kernel(
    x_ref, filt_ref, dres_ref, near_ref, taps_ref, stat_ref, back_ref, params_ref, out_ref,
    tap_grad_ref, *, block, node_total
):
    i = pl.program_id(0)
    width = block + 2 * HALO

    @pl.when(i == 0)
    def _():
        out_ref[...] = jnp.zeros_like(out_ref)
        tap_grad_ref[...] = jnp.zeros_like(tap_grad_ref)

    centre = stat_ref[0:1] / node_total
    inv_std = lax.rsqrt(stat_ref[1:2] / node_total - centre * centre + norm_eps)
    bn_norm = (filt_ref[...] - centre) * inv_std
    grad = (
        params_ref[27:28]
        * inv_std
        * (
            dres_ref[...]
            - back_ref[1:2] * (1.0 / node_total)
            - bn_norm * (back_ref[0:1] * (1.0 / node_total))
        )
    ).astype(BF16)
    window = pl.ds(pl.multiple_of(i * block, block), width)
    place = lax.broadcasted_iota(jnp.int32, (TAPS, block), 1) + near_ref[...] + HALO
    row = lax.broadcasted_iota(jnp.int32, (width, block), 0)
    tokens = x_ref[window, :].astype(F32)
    total = jnp.zeros(tokens.shape, F32)
    for k in range(TAPS):
        hot = (place[k : k + 1, :] == row).astype(F32).astype(BF16)
        spread = dot_plain(hot, grad)
        total += spread * taps_ref[k : k + 1, :]
        tap_grad_ref[k : k + 1, :] += col_sum(spread * tokens)
    out_ref[window, :] += total


def filter_backward(extended, filtered, dres, near_t, taps, stat, back, params, node_total, block=256):
    rows, width = filtered.shape
    outs = [
        jax.ShapeDtypeStruct((rows + 2 * HALO, width), F32),
        jax.ShapeDtypeStruct((32, width), F32),
    ]
    by_rows = pl.BlockSpec((block, width), lambda i: (i, 0))
    return pl.pallas_call(
        functools.partial(filter_back_kernel, block=block, node_total=node_total),
        grid=(rows // block,),
        in_specs=[
            full_spec(extended.shape),
            by_rows,
            by_rows,
            pl.BlockSpec((TAPS, block), lambda i: (0, i)),
            full_spec(taps.shape),
            full_spec(stat.shape),
            full_spec(back.shape),
            full_spec(params.shape),
        ],
        out_specs=[full_spec(outs[0].shape), full_spec(outs[1].shape)],
        out_shape=outs,
        compiler_params=pltpu.CompilerParams(vmem_limit_bytes=48 << 20),
    )(extended, filtered, dres, near_t, taps, stat, back, params)


def block_kernel(
    filt_ref, tok_ref, mask_ref, cot_ref, stat_ref, params_ref, bias_ref, weight_ref,
    out_ref, dres_ref, grad_ref, small_ref, bias_grad_ref, *, node_total, parts, width, units, block
):
    i = pl.program_id(0)

    @pl.when(i == 0)
    def _():
        grad_ref[...] = jnp.zeros_like(grad_ref)
        small_ref[...] = jnp.zeros_like(small_ref)
        bias_grad_ref[...] = jnp.zeros_like(bias_grad_ref)

    part = width // parts
    unit_part = units // parts
    scale = HEAD_DIM**-0.5

    def weight_rows(low, count):
        return jnp.concatenate([weight_ref[h, low : low + count] for h in range(parts)], axis=0)

    def qkv_rows(j):
        return weight_rows(j * part, part)

    def proj_rows():
        return weight_rows(3 * part, part)

    def add_grad(low, value):
        for h in range(parts):
            grad_ref[h, low : low + part] += value[h * part : (h + 1) * part]

    def param(row):
        return params_ref[row : row + 1, :]

    def add_small(row, value):
        small_ref[row : row + 1, :] += value

    centre = stat_ref[0:1] / node_total
    inv_std = lax.rsqrt(stat_ref[1:2] / node_total - centre * centre + norm_eps)
    bn_norm = (filt_ref[...] - centre) * inv_std
    resid = tok_ref[...].astype(F32) + (bn_norm * param(27) + param(28))
    unit_one, factor_one = layer_norm(resid)
    normed_one = (unit_one * param(29) + param(30)).astype(BF16)
    query = ((dot_last(normed_one, qkv_rows(0)) + param(35)) * scale).astype(BF16)
    key = (dot_last(normed_one, qkv_rows(1)) * scale).astype(BF16)
    value = ((dot_last(normed_one, qkv_rows(2)) + param(36)) * scale).astype(BF16)

    side = LANES
    heads = LANES // HEAD_DIM
    groups = width // LANES
    lane_head = lax.broadcasted_iota(jnp.int32, (side, LANES), 1) // HEAD_DIM
    window_q = lax.broadcasted_iota(jnp.int32, (side, side), 0) // WIN
    window_k = lax.broadcasted_iota(jnp.int32, (side, side), 1) // WIN

    def stack_heads(a):
        return jnp.concatenate(
            [jnp.where(lane_head == j, a, jnp.zeros_like(a)) for j in range(heads)], axis=0
        )

    def pick_heads(a):
        picked = a[:side]
        for j in range(1, heads):
            picked = jnp.where(lane_head == j, a[j * side : (j + 1) * side], picked)
        return picked

    def cut(a, s, g):
        return a[s * side : (s + 1) * side, g * LANES : (g + 1) * LANES]

    kept = {}
    mixture = []
    for s in range(block // side):
        keep = (window_q == window_k) & (mask_ref[0:1, s * side : (s + 1) * side] > 0)
        mixed = []
        for g in range(groups):
            query_g = cut(query, s, g)
            keys = stack_heads(cut(key, s, g))
            values = stack_heads(cut(value, s, g))
            scores = dot_last(query_g, keys)
            probs = []
            for j in range(heads):
                score = jnp.where(keep, scores[:, j * side : (j + 1) * side], masked_score)
                power = jnp.exp(score - jnp.max(score, axis=1, keepdims=True))
                probs.append(power / jnp.sum(power, axis=1, keepdims=True))
            probs = jnp.concatenate(probs, axis=1)
            probs_low = probs.astype(BF16)
            mixed.append(dot_plain(probs_low, values))
            kept[s, g] = (query_g, keys, values, probs, probs_low)
        mixture.append(jnp.concatenate(mixed, axis=1))
    mixture = jnp.concatenate(mixture, axis=0).astype(BF16)
    after = resid + (dot_plain(mixture, proj_rows()) + param(33))
    unit_two, factor_two = layer_norm(after)
    normed_two = (unit_two * param(31) + param(32)).astype(BF16)

    cotangent = cot_ref[...]
    grad_ffn = cotangent.astype(BF16)
    ffn = jnp.zeros_like(after)
    grad_normed_two = jnp.zeros_like(after)
    chunk = unit_part // 2
    for h in range(parts):
        for c in range(2):
            low = 4 * part + c * chunk
            unit = h * unit_part + c * chunk
            fc1 = weight_ref[h, low : low + chunk]
            fc2 = weight_ref[h, low + unit_part : low + unit_part + chunk]
            hidden = dot_last(normed_two, fc1) + bias_ref[0:1, unit : unit + chunk]
            cumulative = 0.5 * (1.0 + lax.erf(hidden * 0.5**0.5))
            activation = (hidden * cumulative).astype(BF16)
            density = jnp.exp(-0.5 * hidden * hidden) * (2.0 * jnp.pi) ** (-0.5)
            ffn += dot_plain(activation, fc2)
            grad_hidden = (
                dot_last(grad_ffn, fc2) * (cumulative + hidden * density)
            ).astype(BF16)
            grad_normed_two += dot_plain(grad_hidden, fc1)
            grad_ref[h, low : low + chunk] += dot_first(grad_hidden, normed_two)
            grad_ref[h, low + unit_part : low + unit_part + chunk] += dot_first(activation, grad_ffn)
            bias_grad_ref[0:1, unit : unit + chunk] += col_sum(grad_hidden.astype(F32))
    out_ref[...] = after + (ffn + param(34))
    add_small(34, col_sum(grad_ffn.astype(F32)))

    grad_after = cotangent + norm_back(grad_normed_two, unit_two, factor_two, param(31))
    add_small(31, col_sum(grad_normed_two * unit_two))
    add_small(32, col_sum(grad_normed_two))
    grad_branch = grad_after.astype(BF16)
    add_grad(3 * part, dot_first(mixture, grad_branch))
    add_small(33, col_sum(grad_branch.astype(F32)))
    grad_mixture = dot_last(grad_branch, proj_rows()).astype(BF16)

    grads = ([], [], [])
    for s in range(block // side):
        here = ([], [], [])
        for g in range(groups):
            query_g, keys, values, probs, probs_low = kept[s, g]
            grad_mix = cut(grad_mixture, s, g)
            grad_probs = dot_last(grad_mix, values)
            grad_scores = []
            for j in range(heads):
                prob = probs[:, j * side : (j + 1) * side]
                term = prob * grad_probs[:, j * side : (j + 1) * side]
                grad_scores.append(
                    (term - prob * jnp.sum(term, axis=1, keepdims=True)).astype(BF16)
                )
            grad_scores = jnp.concatenate(grad_scores, axis=1)
            here[0].append(dot_plain(grad_scores, keys))
            here[1].append(pick_heads(dot_first(grad_scores, query_g)))
            here[2].append(pick_heads(dot_first(probs_low, grad_mix)))
        for kind in range(3):
            grads[kind].append(jnp.concatenate(here[kind], axis=1))
    grad_qkv = [jnp.concatenate(kind, axis=0).astype(BF16) for kind in grads]
    grad_normed_one = jnp.zeros_like(resid)
    for j in range(3):
        grad_normed_one += dot_plain(grad_qkv[j], qkv_rows(j))
        add_grad(j * part, scale * dot_first(grad_qkv[j], normed_one))
    grad_normed_one = scale * grad_normed_one
    add_small(35, scale * col_sum(grad_qkv[0].astype(F32)))
    add_small(36, scale * col_sum(grad_qkv[2].astype(F32)))
    dres = grad_after + norm_back(grad_normed_one, unit_one, factor_one, param(29))
    add_small(29, col_sum(grad_normed_one * unit_one))
    add_small(30, col_sum(grad_normed_one))
    add_small(27, col_sum(dres * bn_norm))
    add_small(28, col_sum(dres))
    dres_ref[...] = dres


def block_step(filtered, tokens, mask, cotangent, stat, params, bias, weights, node_total, block=256):
    rows, width = filtered.shape
    parts, units = weights.shape[0], bias.shape[1]
    outs = [
        jax.ShapeDtypeStruct((rows, width), F32),
        jax.ShapeDtypeStruct((rows, width), F32),
        jax.ShapeDtypeStruct(weights.shape, F32),
        jax.ShapeDtypeStruct(params.shape, F32),
        jax.ShapeDtypeStruct(bias.shape, F32),
    ]
    by_rows = pl.BlockSpec((block, width), lambda i: (i, 0))
    return pl.pallas_call(
        functools.partial(
            block_kernel, node_total=node_total, parts=parts, width=width, units=units, block=block
        ),
        grid=(rows // block,),
        in_specs=[
            by_rows,
            by_rows,
            pl.BlockSpec((1, block), lambda i: (0, i)),
            by_rows,
            full_spec(stat.shape),
            full_spec(params.shape),
            full_spec(bias.shape),
            full_spec(weights.shape),
        ],
        out_specs=[by_rows, by_rows] + [full_spec(o.shape) for o in outs[2:]],
        out_shape=outs,
        compiler_params=pltpu.CompilerParams(vmem_limit_bytes=56 << 20),
    )(filtered, tokens, mask, cotangent, stat, params, bias, weights)


def local(
    tokens_in, neighbours, scene_lengths, window_mask, small_params, qkv_weight, proj_weight,
    fc1_weight, fc2_weight, cotangent, owners, small_first, small_second, tile_first, tile_second
):
    rows_here, width = tokens_in.shape
    row_count = lax.axis_size("rows")
    parts = lax.axis_size("heads")
    row_rank = lax.axis_index("rows")
    part_rank = lax.axis_index("heads")
    rows = rows_here // parts
    node_total = rows_here * row_count
    first = part_rank * rows
    both = ("rows", "heads")

    def own(a):
        return lax.dynamic_slice_in_dim(a, first, rows, 0)

    weight_stack = jnp.concatenate(
        [qkv_weight.reshape(-1, width), proj_weight, fc1_weight, fc2_weight], axis=0
    )
    weights = lax.all_gather(weight_stack, "heads")

    up = [(i, i + 1) for i in range(row_count - 1)]
    down = [(j, i) for i, j in up]
    before = lax.ppermute(tokens_in[rows_here - HALO :], "rows", up)
    after = lax.ppermute(tokens_in[:HALO], "rows", down)
    extended = lax.dynamic_slice_in_dim(
        jnp.concatenate([before, tokens_in, after], axis=0), first, rows + 2 * HALO, 0
    )

    scene_ends = (jnp.cumsum(scene_lengths) * WIN).astype(jnp.int32)
    own_rows = row_rank * rows_here + first + jnp.arange(rows, dtype=jnp.int32)
    passed = scene_ends[None, :] <= own_rows[:, None]
    scene_low = jnp.max(jnp.where(passed, scene_ends[None, :], 0), axis=1)
    scene_high = jnp.min(jnp.where(passed, node_total, scene_ends[None, :]), axis=1)
    near = own(neighbours)
    target = own_rows[:, None] + near
    usable = (near >= -HALO) & (target >= scene_low[:, None]) & (target < scene_high[:, None])
    near = jnp.where(usable, near, -8 * HALO)

    taps = small_params[:TAPS]
    filtered, stat = filter_forward(extended, near, taps)
    stat = lax.psum(stat, both)
    bias = small_params[37:].reshape(1, -1)
    output, dres, weight_grad, small_grad, bias_grad = block_step(
        filtered, own(tokens_in), own(window_mask)[None], own(cotangent), stat, small_params, bias,
        weights, node_total
    )
    output = lax.all_gather(output, "heads", axis=0, tiled=True)
    small_rest = lax.psum(
        jnp.concatenate([small_grad[TAPS:37], bias_grad.reshape(-1, width)], axis=0), both
    )

    conv_back, tap_grad = filter_backward(
        extended, filtered, dres, near.T, taps, stat, small_rest[:8], small_params, node_total
    )
    line = [(i, i + 1) for i in range(row_count * parts - 1)]
    back = [(j, i) for i, j in line]
    rims = conv_back.astype(BF16)
    from_before = lax.ppermute(rims[rows + HALO :], both, line).astype(F32)
    from_after = lax.ppermute(rims[:HALO], both, back).astype(F32)
    input_grad = dres + conv_back[HALO : HALO + rows]
    input_grad = jnp.concatenate(
        [
            input_grad[:HALO] + from_before,
            input_grad[HALO : rows - HALO],
            input_grad[rows - HALO :] + from_after,
        ],
        axis=0,
    )
    input_grad = lax.all_gather(input_grad, "heads", axis=0, tiled=True)

    small_all = jnp.concatenate([lax.psum(tap_grad[:TAPS], both), small_rest], axis=0)
    small_new, small_first_new, small_second_new = adam_step(
        small_params, small_all, small_first, small_second, 0.0
    )

    tile_count = owners.shape[0]
    slot_cap = tile_first.shape[1]
    tile_order = jnp.arange(tile_count, dtype=jnp.int32)
    same_owner = (owners[:, None] == owners[None, :]) & (tile_order[None, :] < tile_order[:, None])
    slot_of = owners * slot_cap + jnp.sum(same_owner.astype(jnp.int32), axis=1)
    slot_ids = jnp.arange(row_count * slot_cap, dtype=jnp.int32)
    found = slot_of[None, :] == slot_ids[:, None]
    slot_tile = jnp.max(jnp.where(found, tile_order[None, :], -1), axis=1)
    live = (slot_tile >= 0).astype(F32)[:, None, None]
    chosen = jnp.clip(slot_tile, 0, tile_count - 1)
    own_grad = lax.psum_scatter(weight_grad, "heads", scatter_dimension=0, tiled=False)
    grad_slots = jnp.take(own_grad.reshape(tile_count, BR, width), chosen, axis=0) * live
    tile_grad = lax.psum_scatter(grad_slots, "rows", scatter_dimension=0, tiled=True)
    own_slots = lax.dynamic_slice_in_dim(chosen, row_rank * slot_cap, slot_cap)
    own_live = lax.dynamic_slice_in_dim(live, row_rank * slot_cap, slot_cap)
    tile_old = jnp.take(weight_stack.reshape(tile_count, BR, width), own_slots, axis=0).astype(F32)
    new_weight, new_first, new_second = adam_step(
        tile_old, tile_grad, tile_first[0], tile_second[0], decay_rate
    )
    new_weight = new_weight * own_live
    new_first = new_first * own_live
    new_second = new_second * own_live
    return (
        output,
        input_grad,
        new_weight[None],
        new_first[None],
        new_second[None],
        new_weight.astype(BF16)[None],
        small_new,
        small_first_new,
        small_second_new,
    )


def solution(mesh):
    return jax.shard_map(
        local,
        mesh=mesh,
        in_specs=(
            P("rows", None),
            P("rows", None),
            P(),
            P("rows"),
            P(),
            P(None, "heads", None),
            P("heads", None),
            P("heads", None),
            P("heads", None),
            P("rows", None),
            P(),
            P(),
            P(),
            P("heads", "rows", None, None),
            P("heads", "rows", None, None),
        ),
        out_specs=(
            P("rows", None),
            P("rows", None),
            P("heads", "rows", None, None),
            P("heads", "rows", None, None),
            P("heads", "rows", None, None),
            P("heads", "rows", None, None),
            P(),
            P(),
            P(),
        ),
        check_vma=False,
    )
```

time: 1200 us -> 390 us (0.33)
  other arithmetic: 557 us -> 20.2 us
  local copies, waits for them, and re-layouts: 352 us -> 27.1 us
  matrix products: 82.3 us -> 0 us
  Pallas kernels: 0 us -> 81.9 us
  waiting for transfers between devices: 46.6 us -> 110 us
    scatter-add x29 -> x0, other arithmetic: 425 us -> none  [the longest x27 425 us: local(): spread_back.at[local_index[:, position]].add(weighted * conv_taps[position])]
    gather x29 -> x2, local copies, waits for them, and re-layouts: 247 us -> 7.61 us  [the longest x1 5.36 us: local(): jnp.take(own_grad.reshape(tile_count, BR, width), chosen, axis=0) * live]
    reduce_scatter x0 -> x2, waiting for transfers between devices: none -> 105 us  [the longest x1 105 us: local(): lax.psum_scatter(grad_slots, 'rows', scatter_dimension=0, tiled=True)]
    dot_general x18 -> x0, matrix products: 82.3 us -> none  [the longest x1 12 us: local(): jnp.einsum('whqk,wqhd->wkhd', probs_again, grad_mixture, preferred_elemen...]
    pallas_call x0 -> x3, Pallas kernels: none -> 81.9 us  [the longest x1 48.4 us: block_step(): pl.pallas_call(functools.partial(block_kernel, node_total=node_total, par...]
    reduce_sum x19 -> x1, other arithmetic: 81.5 us -> 0.19 us  [local(): slot_of = owners * slot_cap + jnp.sum(same_owner.astype(jnp.int32), axis=1)]
    another operation x17 -> x0, local copies, waits for them, and re-layouts: 39.3 us -> none  [the longest x4 17.1 us: local(): jnp.stack([query_grad, key_grad, value_grad])]
    psum x4 -> x0, waiting for transfers between devices: 38.8 us -> none  [the longest x1 21.4 us: local(): branch = lax.psum(proj_term, 'heads')]
  transfers between devices with their start and end apart: 10 -> 9, of which waited for: 4 -> 2; matrix products, arithmetic and copies ran while one was open for 46% -> 8% of each run, Pallas kernels for 0% -> 9%
where the time goes in v1:
time: 390 us
  blocking collectives  126 us (32%)
  waiting for transfers between devices  110 us (28%)
  Pallas kernels  81.9 us (21%)
  local copies, waits for them, and re-layouts  27.1 us (7%)
  other arithmetic  20.2 us (5%)
  between operations  14.1 us (4%)
  starting transfers between devices  10.2 us (3%)
    reduce_scatter x1, waiting for transfers between devices, local(): lax.psum_scatter(grad_slots, 'rows', scatter_dimension=0, tiled=True)  105 us
    pallas_call x1, Pallas kernels, block_step(): pl.pallas_call(functools.partial(block_kernel, node_total=node_total, par...  48.4 us
    psum x1, blocking collectives, local(): lax.psum(tap_grad[:TAPS], both)  43.6 us
    psum x1, blocking collectives, local(): stat = lax.psum(stat, both)  42.5 us
    psum x1, blocking collectives, local(): lax.psum(jnp.concatenate([small_grad[TAPS:37], bias_grad.reshape(-1, widt...  40 us
    pallas_call x1, Pallas kernels, filter_backward(): pl.pallas_call(functools.partial(filter_back_kernel, block=block, node_to...  18.3 us
    pallas_call x1, Pallas kernels, filter_forward(): pl.pallas_call(functools.partial(filter_kernel, block=block), grid=(rows...  15.2 us
    unnamed x38, local copies, waits for them, and re-layouts  13.1 us
  transfers between devices with their start and end apart: 9, of which 2 were waited for; matrix products, arithmetic and copies ran while one was open for 8% of the time, Pallas kernels for 9%

profile of v1, /device:TPU:0, one launch (start us, length us, event | category | flops | bytes accessed | tf_op | source)
XLA Modules:
  0.0 389.6 jit_solution(11384429371342493149)
XLA Ops:
  7.2 2.9 pad_maximum_fusion
  10.3 1.6 fusion.12
  11.9 1.3 collective-permute-start.1
  13.2 6.1 %collective-permute-start = (bf16[128,384]{1,0:T(8,128)(2,1)}, bf16[128,384]{1,0:T(8,128)(2,1)}, u32[]{:S(2)}, u32[]{:S(2)}) collective-permute-start(bf16[128,384]{1,0:T(8,128)(2,1)} %get-tuple-element.39), channel_id=1, source_target_pairs={{0,2},{2,4},{4,6},{6,8},{8,10},{10,12},{12,14},{14,16},{16,18},{18... | collective-permute-start | bytes 294920 | tf_op jit(solution)/shard_map/ppermute | solution.py:403
  20.8 1.0 and_select_fusion
  21.8 1.0 copy.26.near_ref
  22.8 1.3 constant_dynamic-slice_fusion.cot_ref
  24.9 1.0 constant_dynamic-slice_fusion.1.tok_ref
  25.8 2.1 fusion.1.x_ref
  28.0 15.2 %shard_map.214 = (f32[1024,384]{1,0:T(8,128)S(1)}, f32[8,384]{1,0:T(8,128)S(1)}) custom-call(bf16[1280,384]{1,0:T(8,128)(2,1)S(1)} %fusion.1.x_ref, s32[1024,27]{1,0:T(8,128)S(1)} %copy-done.6, f32[27,384]{1,0:T(8,128)S(1)} %slice.41.taps_ref), custom_call_target="tpu_custom_call" | custom-call | tf_op jit(solution)/shard_map/pallas_call | solution.py:109
  44.1 1.1 copy-done.4
  45.2 42.5 %psum.21.stat_ref = f32[8,384]{1,0:T(8,128)} all-reduce(f32[8,384]{1,0:T(8,128)S(1)} %get-tuple-element.19), channel_id=1, replica_groups=mesh['rows'=16,'heads'=2] {'rows','heads'}, use_global_device_ids=true, to_apply=%region_3.4 | all-reduce | flops 3072 | bytes 24576 | tf_op jit(solution)/shard_map/psum | solution.py:421
  87.7 48.4 %shard_map.215 = (f32[1024,384]{1,0:T(8,128)}, f32[1024,384]{1,0:T(8,128)}, f32[2,2304,384]{2,1,0:T(8,128)}, f32[41,384]{1,0:T(8,128)}, f32[1,1536]{1,0:T(1,128)}) custom-call(f32[1024,384]{1,0:T(8,128)} %copy-done.4, bf16[1024,384]{1,0:T(8,128)(2,1)} %constant_dynamic-slice_fusion.1.tok_ref, s32[1,1024]{1,0:T(1,128)} %bitcast.45, ...), custom_call_target="tpu_custom_call" | custom-call | tf_op jit(solution)/shard_map/pallas_call | solution.py:358
  138.7 40.0 %psum.22 = f32[14,384]{1,0:T(8,128)S(1)} all-reduce(f32[14,384]{1,0:T(8,128)S(1)} %pad_maximum_fusion.3), channel_id=1, replica_groups=mesh['rows'=16,'heads'=2] {'rows','heads'}, use_global_device_ids=true, to_apply=%region_4.5 | all-reduce | flops 5376 | bytes 43008 | tf_op jit(solution)/shard_map/psum | solution.py:428
  178.7 1.2 copy-done.2
  179.9 1.4 copy-done.3
  181.3 1.4 copy-done.5
  182.7 18.3 %shard_map.216 = (f32[1280,384]{1,0:T(8,128)}, f32[32,384]{1,0:T(8,128)S(1)}) custom-call(bf16[1280,384]{1,0:T(8,128)(2,1)S(1)} %copy-done.2, f32[1024,384]{1,0:T(8,128)S(1)} %copy-done.5, f32[1024,384]{1,0:T(8,128)S(1)} %copy-done.3, s32[27,1024]{1,0:T(8,128)S(1)} %fusion.14.near_ref, f32[27,384]{1,0:T(8,128)S(1)} %slice.41.taps_ref, ...), custom_call_target="tpu_custom_call" | custom-call | tf_op jit(solution)/shard_map/pallas_call | solution.py:167
  201.1 1.8 convert_element_type.25
  202.9 1.3 collective-permute-start.2
  204.2 1.3 collective-permute-start.3
  205.8 4.1 %collective-permute-done.3 = bf16[128,384]{1,0:T(8,128)(2,1)S(1)} collective-permute-done((bf16[128,384]{1,0:T(8,128)(2,1)S(1)}, bf16[128,384]{1,0:T(8,128)(2,1)S(1)}, u32[]{:S(2)}, u32[]{:S(2)}) %collective-permute-start.3) | collective-permute-done | bytes 98336 | tf_op jit(solution)/shard_map/ppermute | solution.py:439
  209.9 1.2 pad_maximum_fusion.1
  211.7 5.4 %gather_fusion.1 = f32[224,16,384]{2,1,0:T(8,128)} fusion(f32[144,16,384]{2,1,0:T(8,128)} %bitcast.39, s32[1024]{0:T(1024)S(1)} %pad_clamp_fusion), kind=kCustom, calls=%fused_computation.1 | custom fusion | bytes 11010944 | tf_op jit(solution)/shard_map/jit(_take)/gather | solution.py:467
  217.0 5.0 %select_multiply_fusion = f32[224,16,384]{2,1,0:T(8,128)} fusion(f32[224,16,384]{2,1,0:T(8,128)} %gather_fusion.1, f32[224]{0:T(256)S(1)} %get-tuple-element.45, pred[224]{0:T(512)(128)(4,1)S(1)} %get-tuple-element.44), kind=kLoop, calls=%fused_computation.2 | loop fusion | flops 2752512 | bytes 11011168 | tf_op jit(solution)/shard_map/mul | solution.py:467
  222.3 2.3 gather_fusion
  224.5 43.6 %psum.23 = f32[27,384]{1,0:T(8,128)S(1)} all-reduce(f32[27,384]{1,0:T(8,128)S(1)} %bitcast.38), channel_id=1, replica_groups=mesh['rows'=16,'heads'=2] {'rows','heads'}, use_global_device_ids=true, to_apply=%region_9.10 | all-reduce | flops 10368 | bytes 82944 | tf_op jit(solution)/shard_map/psum | solution.py:451
  268.1 1.6 multiply_subtract_fusion
  269.7 105.2 %reduce-scatter.5.cloned.1.call-done = f32[14,16,384]{2,1,0:T(8,128)} async-done(((f32[224,16,384]{2,1,0:T(8,128)}), f32[14,16,384]{2,1,0:T(8,128)}) %reduce-scatter.5.cloned.1.call-update) | async-done | bytes 344080 | tf_op jit(solution)/shard_map/reduce_scatter | solution.py:468
  374.9 2.6 convert_bitcast_fusion
  377.5 3.9 %copy.30 = f32[2048,384]{1,0:T(8,128)} copy(f32[2048,384]{1,0:T(8,128)} %all-gather.5.cloned.1.call-done) | data formatting | bytes 6291456
  381.4 1.7 copy.31
  (75 shorter events, 6.8 us)
Async XLA Ops:
  7.2 15.6 %copy-start = (f32[2048,384]{1,0:T(8,128)S(1)}, f32[2048,384]{1,0:T(8,128)}, u32[]{:S(2)}) copy-start(f32[2048,384]{1,0:T(8,128)} %param.24) | copy-start | bytes 9437188
  7.2 80.5 %all-gather.9.cloned.1.call-start = ((), (), s32[]{:S(2)}) async-start(), calls=%async_computation.6 | async-start | bytes 5308416 | tf_op jit(solution)/shard_map/all_gather | solution.py:399
  10.2 9.1 %copy-start.16 = (s32[4]{0:T(128)S(1)}, s32[4]{0:T(128)}, u32[]{:S(2)}) copy-start(s32[4]{0:T(128)} %param.17) | copy-start | bytes 52
  10.2 9.3 %copy-start.7 = (f32[41,384]{1,0:T(8,128)S(1)}, f32[41,384]{1,0:T(8,128)}, u32[]{:S(2)}) copy-start(f32[41,384]{1,0:T(8,128)} %params_ref.3) | copy-start | bytes 188932
  10.2 9.9 %copy-start.15 = (s32[2048]{0:T(1024)S(1)}, s32[2048]{0:T(1024)}, u32[]{:S(2)}) copy-start(s32[2048]{0:T(1024)} %param.18) | copy-start | bytes 24580
  10.2 201.4 %reduce-scatter.3.cloned.1.call-start = ((), (), s32[]{:S(2)}) async-start(), calls=%async_computation.4 | async-start | bytes 10616832 | tf_op jit(solution)/shard_map/reduce_scatter | solution.py:466
  11.9 13.9 %collective-permute-start.1 = (bf16[128,384]{1,0:T(8,128)(2,1)}, bf16[128,384]{1,0:T(8,128)(2,1)S(1)}, u32[]{:S(2)}, u32[]{:S(2)}) collective-permute-start(bf16[128,384]{1,0:T(8,128)(2,1)} %get-tuple-element.38), channel_id=1, source_target_pairs={{2,0},{4,2},{6,4},{8,6},{10,8},{12,10},{14,12},{16,14},{18,16},{20... | collective-permute-start | bytes 294920 | tf_op jit(solution)/shard_map/ppermute | solution.py:404
  13.2 12.7 %collective-permute-start = (bf16[128,384]{1,0:T(8,128)(2,1)}, bf16[128,384]{1,0:T(8,128)(2,1)}, u32[]{:S(2)}, u32[]{:S(2)}) collective-permute-start(bf16[128,384]{1,0:T(8,128)(2,1)} %get-tuple-element.39), channel_id=1, source_target_pairs={{0,2},{2,4},{4,6},{6,8},{8,10},{10,12},{12,14},{14,16},{16,18},{18... | collective-permute-start | bytes 294920 | tf_op jit(solution)/shard_map/ppermute | solution.py:403
  22.8 2.0 copy-start.11
  24.9 3.1 copy-start.6
  43.1 0.9 copy-start.1
  44.1 1.1 copy-start.4
  136.0 1.8 copy-start.14
  136.1 42.6 %copy-start.8 = (f32[41,384]{1,0:T(8,128)S(1)}, f32[41,384]{1,0:T(8,128)}, u32[]{:S(2)}) copy-start(f32[41,384]{1,0:T(8,128)} %params_ref.3) | copy-start | bytes 188932
  136.1 42.6 %copy-start.9 = (f32[8,384]{1,0:T(8,128)S(1)}, f32[8,384]{1,0:T(8,128)}, u32[]{:S(2)}) copy-start(f32[8,384]{1,0:T(8,128)} %psum.21.stat_ref) | copy-start | bytes 36868
  136.1 133.6 %all-gather.5.cloned.1.call-start = ((), (), s32[]{:S(2)}) async-start(), calls=%async_computation.2 | async-start | bytes 4718592 | tf_op jit(solution)/shard_map/all_gather | solution.py:427
  136.8 132.9 %all-gather.7.cloned.1.call-start = ((), (), s32[]{:S(2)}) async-start(), calls=%async_computation.3 | async-start | bytes 4718592 | tf_op jit(solution)/shard_map/all_gather | solution.py:449
  178.7 1.2 copy-start.2
  179.9 1.4 copy-start.3
  181.3 1.4 copy-start.5
  201.1 4.4 %copy-start.10 = (f32[1280,384]{1,0:T(8,128)S(1)}, f32[1280,384]{1,0:T(8,128)}, u32[]{:S(2)}) copy-start(f32[1280,384]{1,0:T(8,128)} %get-tuple-element.24) | copy-start | bytes 5898244
  202.9 2.9 collective-permute-start.2
  204.2 5.7 %collective-permute-start.3 = (bf16[128,384]{1,0:T(8,128)(2,1)S(1)}, bf16[128,384]{1,0:T(8,128)(2,1)S(1)}, u32[]{:S(2)}, u32[]{:S(2)}) collective-permute-start(bf16[128,384]{1,0:T(8,128)(2,1)S(1)} %get-tuple-element.41), channel_id=1, source_target_pairs={{1,0},{2,1},{3,2},{4,3},{5,4},{6,5},{7,6},{8,7},{9,8},{10,9},{11,1... | collective-permute-start | bytes 294920 | tf_op jit(solution)/shard_map/ppermute | solution.py:439
  209.9 1.3 copy-start.13
  211.2 163.7 %reduce-scatter.5.cloned.1.call-start = ((), (), s32[]{:S(2)}) async-start(), calls=%async_computation.5 | async-start | bytes 5849088 | tf_op jit(solution)/shard_map/reduce_scatter | solution.py:468
  377.5 3.9 %copy-start.12 = (f32[2048,384]{1,0:T(8,128)S(1)}, f32[2048,384]{1,0:T(8,128)}, u32[]{:S(2)}) copy-start(f32[2048,384]{1,0:T(8,128)} %all-gather.7.cloned.1.call-done) | copy-start | bytes 9437188
Sparse Core Ops, SparseCore 0:
  10.3 15.3 all-gather.8
  136.2 15.7 reduce-scatter.2
  153.6 13.2 all-gather.4
  211.3 14.9 all-gather.6
  232.2 142.6 reduce-scatter.4

commit v2 on v1

--- a/solution.py
+++ b/solution.py
@@ -74,118 +74,624 @@
     return pl.BlockSpec(shape, lambda i: zeros)
 
 
-def filter_kernel(x_ref, near_ref, taps_ref, out_ref, stat_ref, *, block):
-    i = pl.program_id(0)
-    width = block + 2 * HALO
-
-    @pl.when(i == 0)
+MESH = pl.DeviceIdType.MESH
+
+
+def device_of(index, parts):
+    return (index // parts, lax.rem(index, parts))
+
+
+def greet_all(count, parts, me):
+    barrier = pltpu.get_barrier_semaphore()
+
+    def greet(j, carry):
+        pl.semaphore_signal(
+            barrier, inc=1, device_id=device_of(lax.rem(me + j, count), parts), device_id_type=MESH
+        )
+        return carry
+
+    lax.fori_loop(1, count, greet, 0)
+
+
+def await_all(count):
+    pl.semaphore_wait(pltpu.get_barrier_semaphore(), count - 1)
+
+
+def swap_copy(source, landing, send_sem, recv_sem, device):
+    return pltpu.make_async_remote_copy(
+        src_ref=source, dst_ref=landing, send_sem=send_sem, recv_sem=recv_sem,
+        device_id=device, device_id_type=MESH,
+    )
+
+
+def send_to_all(source_of, landing, send_sem, recv_sem, count, parts, me):
+    def send(j, carry):
+        other = lax.rem(me + j, count)
+        swap_copy(
+            source_of(other), landing.at[count - j], send_sem.at[j], recv_sem.at[count - j],
+            device_of(other, parts),
+        ).start()
+        return carry
+
+    lax.fori_loop(1, count, send, 0)
+
+
+def await_from_all(source, landing, send_sem, recv_sem, count, parts, me):
+    def wait(j, carry):
+        swap_copy(
+            source, landing.at[count - j], send_sem.at[j], recv_sem.at[count - j],
+            device_of(lax.rem(me + j, count), parts),
+        ).wait()
+        return carry
+
+    lax.fori_loop(1, count, wait, 0)
+
+
+def add_landed(own, landing, count):
+    return lax.fori_loop(1, count, lambda j, total: total + landing[j], own)
+
+
+def to_tile(tile_ref, rows):
+    tile_ref[...] = jnp.zeros_like(tile_ref)
+    groups = rows[0].shape[1] // LANES
+    for r, row in enumerate(rows):
+        for g in range(groups):
+            at = r * groups + g
+            tile_ref[at : at + 1, :] = row[:, g * LANES : (g + 1) * LANES]
+
+
+def from_tile(tile, row, groups):
+    at = row * groups
+    return jnp.concatenate([tile[at + g : at + g + 1, :] for g in range(groups)], axis=1)
+
+
+def filter_kernel(
+    lengths_ref, tokens_ref, near_ref, taps_ref, qkv_ref, proj_ref, fc1_ref, fc2_ref,
+    filt_ref, stat_ref, near_t_ref, ext_ref, stack_ref,
+    place_ref, tile, landed, local_sem, side_sem, weight_sem, send_sem, recv_sem,
+    *, block, row_count, parts, scenes
+):
+    row_rank = lax.axis_index("rows")
+    part_rank = lax.axis_index("heads")
+    count = row_count * parts
+    me = row_rank * parts + part_rank
+    rows_here, width = tokens_ref.shape
+    rows = rows_here // parts
+    part = width // parts
+    first = part_rank * rows
+    node_total = rows_here * row_count
+    greet_all(count, parts, me)
+
+    own_copy = pltpu.make_async_copy(
+        tokens_ref.at[pl.ds(first, rows)], ext_ref.at[pl.ds(HALO, rows)], local_sem.at[0]
+    )
+    near_copy = pltpu.make_async_copy(near_ref.at[pl.ds(first, rows)], place_ref, local_sem.at[1])
+    own_copy.start()
+    near_copy.start()
+    low_side = ext_ref.at[pl.ds(0, HALO)]
+    high_side = ext_ref.at[pl.ds(rows + HALO, HALO)]
+
+    @pl.when(part_rank == 0)
     def _():
-        stat_ref[...] = jnp.zeros_like(stat_ref)
-
-    window = x_ref[pl.ds(pl.multiple_of(i * block, block), width), :]
-    place = lax.broadcasted_iota(jnp.int32, (block, TAPS), 0) + near_ref[...] + HALO
-    column = lax.broadcasted_iota(jnp.int32, (block, width), 1)
-    total = jnp.zeros(out_ref.shape, F32)
-    group = 3
-    for first in range(0, TAPS, group):
-        hot = jnp.concatenate(
-            [
-                (place[:, k : k + 1] == column).astype(F32).astype(BF16)
-                for k in range(first, first + group)
-            ],
-            axis=0,
-        )
-        picked = dot_plain(hot, window)
-        for j in range(group):
-            total += picked[j * block : (j + 1) * block] * taps_ref[first + j : first + j + 1, :]
-    out_ref[...] = total
-    stat_ref[0:1, :] += col_sum(total)
-    stat_ref[1:2, :] += col_sum(total * total)
-
-
-def filter_forward(extended, near, taps, block=128):
-    rows, width = near.shape[0], extended.shape[1]
-    outs = [jax.ShapeDtypeStruct((rows, width), F32), jax.ShapeDtypeStruct((8, width), F32)]
+        pltpu.make_async_copy(tokens_ref.at[pl.ds(rows, HALO)], high_side, local_sem.at[2]).start()
+
+    @pl.when(part_rank == 1)
+    def _():
+        pltpu.make_async_copy(
+            tokens_ref.at[pl.ds(rows - HALO, HALO)], low_side, local_sem.at[2]
+        ).start()
+
+    @pl.when(me == 0)
+    def _():
+        ext_ref[0:HALO, :] = jnp.zeros((HALO, width), BF16)
+
+    @pl.when(me == count - 1)
+    def _():
+        ext_ref[rows + HALO :, :] = jnp.zeros((HALO, width), BF16)
+
+    pieces = []
+    low = 0
+    for j in range(3):
+        pieces.append((qkv_ref.at[j], low, part))
+        low += part
+    for ref in (proj_ref, fc1_ref, fc2_ref):
+        pieces.append((ref, low, ref.shape[0]))
+        low += ref.shape[0]
+    other_core = (row_rank, 1 - part_rank)
+
+    def own_weight(i):
+        ref, at, size = pieces[i]
+        return pltpu.make_async_copy(
+            ref, stack_ref.at[part_rank, pl.ds(at, size)], weight_sem.at[0, i]
+        )
+
+    def sent_weight(i):
+        ref, at, size = pieces[i]
+        return swap_copy(
+            ref, stack_ref.at[part_rank, pl.ds(at, size)], weight_sem.at[1, i],
+            weight_sem.at[2, i], other_core,
+        )
+
+    for i in range(len(pieces)):
+        own_weight(i).start()
+
+    def side_up():
+        return swap_copy(
+            tokens_ref.at[pl.ds(rows_here - HALO, HALO)], low_side, side_sem.at[0], side_sem.at[1],
+            (jnp.minimum(row_rank + 1, row_count - 1), part_rank),
+        )
+
+    def side_down():
+        return swap_copy(
+            tokens_ref.at[pl.ds(0, HALO)], high_side, side_sem.at[0], side_sem.at[1],
+            (jnp.maximum(row_rank - 1, 0), part_rank),
+        )
+
+    stat_ref[...] = jnp.zeros_like(stat_ref)
+    near_copy.wait()
+    own_copy.wait()
+
+    ends = []
+    reached = 0
+    for s in range(scenes):
+        reached = reached + lengths_ref[s]
+        ends.append(reached * WIN)
+
+    blocks = rows // block
+    span = block + 2 * HALO
+
+    def step(it, carry):
+        @pl.when(it == 2)
+        def _():
+            await_all(count)
+
+            @pl.when((part_rank == 0) & (row_rank < row_count - 1))
+            def _():
+                side_up().start()
+
+            @pl.when((part_rank == 1) & (row_rank > 0))
+            def _():
+                side_down().start()
+
+            for i in range(len(pieces)):
+                sent_weight(i).start()
+
+        @pl.when(it == blocks - 2)
+        def _():
+            pltpu.make_async_copy(
+                tokens_ref.at[pl.ds(0, HALO)], low_side, local_sem.at[2]
+            ).wait()
+
+            @pl.when((part_rank == 0) & (row_rank < row_count - 1))
+            def _():
+                side_up().wait_send()
+
+            @pl.when((part_rank == 0) & (row_rank > 0))
+            def _():
+                side_up().wait_recv()
+
+            @pl.when((part_rank == 1) & (row_rank > 0))
+            def _():
+                side_down().wait_send()
+
+            @pl.when((part_rank == 1) & (row_rank < row_count - 1))
+            def _():
+                side_down().wait_recv()
+
+        b = lax.rem(it + 1, blocks)
+        base = pl.multiple_of(b * block, block)
+        window = ext_ref[pl.ds(base, span), :]
+        near = place_ref[pl.ds(base, block), :]
+        own_row = row_rank * rows_here + first + base + lax.broadcasted_iota(
+            jnp.int32, (block, 1), 0
+        )
+        scene_low = jnp.zeros_like(own_row)
+        scene_high = jnp.full_like(own_row, node_total)
+        for end in reversed(ends):
+            passed = own_row >= end
+            scene_low = jnp.maximum(scene_low, jnp.where(passed, end, 0))
+            scene_high = jnp.minimum(scene_high, jnp.where(passed, node_total, end))
+        target = own_row + near
+        usable = (near >= -HALO) & (target >= scene_low) & (target < scene_high)
+        near = jnp.where(usable, near, -8 * HALO)
+        padded = jnp.concatenate(
+            [near, jnp.zeros((block, LANES - TAPS), jnp.int32)], axis=1
+        )
+        near_t_ref[:, pl.ds(base, block)] = jnp.transpose(padded)[: near_t_ref.shape[0]]
+        place = lax.broadcasted_iota(jnp.int32, (block, TAPS), 0) + near + HALO
+        column = lax.broadcasted_iota(jnp.int32, (block, span), 1)
+        total = jnp.zeros((block, width), F32)
+        group = 3
+        for k0 in range(0, TAPS, group):
+            hot = jnp.concatenate(
+                [
+                    (place[:, k : k + 1] == column).astype(F32).astype(BF16)
+                    for k in range(k0, k0 + group)
+                ],
+                axis=0,
+            )
+            picked = dot_plain(hot, window)
+            for j in range(group):
+                total += picked[j * block : (j + 1) * block] * taps_ref[k0 + j : k0 + j + 1, :]
+        filt_ref[pl.ds(base, block), :] = total
+        stat_ref[0:1, :] += col_sum(total)
+        stat_ref[1:2, :] += col_sum(total * total)
+        return carry
+
+    lax.fori_loop(0, blocks, step, 0)
+
+    to_tile(tile, [stat_ref[0:1], stat_ref[1:2]])
+    send_to_all(lambda other: tile, landed, send_sem, recv_sem, count, parts, me)
+    for i in range(len(pieces)):
+        own_weight(i).wait()
+        sent_weight(i).wait()
+    await_from_all(tile, landed, send_sem, recv_sem, count, parts, me)
+    total = add_landed(tile[...], landed, count)
+    groups = width // LANES
+    stat_ref[0:1, :] = from_tile(total, 0, groups)
+    stat_ref[1:2, :] = from_tile(total, 1, groups)
+
+
+def filter_forward(lengths, tokens, near, params, qkv, proj, fc1, fc2, row_count, parts, block=128):
+    rows_here, width = tokens.shape
+    rows = rows_here // parts
+    stack_rows = qkv.shape[0] * qkv.shape[1] + proj.shape[0] + fc1.shape[0] + fc2.shape[0]
+    count = row_count * parts
+    anywhere = pl.BlockSpec(memory_space=pl.ANY)
+    vmem = pl.BlockSpec(memory_space=pltpu.VMEM)
     return pl.pallas_call(
-        functools.partial(filter_kernel, block=block),
-        grid=(rows // block,),
-        in_specs=[
-            full_spec(extended.shape),
-            pl.BlockSpec((block, TAPS), lambda i: (i, 0)),
-            full_spec(taps.shape),
+        functools.partial(
+            filter_kernel, block=block, row_count=row_count, parts=parts, scenes=lengths.shape[0]
+        ),
+        in_specs=[pl.BlockSpec(memory_space=pltpu.SMEM), anywhere, anywhere, vmem] + [anywhere] * 4,
+        out_specs=[vmem, vmem, vmem, vmem, anywhere],
+        out_shape=[
+            jax.ShapeDtypeStruct((rows, width), F32),
+            jax.ShapeDtypeStruct((8, width), F32),
+            jax.ShapeDtypeStruct((32, rows), jnp.int32),
+            jax.ShapeDtypeStruct((rows + 2 * HALO, width), BF16),
+            jax.ShapeDtypeStruct((parts, stack_rows, width), BF16),
         ],
-        out_specs=[pl.BlockSpec((block, width), lambda i: (i, 0)), full_spec(outs[1].shape)],
-        out_shape=outs,
-        compiler_params=pltpu.CompilerParams(vmem_limit_bytes=40 << 20),
-    )(extended, near, taps)
+        scratch_shapes=[
+            pltpu.VMEM((rows, TAPS), jnp.int32),
+            pltpu.VMEM((8, LANES), F32),
+            pltpu.VMEM((count, 8, LANES), F32),
+            pltpu.SemaphoreType.DMA((3,)),
+            pltpu.SemaphoreType.DMA((2,)),
+            pltpu.SemaphoreType.DMA((3, 6)),
+            pltpu.SemaphoreType.DMA((count,)),
+            pltpu.SemaphoreType.DMA((count,)),
+        ],
+        compiler_params=pltpu.CompilerParams(
+            collective_id=0, has_side_effects=True, vmem_limit_bytes=40 << 20
+        ),
+    )(lengths, tokens, near, params, qkv, proj, fc1, fc2)
+
+
+def streams_of(cap, pieces):
+    halves = []
+    middle = (cap + 1) // 2
+    for order, low, high in ((0, 0, middle), (1, middle, cap)):
+        cuts = min(pieces, high - low)
+        edges = [low + (high - low) * i // cuts for i in range(cuts + 1)] if cuts else []
+        halves.append([(order, a, b - a) for a, b in zip(edges[:-1], edges[1:])])
+    return [s for pair in zip(*halves) for s in pair] + halves[0][len(halves[1]) :]
+
+
+def bits_of(row_count, order):
+    bits = list(range(row_count.bit_length() - 1))
+    if order and len(bits) > 1:
+        bits[0], bits[1] = bits[1], bits[0]
+    return bits
+
+
+def flip(rank, bit):
+    weight = 1 << bit
+    return rank + weight - 2 * weight * lax.rem(rank // weight, 2)
 
 
 def filter_back_kernel(
-    x_ref, filt_ref, dres_ref, near_ref, taps_ref, stat_ref, back_ref, params_ref, out_ref,
-    tap_grad_ref, *, block, node_total
+    slot_ref, ext_ref, filt_ref, dres_ref, near_t_ref, params_ref, stat_ref, small_ref, bias_ref,
+    own_ref, peer_ref,
+    back_ref, small_out_ref, tile_out_ref, *scratch,
+    block, row_count, parts, cap, streams, node_total
 ):
-    i = pl.program_id(0)
-    width = block + 2 * HALO
-
-    @pl.when(i == 0)
-    def _():
-        out_ref[...] = jnp.zeros_like(out_ref)
-        tap_grad_ref[...] = jnp.zeros_like(tap_grad_ref)
-
+    wide = len(streams)
+    sums, staged, arrived = scratch[:wide], scratch[wide : 2 * wide], scratch[2 * wide : 3 * wide]
+    (
+        total_ref, grad_ref, rim_ref, rim_in, pair_in, tile, landed, flat, flat_in, part_sum,
+        flat_all, pair_sem, sum_send, sum_recv, tree_send, tree_recv, rim_sem, flat_send, flat_recv,
+        all_send, all_recv, out_sem,
+    ) = scratch[3 * wide :]
+    row_rank = lax.axis_index("rows")
+    part_rank = lax.axis_index("heads")
+    count = row_count * parts
+    me = row_rank * parts + part_rank
+    rows, width = filt_ref.shape
+    groups = width // LANES
+    first = part_rank * rows
+    depth = row_count.bit_length() - 1
+    other_core = (row_rank, 1 - part_rank)
+    small_rows = params_ref.shape[0]
+    bias_rows = bias_ref.shape[1] // width
+
+    greet_all(count, parts, me)
+    to_tile(tile, [small_ref[27:28], small_ref[28:29]])
+    total_ref[...] = jnp.zeros_like(total_ref)
+    small_out_ref[...] = jnp.zeros_like(small_out_ref)
+    await_all(count)
+    send_to_all(lambda other: tile, landed, sum_send, sum_recv, count, parts, me)
+    pair_copy = swap_copy(peer_ref, pair_in, pair_sem.at[0], pair_sem.at[1], other_core)
+    pair_copy.start()
+
+    keep_at = {}
+    for i, (order, _, size) in enumerate(streams):
+        keep_at[i, 0] = 0
+        for t, bit in enumerate(bits_of(row_count, order)):
+            half = (row_count >> (t + 1)) * size
+            keep_at[i, t + 1] = keep_at[i, t] + lax.rem(row_rank // (1 << bit), 2) * half
+
+    def pack(i):
+        order, low, size = streams[i]
+        bits = bits_of(row_count, order)
+
+        def body(p, carry):
+            owner = 0
+            for t, bit in enumerate(bits):
+                owner = owner + lax.rem(p // (1 << (depth - 1 - t)), 2) * (1 << bit)
+            for c in range(size):
+                tile_id = slot_ref[owner * cap + low + c]
+                at = jnp.maximum(tile_id, 0)
+                value = own_ref[at] + pair_in[at].astype(F32)
+                sums[i][p * size + c] = jnp.where(tile_id >= 0, value, 0.0)
+            return carry
+
+        lax.fori_loop(0, row_count, body, 0)
+
+    def tree_copy(i, t):
+        order, _, size = streams[i]
+        half = (row_count >> (t + 1)) * size
+        at = (row_count - (row_count >> t)) * size
+        return swap_copy(
+            staged[i].at[pl.ds(at, half)], arrived[i].at[pl.ds(at, half)], tree_send.at[i, t],
+            tree_recv.at[i, t], (flip(row_rank, bits_of(row_count, order)[t]), part_rank),
+        )
+
+    def tree_start(i, t):
+        order, _, size = streams[i]
+        half = row_count >> (t + 1)
+        at = (row_count - (row_count >> t)) * size
+        give = keep_at[i, t] * 2 + half * size - keep_at[i, t + 1]
+
+        def body(p, carry):
+            for c in range(size):
+                staged[i][at + p * size + c] = sums[i][give + p * size + c].astype(BF16)
+            return carry
+
+        lax.fori_loop(0, half, body, 0)
+        tree_copy(i, t).start()
+
+    def tree_end(i, t):
+        _, _, size = streams[i]
+        half = row_count >> (t + 1)
+        at = (row_count - (row_count >> t)) * size
+        tree_copy(i, t).wait()
+
+        def body(p, carry):
+            for c in range(size):
+                k = keep_at[i, t + 1] + p * size + c
+                sums[i][k] = sums[i][k] + arrived[i][at + p * size + c].astype(F32)
+            return carry
+
+        lax.fori_loop(0, half, body, 0)
+
+    def tree_step(i, t):
+        tree_end(i, t)
+        if t + 1 < depth:
+            tree_start(i, t + 1)
+
+    pair_copy.wait()
+    for i in range(wide):
+        pack(i)
+        tree_start(i, 0)
+
+    await_from_all(tile, landed, sum_send, sum_recv, count, parts, me)
+    back = add_landed(tile[...], landed, count)
+    gain_mean = from_tile(back, 0, groups) * (1.0 / node_total)
+    shift_mean = from_tile(back, 1, groups) * (1.0 / node_total)
     centre = stat_ref[0:1] / node_total
     inv_std = lax.rsqrt(stat_ref[1:2] / node_total - centre * centre + norm_eps)
-    bn_norm = (filt_ref[...] - centre) * inv_std
-    grad = (
-        params_ref[27:28]
-        * inv_std
-        * (
-            dres_ref[...]
-            - back_ref[1:2] * (1.0 / node_total)
-            - bn_norm * (back_ref[0:1] * (1.0 / node_total))
-        )
+    factor = params_ref[27:28] * inv_std
+    grad_ref[...] = (
+        factor * (dres_ref[...] - shift_mean - (filt_ref[...] - centre) * inv_std * gain_mean)
     ).astype(BF16)
-    window = pl.ds(pl.multiple_of(i * block, block), width)
-    place = lax.broadcasted_iota(jnp.int32, (TAPS, block), 1) + near_ref[...] + HALO
-    row = lax.broadcasted_iota(jnp.int32, (width, block), 0)
-    tokens = x_ref[window, :].astype(F32)
-    total = jnp.zeros(tokens.shape, F32)
-    for k in range(TAPS):
-        hot = (place[k : k + 1, :] == row).astype(F32).astype(BF16)
-        spread = dot_plain(hot, grad)
-        total += spread * taps_ref[k : k + 1, :]
-        tap_grad_ref[k : k + 1, :] += col_sum(spread * tokens)
-    out_ref[window, :] += total
-
-
-def filter_backward(extended, filtered, dres, near_t, taps, stat, back, params, node_total, block=256):
+
+    blocks = rows // block
+    span = block + 2 * HALO
+    has_before = me > 0
+    has_after = me < count - 1
+
+    def rim_low():
+        return swap_copy(
+            rim_ref.at[0], rim_in.at[1], rim_sem.at[0, 0], rim_sem.at[1, 1],
+            device_of(jnp.maximum(me - 1, 0), parts),
+        )
+
+    def rim_high():
+        return swap_copy(
+            rim_ref.at[1], rim_in.at[0], rim_sem.at[0, 1], rim_sem.at[1, 0],
+            device_of(jnp.minimum(me + 1, count - 1), parts),
+        )
+
+    def finish_rows(low, size):
+        back_ref[pl.ds(first + low, size), :] = total_ref[HALO + low : HALO + low + size].astype(BF16)
+
+    late = rows - 384
+
+    def out_copy(i):
+        low, size = ((late, rows - late), (0, late))[i]
+        here = back_ref.at[pl.ds(first + low, size)]
+        return swap_copy(here, here, out_sem.at[0, i], out_sem.at[1, i], other_core)
+
+    schedule = [[] for _ in range(blocks)]
+    for i in range(wide):
+        for t in range(depth):
+            schedule[min(i // 2 + t, blocks - 1)].append((t, i))
+
+    def step(it, carry):
+        b = lax.rem(it * (blocks - 1), blocks)
+        base = pl.multiple_of(b * block, block)
+        window = pl.ds(base, span)
+        place = lax.broadcasted_iota(jnp.int32, (TAPS, block), 1) + HALO + (
+            near_t_ref[:, pl.ds(base, block)][:TAPS]
+        )
+        row = lax.broadcasted_iota(jnp.int32, (span, block), 0)
+        tokens = ext_ref[window, :].astype(F32)
+        grad = grad_ref[pl.ds(base, block), :]
+        total = jnp.zeros((span, width), F32)
+        for k in range(TAPS):
+            hot = (place[k : k + 1, :] == row).astype(F32).astype(BF16)
+            spread = dot_plain(hot, grad)
+            total += spread * params_ref[k : k + 1, :]
+            small_out_ref[k : k + 1, :] += col_sum(spread * tokens)
+        total_ref[window, :] += total
+
+        @pl.when(it == 1)
+        def _():
+            rim_ref[0] = total_ref[0:HALO].astype(BF16)
+            rim_ref[1] = total_ref[rows + HALO : rows + 2 * HALO].astype(BF16)
+
+            @pl.when(has_before)
+            def _():
+                rim_low().start()
+
+            @pl.when(has_after)
+            def _():
+                rim_high().start()
+
+        @pl.when(it == 2)
+        def _():
+            @pl.when(has_before)
+            def _():
+                rim_low().wait_send()
+                rim_high().wait_recv()
+                total_ref[HALO : 2 * HALO] += rim_in[0].astype(F32)
+
+            @pl.when(has_after)
+            def _():
+                rim_high().wait_send()
+                rim_low().wait_recv()
+                total_ref[rows : rows + HALO] += rim_in[1].astype(F32)
+
+            finish_rows(late, rows - late)
+            out_copy(0).start()
+
+        for s in range(blocks - 1):
+
+            @pl.when(it == s)
+            def _(s=s):
+                for t, i in sorted(schedule[s]):
+                    tree_step(i, t)
+
+        return carry
+
+    lax.fori_loop(0, blocks, step, 0)
+
+    flat[...] = jnp.zeros_like(flat)
+    for r in range(small_rows):
+        if r < TAPS:
+            row = small_out_ref[r : r + 1, :]
+        elif r < small_rows - bias_rows:
+            row = small_ref[r : r + 1, :]
+        else:
+            at = (r - small_rows + bias_rows) * width
+            row = bias_ref[0:1, at : at + width]
+        for g in range(groups):
+            at = r * groups + g
+            flat[at // 8, at % 8 : at % 8 + 1, :] = row[:, g * LANES : (g + 1) * LANES]
+    send_to_all(lambda other: flat.at[other], flat_in, flat_send, flat_recv, count, parts, me)
+    finish_rows(0, late)
+    out_copy(1).start()
+    await_from_all(flat.at[0], flat_in, flat_send, flat_recv, count, parts, me)
+    part_sum[...] = add_landed(flat[me], flat_in, count)
+    send_to_all(lambda other: part_sum, flat_all, all_send, all_recv, count, parts, me)
+    for t, i in sorted(schedule[blocks - 1]):
+        tree_step(i, t)
+    for i, (_, low, size) in enumerate(streams):
+        for c in range(size):
+            tile_out_ref[low + c] = sums[i][keep_at[i, depth] + c]
+    await_from_all(part_sum, flat_all, all_send, all_recv, count, parts, me)
+    flat_all[0] = part_sum[...]
+    for r in range(small_rows):
+        for g in range(groups):
+            at = r * groups + g
+            tile_at = lax.rem(at // 8 - me + count, count)
+            small_out_ref[r : r + 1, g * LANES : (g + 1) * LANES] = flat_all[
+                tile_at, at % 8 : at % 8 + 1, :
+            ]
+    out_copy(0).wait()
+    out_copy(1).wait()
+
+
+def filter_backward(
+    slots, extended, filtered, dres, near_t, params, stat, small, bias, own_grad, peer_grad, cap,
+    row_count, parts, block=256, pieces=3
+):
     rows, width = filtered.shape
-    outs = [
-        jax.ShapeDtypeStruct((rows + 2 * HALO, width), F32),
-        jax.ShapeDtypeStruct((32, width), F32),
-    ]
-    by_rows = pl.BlockSpec((block, width), lambda i: (i, 0))
+    count = row_count * parts
+    depth = row_count.bit_length() - 1
+    streams = streams_of(cap, pieces)
+    wide = len(streams)
+    vmem = pl.BlockSpec(memory_space=pltpu.VMEM)
+    by_owner = [row_count * size for _, _, size in streams]
+    dma = pltpu.SemaphoreType.DMA
     return pl.pallas_call(
-        functools.partial(filter_back_kernel, block=block, node_total=node_total),
-        grid=(rows // block,),
-        in_specs=[
-            full_spec(extended.shape),
-            by_rows,
-            by_rows,
-            pl.BlockSpec((TAPS, block), lambda i: (0, i)),
-            full_spec(taps.shape),
-            full_spec(stat.shape),
-            full_spec(back.shape),
-            full_spec(params.shape),
+        functools.partial(
+            filter_back_kernel, block=block, row_count=row_count, parts=parts, cap=cap,
+            streams=streams, node_total=rows * count,
+        ),
+        in_specs=[pl.BlockSpec(memory_space=pltpu.SMEM)] + [vmem] * 10,
+        out_specs=[vmem] * 3,
+        out_shape=[
+            jax.ShapeDtypeStruct((rows * parts, width), BF16),
+            jax.ShapeDtypeStruct(params.shape, F32),
+            jax.ShapeDtypeStruct((cap, BR, width), F32),
         ],
-        out_specs=[full_spec(outs[0].shape), full_spec(outs[1].shape)],
-        out_shape=outs,
-        compiler_params=pltpu.CompilerParams(vmem_limit_bytes=48 << 20),
-    )(extended, filtered, dres, near_t, taps, stat, back, params)
+        scratch_shapes=[pltpu.VMEM((n, BR, width), F32) for n in by_owner]
+        + [pltpu.VMEM((n, BR, width), BF16) for n in by_owner] * 2
+        + [
+            pltpu.VMEM((rows + 2 * HALO, width), F32),
+            pltpu.VMEM((rows, width), BF16),
+            pltpu.VMEM((2, HALO, width), BF16),
+            pltpu.VMEM((2, HALO, width), BF16),
+            pltpu.VMEM(peer_grad.shape, BF16),
+            pltpu.VMEM((8, LANES), F32),
+            pltpu.VMEM((count, 8, LANES), F32),
+            pltpu.VMEM((count, 8, LANES), F32),
+            pltpu.VMEM((count, 8, LANES), F32),
+            pltpu.VMEM((8, LANES), F32),
+            pltpu.VMEM((count, 8, LANES), F32),
+            dma((2,)),
+            dma((count,)),
+            dma((count,)),
+            dma((wide, depth)),
+            dma((wide, depth)),
+            dma((2, 2)),
+            dma((count,)),
+            dma((count,)),
+            dma((count,)),
+            dma((count,)),
+            dma((2, 2)),
+        ],
+        compiler_params=pltpu.CompilerParams(
+            collective_id=1, has_side_effects=True, vmem_limit_bytes=58 << 20
+        ),
+    )(slots, extended, filtered, dres, near_t, params, stat, small, bias, own_grad, peer_grad)
 
 
 def block_kernel(
     filt_ref, tok_ref, mask_ref, cot_ref, stat_ref, params_ref, bias_ref, weight_ref,
-    out_ref, dres_ref, grad_ref, small_ref, bias_grad_ref, *, node_total, parts, width, units, block
+    out_ref, dres_ref, own_ref, peer_ref, small_ref, bias_grad_ref, grad_ref, *, node_total, parts, width, units, block
 ):
     i = pl.program_id(0)
 
@@ -343,6 +849,12 @@
     add_small(28, col_sum(dres))
     dres_ref[...] = dres
 
+    @pl.when(i == pl.num_programs(0) - 1)
+    def _():
+        mine = lax.axis_index("heads")
+        own_ref[...] = grad_ref[mine]
+        peer_ref[...] = grad_ref[1 - mine].astype(BF16)
+
 
 def block_step(filtered, tokens, mask, cotangent, stat, params, bias, weights, node_total, block=256):
     rows, width = filtered.shape
@@ -350,7 +862,8 @@
     outs = [
         jax.ShapeDtypeStruct((rows, width), F32),
         jax.ShapeDtypeStruct((rows, width), F32),
-        jax.ShapeDtypeStruct(weights.shape, F32),
+        jax.ShapeDtypeStruct(weights.shape[1:], F32),
+        jax.ShapeDtypeStruct(weights.shape[1:], BF16),
         jax.ShapeDtypeStruct(params.shape, F32),
         jax.ShapeDtypeStruct(bias.shape, F32),
     ]
@@ -372,7 +885,8 @@
         ],
         out_specs=[by_rows, by_rows] + [full_spec(o.shape) for o in outs[2:]],
         out_shape=outs,
-        compiler_params=pltpu.CompilerParams(vmem_limit_bytes=56 << 20),
+        scratch_shapes=[pltpu.VMEM(weights.shape, F32)],
+        compiler_params=pltpu.CompilerParams(vmem_limit_bytes=58 << 20),
     )(filtered, tokens, mask, cotangent, stat, params, bias, weights)
 
 
@@ -388,93 +902,52 @@
     rows = rows_here // parts
     node_total = rows_here * row_count
     first = part_rank * rows
-    both = ("rows", "heads")
+    tile_count = owners.shape[0]
+    slot_cap = tile_first.shape[1]
 
     def own(a):
         return lax.dynamic_slice_in_dim(a, first, rows, 0)
 
-    weight_stack = jnp.concatenate(
-        [qkv_weight.reshape(-1, width), proj_weight, fc1_weight, fc2_weight], axis=0
-    )
-    weights = lax.all_gather(weight_stack, "heads")
-
-    up = [(i, i + 1) for i in range(row_count - 1)]
-    down = [(j, i) for i, j in up]
-    before = lax.ppermute(tokens_in[rows_here - HALO :], "rows", up)
-    after = lax.ppermute(tokens_in[:HALO], "rows", down)
-    extended = lax.dynamic_slice_in_dim(
-        jnp.concatenate([before, tokens_in, after], axis=0), first, rows + 2 * HALO, 0
-    )
-
-    scene_ends = (jnp.cumsum(scene_lengths) * WIN).astype(jnp.int32)
-    own_rows = row_rank * rows_here + first + jnp.arange(rows, dtype=jnp.int32)
-    passed = scene_ends[None, :] <= own_rows[:, None]
-    scene_low = jnp.max(jnp.where(passed, scene_ends[None, :], 0), axis=1)
-    scene_high = jnp.min(jnp.where(passed, node_total, scene_ends[None, :]), axis=1)
-    near = own(neighbours)
-    target = own_rows[:, None] + near
-    usable = (near >= -HALO) & (target >= scene_low[:, None]) & (target < scene_high[:, None])
-    near = jnp.where(usable, near, -8 * HALO)
-
-    taps = small_params[:TAPS]
-    filtered, stat = filter_forward(extended, near, taps)
-    stat = lax.psum(stat, both)
+    filtered, stat, near_t, extended, weights = filter_forward(
+        scene_lengths, tokens_in, neighbours, small_params, qkv_weight, proj_weight, fc1_weight,
+        fc2_weight, row_count, parts
+    )
     bias = small_params[37:].reshape(1, -1)
-    output, dres, weight_grad, small_grad, bias_grad = block_step(
+    output, dres, own_grad, peer_grad, small_grad, bias_grad = block_step(
         filtered, own(tokens_in), own(window_mask)[None], own(cotangent), stat, small_params, bias,
         weights, node_total
     )
     output = lax.all_gather(output, "heads", axis=0, tiled=True)
-    small_rest = lax.psum(
-        jnp.concatenate([small_grad[TAPS:37], bias_grad.reshape(-1, width)], axis=0), both
-    )
-
-    conv_back, tap_grad = filter_backward(
-        extended, filtered, dres, near.T, taps, stat, small_rest[:8], small_params, node_total
-    )
-    line = [(i, i + 1) for i in range(row_count * parts - 1)]
-    back = [(j, i) for i, j in line]
-    rims = conv_back.astype(BF16)
-    from_before = lax.ppermute(rims[rows + HALO :], both, line).astype(F32)
-    from_after = lax.ppermute(rims[:HALO], both, back).astype(F32)
-    input_grad = dres + conv_back[HALO : HALO + rows]
-    input_grad = jnp.concatenate(
-        [
-            input_grad[:HALO] + from_before,
-            input_grad[HALO : rows - HALO],
-            input_grad[rows - HALO :] + from_after,
-        ],
-        axis=0,
-    )
-    input_grad = lax.all_gather(input_grad, "heads", axis=0, tiled=True)
-
-    small_all = jnp.concatenate([lax.psum(tap_grad[:TAPS], both), small_rest], axis=0)
-    small_new, small_first_new, small_second_new = adam_step(
-        small_params, small_all, small_first, small_second, 0.0
-    )
-
-    tile_count = owners.shape[0]
-    slot_cap = tile_first.shape[1]
+    dres_all = lax.all_gather(dres, "heads", axis=0, tiled=True)
+
     tile_order = jnp.arange(tile_count, dtype=jnp.int32)
     same_owner = (owners[:, None] == owners[None, :]) & (tile_order[None, :] < tile_order[:, None])
     slot_of = owners * slot_cap + jnp.sum(same_owner.astype(jnp.int32), axis=1)
     slot_ids = jnp.arange(row_count * slot_cap, dtype=jnp.int32)
     found = slot_of[None, :] == slot_ids[:, None]
     slot_tile = jnp.max(jnp.where(found, tile_order[None, :], -1), axis=1)
-    live = (slot_tile >= 0).astype(F32)[:, None, None]
-    chosen = jnp.clip(slot_tile, 0, tile_count - 1)
-    own_grad = lax.psum_scatter(weight_grad, "heads", scatter_dimension=0, tiled=False)
-    grad_slots = jnp.take(own_grad.reshape(tile_count, BR, width), chosen, axis=0) * live
-    tile_grad = lax.psum_scatter(grad_slots, "rows", scatter_dimension=0, tiled=True)
-    own_slots = lax.dynamic_slice_in_dim(chosen, row_rank * slot_cap, slot_cap)
-    own_live = lax.dynamic_slice_in_dim(live, row_rank * slot_cap, slot_cap)
-    tile_old = jnp.take(weight_stack.reshape(tile_count, BR, width), own_slots, axis=0).astype(F32)
+
+    conv_back, small_sum, tile_grad = filter_backward(
+        slot_tile, extended, filtered, dres, near_t, small_params, stat, small_grad, bias_grad,
+        own_grad.reshape(tile_count, BR, width), peer_grad.reshape(tile_count, BR, width), slot_cap,
+        row_count, parts
+    )
+    input_grad = dres_all + conv_back.astype(F32)
+    small_new, small_first_new, small_second_new = adam_step(
+        small_params, small_sum, small_first, small_second, 0.0
+    )
+    own_slots = lax.dynamic_slice_in_dim(slot_tile, row_rank * slot_cap, slot_cap)
+    live = (own_slots >= 0).astype(F32)[:, None, None]
+    weight_tiles = lax.dynamic_index_in_dim(weights, part_rank, 0, keepdims=False)
+    tile_old = jnp.take(
+        weight_tiles.reshape(tile_count, BR, width), jnp.maximum(own_slots, 0), axis=0
+    ).astype(F32)
     new_weight, new_first, new_second = adam_step(
         tile_old, tile_grad, tile_first[0], tile_second[0], decay_rate
     )
-    new_weight = new_weight * own_live
-    new_first = new_first * own_live
-    new_second = new_second * own_live
+    new_weight = new_weight * live
+    new_first = new_first * live
+    new_second = new_second * live
     return (
         output,
         input_grad,

time: 390 us -> 190 us (0.49)
  blocking collectives: 126 us -> 0 us
  waiting for transfers between devices: 110 us -> 0.71 us
  Pallas kernels: 81.9 us -> 139 us
  other arithmetic: 20.2 us -> 8.8 us
  starting transfers between devices: 10.2 us -> 0.08 us
    psum x3 -> x0, blocking collectives: 126 us -> none  [the longest x1 43.6 us: local(): lax.psum(tap_grad[:TAPS], both)]
    reduce_scatter x2 -> x0, waiting for transfers between devices: 105 us -> none  [the longest x1 105 us: local(): lax.psum_scatter(grad_slots, 'rows', scatter_dimension=0, tiled=True)]
    pallas_call x2, Pallas kernels: 33.5 us -> 90.7 us  [the longest x1 62.9 us: filter_backward(): pl.pallas_call(functools.partial(filter_back_kernel, block=block, row_cou...]
    ppermute x4 -> x0, starting transfers between devices: 9.98 us -> none  [the longest x1 6.11 us: local(): before = lax.ppermute(tokens_in[rows_here - HALO:], 'rows', up)]
    concatenate x4 -> x0, other arithmetic: 6.31 us -> none  [the longest x1 2.95 us: local(): jnp.concatenate([qkv_weight.reshape(-1, width), proj_weight, fc1_weight,...]
    gather x2 -> x1, local copies, waits for them, and re-layouts: 7.61 us -> 2.27 us  [local(): jnp.take(weight_tiles.reshape(tile_count, BR, width), jnp.maximum(own_slo...]
    unnamed x38 -> x52, local copies, waits for them, and re-layouts: 13.1 us -> 18.1 us
    mul x2 -> x0, other arithmetic: 5.04 us -> none  [the longest x1 5.04 us: local(): jnp.take(own_grad.reshape(tile_count, BR, width), chosen, axis=0) * live]
  transfers between devices with their start and end apart: 9 -> 2, of which waited for: 2 -> 0; matrix products, arithmetic and copies ran while one was open for 8% -> 5% of each run, Pallas kernels for 9% -> 33%
where the time goes in v2:
time: 190 us; the launch traced here: 189 us
  Pallas kernels  139 us (73%)
  local copies, waits for them, and re-layouts  26.1 us (14%)
  between operations  14.2 us (7%)
  other arithmetic  8.8 us (5%)
    pallas_call x1, Pallas kernels, filter_backward(): pl.pallas_call(functools.partial(filter_back_kernel, block=block, row_cou...  62.9 us
    pallas_call x1, Pallas kernels, block_step(): pl.pallas_call(functools.partial(block_kernel, node_total=node_total, par...  48.5 us
    pallas_call x1, Pallas kernels, filter_forward(): pl.pallas_call(functools.partial(filter_kernel, block=block, row_count=ro...  27.7 us
    unnamed x52, local copies, waits for them, and re-layouts  18.1 us
    add x1, other arithmetic, local(): input_grad = dres_all + conv_back.astype(F32)  4.42 us
  transfers between devices with their start and end apart: 2, of which 0 were waited for; matrix products, arithmetic and copies ran while one was open for 5% of the time, Pallas kernels for 33%

profile of v2, /device:TPU:0, one launch (start us, length us, event | category | flops | bytes accessed | tf_op | source)
XLA Modules:
  0.0 189.1 jit_solution(17043774739281070133)
XLA Ops:
  7.2 0.0 all-gather.3.cloned.1.call-start
  7.2 1.8 copy-done
  9.1 1.2 constant_dynamic-slice_fusion.1.cot_ref
  10.3 0.7 copy-done.4
  11.1 1.0 constant_dynamic-slice_fusion.2.tok_ref
  12.0 0.6 dynamic_slice.17
  12.6 2.3 %copy.25.near_ref = s32[2048,27]{1,0:T(8,128)} copy(s32[2048,27]{0,1:T(8,128)} %param.16) | data formatting | bytes 442368 | tf_op args[1]
  14.9 0.6 copy.26
  15.5 1.2 copy-done.3
  16.7 1.4 copy-done.5
  18.2 1.1 copy-done.9
  19.2 1.1 copy-done.10
  20.3 1.0 copy-done.11
  21.3 27.7 %shard_map.214 = (f32[1024,384]{1,0:T(8,128)S(1)}, f32[8,384]{1,0:T(8,128)S(1)}, s32[32,1024]{1,0:T(8,128)S(1)}, bf16[1280,384]{1,0:T(8,128)(2,1)S(1)}, bf16[2,2304,384]{2,1,0:T(8,128)(2,1)S(1)}) custom-call(s32[4]{0:T(128)S(1)} %copy-done.15, bf16[2048,384]{1,0:T(8,128)(2,1)S(1)} %copy-done.5, s32[2048,27]{1,0:T(8,128)S(1)} %copy-done.3, ...), custom_call_target="tpu_custom_call" | custom-call | tf_op jit(solution)/shard_map/pallas_call | solution.py:342
  49.0 1.8 copy-done.1
  50.8 1.2 copy-done.2
  52.0 0.9 copy-done.8
  52.9 0.7 copy-done.13
  53.6 0.6 copy-done.14
  54.2 48.5 %shard_map.215 = (f32[1024,384]{1,0:T(8,128)}, f32[1024,384]{1,0:T(8,128)}, f32[2304,384]{1,0:T(8,128)}, bf16[2304,384]{1,0:T(8,128)(2,1)}, f32[41,384]{1,0:T(8,128)}, /*index=5*/f32[1,1536]{1,0:T(1,128)}) custom-call(f32[1024,384]{1,0:T(8,128)} %copy-done.2, bf16[1024,384]{1,0:T(8,128)(2,1)} %constant_dynamic-slice_fusion.2.tok_ref, s32[1,1024]{1,0:T(1,128)} %bitcast.34, ...), custom_call_target="tpu_custom_call" | custom-call | tf_op jit(solution)/shard_map/pallas_call | solution.py:871
  102.8 0.0 all-gather.5.cloned.1.call-start
  102.8 0.7 all-gather.5.cloned.1.call-update
  103.5 0.2 convert_reduce_fusion
  103.7 0.1 select_reduce_fusion.slot_ref
  103.9 0.1 broadcast_compare_fusion
  103.9 2.9 %constant_dynamic-slice_fusion = bf16[1,2304,384]{2,1,0:T(8,128)(2,1)} fusion(bf16[2,2304,384]{2,1,0:T(8,128)(2,1)} %copy-done.1, s32[]{:T(128)S(6)} %select_n.26), kind=kLoop, calls=%fused_computation.26 | loop fusion | bytes 3538948 | tf_op jit(solution)/shard_map/jit(dynamic_index_in_dim)/dynamic_slice | solution.py:941
  106.8 2.3 %gather_fusion = bf16[14,16,384]{2,1,0:T(8,128)(2,1)S(1)} fusion(bf16[144,16,384]{2,1,0:T(8,128)(2,1)} %bitcast.30, s32[1024]{0:T(1024)S(1)} %pad_clamp_fusion), kind=kCustom, calls=%fused_computation | custom fusion | bytes 344120 | tf_op jit(solution)/shard_map/jit(_take)/gather | solution.py:942
  109.2 62.9 %shard_map.216 = (bf16[2048,384]{1,0:T(8,128)(2,1)}, f32[41,384]{1,0:T(8,128)}, f32[14,16,384]{2,1,0:T(8,128)}) custom-call(s32[224]{0:T(256)} %copy-done.22, bf16[1280,384]{1,0:T(8,128)(2,1)} %copy-done.8, f32[1024,384]{1,0:T(8,128)} %copy-done.2, f32[1024,384]{1,0:T(8,128)} %get-tuple-element.27.dres_ref, s32[32,1024]{1,0:T(8,128)} %copy-done.13, ...), custom_call_target="tpu_custom_call" | custom-call | tf_op jit(solution)/shard_map/pallas_call | solution.py:648
  172.1 1.6 multiply_subtract_fusion
  173.7 2.4 %convert_bitcast_fusion = (bf16[1,14,16,384]{3,2,1,0:T(8,128)(2,1)}, f32[14,16,384]{2,1,0:T(8,128)}, f32[1,14,16,384]{3,2,1,0:T(8,128)}, f32[1,14,16,384]{3,2,1,0:T(8,128)}) fusion(f32[14]{0:T(128)S(1)} %get-tuple-element.46, f32[14,16,384]{2,1,0:T(8,128)} %get-tuple-element.35, f32[1,14,16,384]{3,2,1,0:T(8,128)S(1)} %copy-done.17, ...), kind=kLoop, calls=%fused_computation.12 | loop fusion | flops 1720320 | bytes 2408518 | tf_op jit(solution)/shard_map/broadcast_in_dim | solution.py:957
  176.1 4.4 %convert_add_fusion = f32[2048,384]{1,0:T(8,128)} fusion(f32[2048,384]{1,0:T(8,128)} %all-gather.5.cloned.1.call-done, bf16[2048,384]{1,0:T(8,128)(2,1)} %get-tuple-element.34), kind=kLoop, calls=%fused_computation.1 | loop fusion | flops 1572864 | bytes 7864320 | tf_op jit(solution)/shard_map/add | solution.py:935
  180.6 1.7 copy.28
  (42 shorter events, 0.1 us)
Async XLA Ops:
  7.2 1.9 %copy-start = (f32[2048,384]{1,0:T(8,128)S(1)}, f32[2048,384]{1,0:T(8,128)}, u32[]{:S(2)}) copy-start(f32[2048,384]{1,0:T(8,128)} %param.24) | copy-start | bytes 9437188
  7.2 168.9 %all-gather.3.cloned.1.call-start = ((), (), s32[]{:S(2)}) async-start(), calls=%async_computation | async-start | bytes 4718592 | tf_op jit(solution)/shard_map/all_gather | solution.py:920
  9.1 2.0 %copy-start.4 = (bf16[2048,384]{1,0:T(8,128)(2,1)S(1)}, bf16[2048,384]{1,0:T(8,128)(2,1)}, u32[]{:S(2)}) copy-start(bf16[2048,384]{1,0:T(8,128)(2,1)} %tokens_ref.1) | copy-start | bytes 4718596
  9.1 3.0 %copy-start.23 = (s32[2048]{0:T(1024)S(1)}, s32[2048]{0:T(1024)}, u32[]{:S(2)}) copy-start(s32[2048]{0:T(1024)} %param.18) | copy-start | bytes 24580
  11.0 3.9 %copy-start.6 = (f32[41,384]{1,0:T(8,128)S(1)}, f32[41,384]{1,0:T(8,128)}, u32[]{:S(2)}) copy-start(f32[41,384]{1,0:T(8,128)} %params_ref.3) | copy-start | bytes 188932
  11.1 4.5 %copy-start.12 = (bf16[192,384]{1,0:T(8,128)(2,1)S(1)}, bf16[192,384]{1,0:T(8,128)(2,1)}, u32[]{:S(2)}) copy-start(bf16[192,384]{1,0:T(8,128)(2,1)} %proj_ref.1) | copy-start | bytes 442372
  11.1 4.5 %copy-start.15 = (s32[4]{0:T(128)S(1)}, s32[4]{0:T(128)}, u32[]{:S(2)}) copy-start(s32[4]{0:T(128)} %lengths_ref.1) | copy-start | bytes 52
  15.5 1.2 copy-start.3
  16.7 1.4 copy-start.5
  18.1 1.1 copy-start.9
  19.2 1.1 copy-start.10
  20.3 1.0 copy-start.11
  49.0 1.8 copy-start.1
  50.8 1.2 copy-start.2
  52.0 1.0 copy-start.8
  52.9 0.7 copy-start.13
  53.6 0.6 copy-start.14
  102.7 0.8 copy-start.21
  102.8 73.4 %all-gather.5.cloned.1.call-start = ((), (), s32[]{:S(2)}) async-start(), calls=%async_computation.1 | async-start | bytes 4718592 | tf_op jit(solution)/shard_map/all_gather | solution.py:921
  103.8 3.0 %copy-start.22 = (s32[224]{0:T(256)}, s32[224]{0:T(256)S(1)}, u32[]{:S(2)}) copy-start(s32[224]{0:T(256)S(1)} %select_reduce_fusion.slot_ref) | copy-start | bytes 2692
  109.1 63.0 %copy-start.7 = (f32[41,384]{1,0:T(8,128)S(1)}, f32[41,384]{1,0:T(8,128)}, u32[]{:S(2)}) copy-start(f32[41,384]{1,0:T(8,128)} %params_ref.3) | copy-start | bytes 188932
  109.1 63.0 %copy-start.19 = (f32[41,384]{1,0:T(8,128)S(1)}, f32[41,384]{1,0:T(8,128)}, u32[]{:S(2)}) copy-start(f32[41,384]{1,0:T(8,128)} %param.26) | copy-start | bytes 188932
  109.1 63.0 %copy-start.20 = (f32[41,384]{1,0:T(8,128)S(1)}, f32[41,384]{1,0:T(8,128)}, u32[]{:S(2)}) copy-start(f32[41,384]{1,0:T(8,128)} %param.27) | copy-start | bytes 188932
  109.1 64.6 %copy-start.17 = (f32[1,14,16,384]{3,2,1,0:T(8,128)S(1)}, f32[1,14,16,384]{3,2,1,0:T(8,128)}, u32[]{:S(2)}) copy-start(f32[1,14,16,384]{3,2,1,0:T(8,128)} %param.29) | copy-start | bytes 1032196
  109.1 64.6 %copy-start.18 = (f32[1,14,16,384]{3,2,1,0:T(8,128)S(1)}, f32[1,14,16,384]{3,2,1,0:T(8,128)}, u32[]{:S(2)}) copy-start(f32[1,14,16,384]{3,2,1,0:T(8,128)} %param.28) | copy-start | bytes 1032196
  176.1 4.4 %copy-start.16 = (f32[2048,384]{1,0:T(8,128)S(1)}, f32[2048,384]{1,0:T(8,128)}, u32[]{:S(2)}) copy-start(f32[2048,384]{1,0:T(8,128)} %all-gather.3.cloned.1.call-done) | copy-start | bytes 9437188
Sparse Core Ops, SparseCore 0:
  102.9 9.9 all-gather.2
  114.4 13.2 all-gather.4

commit v3 on v2

--- a/solution.py
+++ b/solution.py
@@ -148,7 +148,7 @@
 def filter_kernel(
     lengths_ref, tokens_ref, near_ref, taps_ref, qkv_ref, proj_ref, fc1_ref, fc2_ref,
     filt_ref, stat_ref, near_t_ref, ext_ref, stack_ref,
-    place_ref, tile, landed, local_sem, side_sem, weight_sem, send_sem, recv_sem,
+    near_in, tile, landed, local_sem, side_sem, weight_sem, send_sem, recv_sem,
     *, block, row_count, parts, scenes
 ):
     row_rank = lax.axis_index("rows")
@@ -165,7 +165,9 @@
     own_copy = pltpu.make_async_copy(
         tokens_ref.at[pl.ds(first, rows)], ext_ref.at[pl.ds(HALO, rows)], local_sem.at[0]
     )
-    near_copy = pltpu.make_async_copy(near_ref.at[pl.ds(first, rows)], place_ref, local_sem.at[1])
+    near_copy = pltpu.make_async_copy(
+        near_ref.at[:, pl.ds(pl.multiple_of(first, LANES), rows)], near_in, local_sem.at[1]
+    )
     own_copy.start()
     near_copy.start()
     low_side = ext_ref.at[pl.ds(0, HALO)]
@@ -207,10 +209,8 @@
 
     def sent_weight(i):
         ref, at, size = pieces[i]
-        return swap_copy(
-            ref, stack_ref.at[part_rank, pl.ds(at, size)], weight_sem.at[1, i],
-            weight_sem.at[2, i], other_core,
-        )
+        here = stack_ref.at[part_rank, pl.ds(at, size)]
+        return swap_copy(here, here, weight_sem.at[1, i], weight_sem.at[2, i], other_core)
 
     for i in range(len(pieces)):
         own_weight(i).start()
@@ -254,6 +254,7 @@
                 side_down().start()
 
             for i in range(len(pieces)):
+                own_weight(i).wait()
                 sent_weight(i).start()
 
         @pl.when(it == blocks - 2)
@@ -281,24 +282,22 @@
         b = lax.rem(it + 1, blocks)
         base = pl.multiple_of(b * block, block)
         window = ext_ref[pl.ds(base, span), :]
-        near = place_ref[pl.ds(base, block), :]
-        own_row = row_rank * rows_here + first + base + lax.broadcasted_iota(
-            jnp.int32, (block, 1), 0
-        )
+        near = near_in[:, pl.ds(base, block)]
+        lane = lax.broadcasted_iota(jnp.int32, (1, block), 1)
+        own_row = row_rank * rows_here + first + base + lane
         scene_low = jnp.zeros_like(own_row)
         scene_high = jnp.full_like(own_row, node_total)
-        for end in reversed(ends):
+        for end in ends:
             passed = own_row >= end
             scene_low = jnp.maximum(scene_low, jnp.where(passed, end, 0))
             scene_high = jnp.minimum(scene_high, jnp.where(passed, node_total, end))
         target = own_row + near
         usable = (near >= -HALO) & (target >= scene_low) & (target < scene_high)
-        near = jnp.where(usable, near, -8 * HALO)
-        padded = jnp.concatenate(
-            [near, jnp.zeros((block, LANES - TAPS), jnp.int32)], axis=1
-        )
-        near_t_ref[:, pl.ds(base, block)] = jnp.transpose(padded)[: near_t_ref.shape[0]]
-        place = lax.broadcasted_iota(jnp.int32, (block, TAPS), 0) + near + HALO
+        place_t = jnp.where(usable, near + lane + HALO, -8 * HALO)
+        near_t_ref[0:TAPS, pl.ds(base, block)] = place_t
+        place = jnp.transpose(
+            jnp.concatenate([place_t, jnp.zeros((LANES - TAPS, block), jnp.int32)], axis=0)
+        )
         column = lax.broadcasted_iota(jnp.int32, (block, span), 1)
         total = jnp.zeros((block, width), F32)
         group = 3
@@ -323,7 +322,6 @@
     to_tile(tile, [stat_ref[0:1], stat_ref[1:2]])
     send_to_all(lambda other: tile, landed, send_sem, recv_sem, count, parts, me)
     for i in range(len(pieces)):
-        own_weight(i).wait()
         sent_weight(i).wait()
     await_from_all(tile, landed, send_sem, recv_sem, count, parts, me)
     total = add_landed(tile[...], landed, count)
@@ -344,7 +342,7 @@
             filter_kernel, block=block, row_count=row_count, parts=parts, scenes=lengths.shape[0]
         ),
         in_specs=[pl.BlockSpec(memory_space=pltpu.SMEM), anywhere, anywhere, vmem] + [anywhere] * 4,
-        out_specs=[vmem, vmem, vmem, vmem, anywhere],
+        out_specs=[vmem] * 5,
         out_shape=[
             jax.ShapeDtypeStruct((rows, width), F32),
             jax.ShapeDtypeStruct((8, width), F32),
@@ -353,7 +351,7 @@
             jax.ShapeDtypeStruct((parts, stack_rows, width), BF16),
         ],
         scratch_shapes=[
-            pltpu.VMEM((rows, TAPS), jnp.int32),
+            pltpu.VMEM((TAPS, rows), jnp.int32),
             pltpu.VMEM((8, LANES), F32),
             pltpu.VMEM((count, 8, LANES), F32),
             pltpu.SemaphoreType.DMA((3,)),
@@ -363,25 +361,32 @@
             pltpu.SemaphoreType.DMA((count,)),
         ],
         compiler_params=pltpu.CompilerParams(
-            collective_id=0, has_side_effects=True, vmem_limit_bytes=40 << 20
+            collective_id=0, has_side_effects=True, vmem_limit_bytes=60 << 20
         ),
     )(lengths, tokens, near, params, qkv, proj, fc1, fc2)
 
 
-def streams_of(cap, pieces):
-    halves = []
-    middle = (cap + 1) // 2
-    for order, low, high in ((0, 0, middle), (1, middle, cap)):
-        cuts = min(pieces, high - low)
-        edges = [low + (high - low) * i // cuts for i in range(cuts + 1)] if cuts else []
-        halves.append([(order, a, b - a) for a, b in zip(edges[:-1], edges[1:])])
-    return [s for pair in zip(*halves) for s in pair] + halves[0][len(halves[1]) :]
-
-
-def bits_of(row_count, order):
-    bits = list(range(row_count.bit_length() - 1))
-    if order and len(bits) > 1:
-        bits[0], bits[1] = bits[1], bits[0]
+def streams_of(cap, depth):
+    third = cap // 7 if depth > 2 else 0
+    counts = [(cap - 2 * third + 1) // 2, (cap - 2 * third) // 2, third, third]
+    found = []
+    slot = 0
+    for order, count in enumerate(counts):
+        for j in range(count):
+            place = j if order < 2 else 2 * j + order - 2
+            found.append((place, order, slot))
+            slot += 1
+    return [(order, slot, place) for place, order, slot in sorted(found)]
+
+
+def bits_of(depth, order):
+    bits = list(range(depth))
+    if order == 1 and depth > 1:
+        bits[:2] = [1, 0]
+    if order == 2:
+        bits[:3] = [2, 0, 1]
+    if order == 3:
+        bits[:3] = [2, 1, 0]
     return bits
 
 
@@ -391,18 +396,15 @@
 
 
 def filter_back_kernel(
-    slot_ref, ext_ref, filt_ref, dres_ref, near_t_ref, params_ref, stat_ref, small_ref, bias_ref,
-    own_ref, peer_ref,
-    back_ref, small_out_ref, tile_out_ref, *scratch,
-    block, row_count, parts, cap, streams, node_total
+    slot_ref, ext_hbm, filt_hbm, dres_hbm, near_ref, params_ref, stat_ref, small_ref, own_hbm,
+    peer_hbm, output_hbm,
+    input_grad_ref, output_in, small_out_ref, tile_out_ref,
+    ext_ref, filt_ref, dres_ref, own_ref, peer_ref, output_ref, pair_out, pair_in, sums, staged, arrived,
+    total_ref, grad_ref, rim_ref, rim_in, tile, landed, flat, flat_in, part_sum, flat_all,
+    local_sem, output_sem, pair_send, pair_recv, sum_send, sum_recv, tree_send, tree_recv, rim_sem,
+    flat_send, flat_recv, all_send, all_recv, out_sem,
+    *, block, row_count, parts, cap, node_total
 ):
-    wide = len(streams)
-    sums, staged, arrived = scratch[:wide], scratch[wide : 2 * wide], scratch[2 * wide : 3 * wide]
-    (
-        total_ref, grad_ref, rim_ref, rim_in, pair_in, tile, landed, flat, flat_in, part_sum,
-        flat_all, pair_sem, sum_send, sum_recv, tree_send, tree_recv, rim_sem, flat_send, flat_recv,
-        all_send, all_recv, out_sem,
-    ) = scratch[3 * wide :]
     row_rank = lax.axis_index("rows")
     part_rank = lax.axis_index("heads")
     count = row_count * parts
@@ -411,90 +413,133 @@
     groups = width // LANES
     first = part_rank * rows
     depth = row_count.bit_length() - 1
+    streams = streams_of(cap, depth)
+    wide = len(streams)
     other_core = (row_rank, 1 - part_rank)
     small_rows = params_ref.shape[0]
-    bias_rows = bias_ref.shape[1] // width
-
+
+    loads = [
+        pltpu.make_async_copy(source, landing, local_sem.at[i])
+        for i, (source, landing) in enumerate(
+            (
+                (peer_hbm, peer_ref),
+                (own_hbm, own_ref),
+                (filt_hbm, filt_ref),
+                (dres_hbm, dres_ref),
+                (ext_hbm, ext_ref),
+                (output_hbm, output_ref),
+            )
+        )
+    ]
     greet_all(count, parts, me)
+    for load in loads:
+        load.start()
     to_tile(tile, [small_ref[27:28], small_ref[28:29]])
     total_ref[...] = jnp.zeros_like(total_ref)
     small_out_ref[...] = jnp.zeros_like(small_out_ref)
     await_all(count)
     send_to_all(lambda other: tile, landed, sum_send, sum_recv, count, parts, me)
-    pair_copy = swap_copy(peer_ref, pair_in, pair_sem.at[0], pair_sem.at[1], other_core)
-    pair_copy.start()
 
     keep_at = {}
-    for i, (order, _, size) in enumerate(streams):
+    for i, (order, _, _) in enumerate(streams):
         keep_at[i, 0] = 0
-        for t, bit in enumerate(bits_of(row_count, order)):
-            half = (row_count >> (t + 1)) * size
+        for t, bit in enumerate(bits_of(depth, order)):
+            half = row_count >> (t + 1)
             keep_at[i, t + 1] = keep_at[i, t] + lax.rem(row_rank // (1 << bit), 2) * half
 
-    def pack(i):
-        order, low, size = streams[i]
-        bits = bits_of(row_count, order)
-
+    in_flight = 2
+    follower = {}
+    for i, (order, _, place) in enumerate(streams):
+        for j, (other_order, _, other_place) in enumerate(streams):
+            if min(order, 2) == min(other_order, 2) and other_place == place + in_flight:
+                follower[i] = j
+
+    def give_at(i, t):
+        return 2 * keep_at[i, t] + (row_count >> (t + 1)) - keep_at[i, t + 1]
+
+    def tile_at(i, p):
+        order, slot, _ = streams[i]
+        owner = 0
+        for t, bit in enumerate(bits_of(depth, order)):
+            owner = owner + lax.rem(p // (1 << (depth - 1 - t)), 2) * (1 << bit)
+        return slot_ref[owner * cap + slot]
+
+    def pair_copy(i):
+        return swap_copy(
+            pair_out.at[i], pair_in.at[i], pair_send.at[i], pair_recv.at[i], other_core
+        )
+
+    def pair_start(i):
         def body(p, carry):
-            owner = 0
-            for t, bit in enumerate(bits):
-                owner = owner + lax.rem(p // (1 << (depth - 1 - t)), 2) * (1 << bit)
-            for c in range(size):
-                tile_id = slot_ref[owner * cap + low + c]
-                at = jnp.maximum(tile_id, 0)
-                value = own_ref[at] + pair_in[at].astype(F32)
-                sums[i][p * size + c] = jnp.where(tile_id >= 0, value, 0.0)
+            index = tile_at(i, p)
+            value = peer_ref[jnp.maximum(index, 0)]
+            pair_out[i, p] = jnp.where(index >= 0, value, jnp.zeros_like(value))
             return carry
 
-        lax.fori_loop(0, row_count, body, 0)
+        lax.fori_loop(0, row_count, body, 0, unroll=8)
+        pair_copy(i).start()
 
     def tree_copy(i, t):
-        order, _, size = streams[i]
-        half = (row_count >> (t + 1)) * size
-        at = (row_count - (row_count >> t)) * size
+        order, _, _ = streams[i]
+        half = row_count >> (t + 1)
+        part = pl.ds(row_count - (row_count >> t), half)
         return swap_copy(
-            staged[i].at[pl.ds(at, half)], arrived[i].at[pl.ds(at, half)], tree_send.at[i, t],
-            tree_recv.at[i, t], (flip(row_rank, bits_of(row_count, order)[t]), part_rank),
-        )
-
-    def tree_start(i, t):
-        order, _, size = streams[i]
-        half = row_count >> (t + 1)
-        at = (row_count - (row_count >> t)) * size
-        give = keep_at[i, t] * 2 + half * size - keep_at[i, t + 1]
-
-        def body(p, carry):
-            for c in range(size):
-                staged[i][at + p * size + c] = sums[i][give + p * size + c].astype(BF16)
+            staged.at[i, part], arrived.at[i, part], tree_send.at[i, t], tree_recv.at[i, t],
+            (flip(row_rank, bits_of(depth, order)[t]), part_rank),
+        )
+
+    def pair_end(i):
+        pair_copy(i).wait()
+
+        def value_at(p):
+            index = tile_at(i, p)
+            value = own_ref[jnp.maximum(index, 0)]
+            return jnp.where(index >= 0, value, 0.0) + pair_in[i, p].astype(F32)
+
+        def give(p, carry):
+            staged[i, p] = value_at(give_at(i, 0) + p).astype(BF16)
             return carry
 
-        lax.fori_loop(0, half, body, 0)
-        tree_copy(i, t).start()
-
-    def tree_end(i, t):
-        _, _, size = streams[i]
-        half = row_count >> (t + 1)
-        at = (row_count - (row_count >> t)) * size
+        def keep(p, carry):
+            sums[i, keep_at[i, 1] + p] = value_at(keep_at[i, 1] + p)
+            return carry
+
+        lax.fori_loop(0, row_count // 2, give, 0, unroll=8)
+        if streams[i][2] < in_flight:
+            tree_copy(i, 0).start()
+        lax.fori_loop(0, row_count // 2, keep, 0, unroll=8)
+
+    def tree_step(i, t):
+        came = row_count - (row_count >> t)
         tree_copy(i, t).wait()
-
-        def body(p, carry):
-            for c in range(size):
-                k = keep_at[i, t + 1] + p * size + c
-                sums[i][k] = sums[i][k] + arrived[i][at + p * size + c].astype(F32)
-            return carry
-
-        lax.fori_loop(0, half, body, 0)
-
-    def tree_step(i, t):
-        tree_end(i, t)
+        if t == 0 and i in follower:
+            tree_copy(follower[i], 0).start()
+        low = keep_at[i, t + 1]
+
+        def values(k, size):
+            return sums[i, pl.ds(k, size)] + arrived[i, pl.ds(came + k - low, size)].astype(F32)
+
         if t + 1 < depth:
-            tree_start(i, t + 1)
-
-    pair_copy.wait()
+            half = row_count >> (t + 2)
+            at = row_count - (row_count >> (t + 1))
+            staged[i, at : at + half] = values(give_at(i, t + 1), half).astype(BF16)
+            tree_copy(i, t + 1).start()
+            k = keep_at[i, t + 2]
+            sums[i, pl.ds(k, half)] = values(k, half)
+        else:
+            tile_out_ref[streams[i][1]] = values(low, 1)[0]
+
+    loads[0].wait()
     for i in range(wide):
-        pack(i)
-        tree_start(i, 0)
-
+        pair_start(i)
+    output_copy = swap_copy(output_ref, output_in, output_sem.at[0], output_sem.at[1], other_core)
+    loads[1].wait()
+    for i in range(wide):
+        pair_end(i)
+
+    for load in loads[2:]:
+        load.wait()
+    output_copy.start()
     await_from_all(tile, landed, sum_send, sum_recv, count, parts, me)
     back = add_landed(tile[...], landed, count)
     gain_mean = from_tile(back, 0, groups) * (1.0 / node_total)
@@ -524,37 +569,49 @@
         )
 
     def finish_rows(low, size):
-        back_ref[pl.ds(first + low, size), :] = total_ref[HALO + low : HALO + low + size].astype(BF16)
-
-    late = rows - 384
+        input_grad_ref[pl.ds(first + low, size), :] = (
+            dres_ref[low : low + size] + total_ref[HALO + low : HALO + low + size]
+        )
+
+    late = rows - block - HALO
 
     def out_copy(i):
         low, size = ((late, rows - late), (0, late))[i]
-        here = back_ref.at[pl.ds(first + low, size)]
+        here = input_grad_ref.at[pl.ds(first + low, size)]
         return swap_copy(here, here, out_sem.at[0, i], out_sem.at[1, i], other_core)
 
-    schedule = [[] for _ in range(blocks)]
-    for i in range(wide):
+    group = 3
+    points = TAPS // group
+    schedule = {}
+    for i, (_, _, place) in enumerate(streams):
         for t in range(depth):
-            schedule[min(i // 2 + t, blocks - 1)].append((t, i))
+            due = 2 * place + 9 * t + 8
+            schedule.setdefault(min(due, blocks * points), []).append((due, t, i))
 
     def step(it, carry):
         b = lax.rem(it * (blocks - 1), blocks)
         base = pl.multiple_of(b * block, block)
         window = pl.ds(base, span)
-        place = lax.broadcasted_iota(jnp.int32, (TAPS, block), 1) + HALO + (
-            near_t_ref[:, pl.ds(base, block)][:TAPS]
-        )
+        place = near_ref[0:TAPS, pl.ds(base, block)]
+        place = place + lax.broadcasted_iota(jnp.int32, place.shape, 1) // LANES * LANES
         row = lax.broadcasted_iota(jnp.int32, (span, block), 0)
-        tokens = ext_ref[window, :].astype(F32)
         grad = grad_ref[pl.ds(base, block), :]
-        total = jnp.zeros((span, width), F32)
-        for k in range(TAPS):
-            hot = (place[k : k + 1, :] == row).astype(F32).astype(BF16)
-            spread = dot_plain(hot, grad)
-            total += spread * params_ref[k : k + 1, :]
-            small_out_ref[k : k + 1, :] += col_sum(spread * tokens)
-        total_ref[window, :] += total
+        for point in range(points):
+            total = total_ref[window, :]
+            tokens = ext_ref[window, :].astype(F32)
+            for k in range(point * group, (point + 1) * group):
+                hot = (place[k : k + 1, :] == row).astype(F32).astype(BF16)
+                spread = dot_plain(hot, grad)
+                total += spread * params_ref[k : k + 1, :]
+                small_out_ref[k : k + 1, :] += col_sum(spread * tokens)
+            total_ref[window, :] = total
+            for s in range(blocks):
+                if s * points + point in schedule:
+
+                    @pl.when(it == s)
+                    def _(s=s, point=point):
+                        for _, t, i in sorted(schedule[s * points + point]):
+                            tree_step(i, t)
 
         @pl.when(it == 1)
         def _():
@@ -586,26 +643,13 @@
             finish_rows(late, rows - late)
             out_copy(0).start()
 
-        for s in range(blocks - 1):
-
-            @pl.when(it == s)
-            def _(s=s):
-                for t, i in sorted(schedule[s]):
-                    tree_step(i, t)
-
         return carry
 
     lax.fori_loop(0, blocks, step, 0)
 
     flat[...] = jnp.zeros_like(flat)
     for r in range(small_rows):
-        if r < TAPS:
-            row = small_out_ref[r : r + 1, :]
-        elif r < small_rows - bias_rows:
-            row = small_ref[r : r + 1, :]
-        else:
-            at = (r - small_rows + bias_rows) * width
-            row = bias_ref[0:1, at : at + width]
+        row = small_out_ref[r : r + 1, :] if r < TAPS else small_ref[r : r + 1, :]
         for g in range(groups):
             at = r * groups + g
             flat[at // 8, at % 8 : at % 8 + 1, :] = row[:, g * LANES : (g + 1) * LANES]
@@ -615,63 +659,76 @@
     await_from_all(flat.at[0], flat_in, flat_send, flat_recv, count, parts, me)
     part_sum[...] = add_landed(flat[me], flat_in, count)
     send_to_all(lambda other: part_sum, flat_all, all_send, all_recv, count, parts, me)
-    for t, i in sorted(schedule[blocks - 1]):
+    for _, t, i in sorted(schedule.get(blocks * points, [])):
         tree_step(i, t)
-    for i, (_, low, size) in enumerate(streams):
-        for c in range(size):
-            tile_out_ref[low + c] = sums[i][keep_at[i, depth] + c]
     await_from_all(part_sum, flat_all, all_send, all_recv, count, parts, me)
     flat_all[0] = part_sum[...]
     for r in range(small_rows):
         for g in range(groups):
             at = r * groups + g
-            tile_at = lax.rem(at // 8 - me + count, count)
+            tile_from = lax.rem(at // 8 - me + count, count)
             small_out_ref[r : r + 1, g * LANES : (g + 1) * LANES] = flat_all[
-                tile_at, at % 8 : at % 8 + 1, :
+                tile_from, at % 8 : at % 8 + 1, :
             ]
+    output_copy.wait()
     out_copy(0).wait()
     out_copy(1).wait()
 
 
 def filter_backward(
-    slots, extended, filtered, dres, near_t, params, stat, small, bias, own_grad, peer_grad, cap,
-    row_count, parts, block=256, pieces=3
+    slots, extended, filtered, dres, near_t, params, stat, small, own_grad, peer_grad, output, cap,
+    row_count, parts, block=256
 ):
     rows, width = filtered.shape
     count = row_count * parts
     depth = row_count.bit_length() - 1
-    streams = streams_of(cap, pieces)
-    wide = len(streams)
+    wide = len(streams_of(cap, depth))
     vmem = pl.BlockSpec(memory_space=pltpu.VMEM)
-    by_owner = [row_count * size for _, _, size in streams]
+    anywhere = pl.BlockSpec(memory_space=pl.ANY)
     dma = pltpu.SemaphoreType.DMA
+    of_streams = (wide, row_count, BR, width)
     return pl.pallas_call(
         functools.partial(
             filter_back_kernel, block=block, row_count=row_count, parts=parts, cap=cap,
-            streams=streams, node_total=rows * count,
+            node_total=rows * count,
         ),
-        in_specs=[pl.BlockSpec(memory_space=pltpu.SMEM)] + [vmem] * 10,
-        out_specs=[vmem] * 3,
+        in_specs=[pl.BlockSpec(memory_space=pltpu.SMEM)]
+        + [anywhere] * 3
+        + [vmem] * 4
+        + [anywhere] * 3,
+        out_specs=[vmem] * 4,
         out_shape=[
-            jax.ShapeDtypeStruct((rows * parts, width), BF16),
+            jax.ShapeDtypeStruct((rows * parts, width), F32),
+            jax.ShapeDtypeStruct((rows, width), F32),
             jax.ShapeDtypeStruct(params.shape, F32),
             jax.ShapeDtypeStruct((cap, BR, width), F32),
         ],
-        scratch_shapes=[pltpu.VMEM((n, BR, width), F32) for n in by_owner]
-        + [pltpu.VMEM((n, BR, width), BF16) for n in by_owner] * 2
-        + [
+        scratch_shapes=[
+            pltpu.VMEM(extended.shape, BF16),
+            pltpu.VMEM(filtered.shape, F32),
+            pltpu.VMEM(dres.shape, F32),
+            pltpu.VMEM(own_grad.shape, F32),
+            pltpu.VMEM(peer_grad.shape, BF16),
+            pltpu.VMEM(output.shape, F32),
+            pltpu.VMEM(of_streams, BF16),
+            pltpu.VMEM(of_streams, BF16),
+            pltpu.VMEM(of_streams, F32),
+            pltpu.VMEM(of_streams, BF16),
+            pltpu.VMEM(of_streams, BF16),
             pltpu.VMEM((rows + 2 * HALO, width), F32),
             pltpu.VMEM((rows, width), BF16),
             pltpu.VMEM((2, HALO, width), BF16),
             pltpu.VMEM((2, HALO, width), BF16),
-            pltpu.VMEM(peer_grad.shape, BF16),
             pltpu.VMEM((8, LANES), F32),
             pltpu.VMEM((count, 8, LANES), F32),
             pltpu.VMEM((count, 8, LANES), F32),
             pltpu.VMEM((count, 8, LANES), F32),
             pltpu.VMEM((8, LANES), F32),
             pltpu.VMEM((count, 8, LANES), F32),
+            dma((6,)),
             dma((2,)),
+            dma((wide,)),
+            dma((wide,)),
             dma((count,)),
             dma((count,)),
             dma((wide, depth)),
@@ -684,14 +741,110 @@
             dma((2, 2)),
         ],
         compiler_params=pltpu.CompilerParams(
-            collective_id=1, has_side_effects=True, vmem_limit_bytes=58 << 20
+            collective_id=1, has_side_effects=True, vmem_limit_bytes=60 << 20
         ),
-    )(slots, extended, filtered, dres, near_t, params, stat, small, bias, own_grad, peer_grad)
+    )(
+        slots, extended, filtered, dres, near_t, params, stat, small, own_grad, peer_grad, output
+    )
+
+
+def last_kernel(
+    slot_ref, rank_ref, output_own, output_in, grad_in, weight_ref, params_ref, first_ref,
+    second_ref, small_ref, tile_grad_ref, tile_first_ref, tile_second_ref,
+    output_ref, input_grad_ref, weight_out, first_out, second_out, low_out, params_out,
+    small_first_out, small_second_out,
+    stage_ref, old_ref, copy_sem, tile_sem
+):
+    row_rank, part_rank = rank_ref[0], rank_ref[1]
+    rows = output_own.shape[0]
+    cap = tile_grad_ref.shape[0]
+    cuts = 4
+    copies = []
+    size = rows // cuts
+    for j in range(cuts):
+        own_rows = pl.ds(part_rank * rows + j * size, size)
+        other_rows = pl.ds((1 - part_rank) * rows + j * size, size)
+        part = pl.ds(j * size, size)
+        copies.append((output_own.at[part], output_ref.at[own_rows]))
+        copies.append((output_in.at[part], output_ref.at[other_rows]))
+        copies.append((grad_in.at[own_rows], input_grad_ref.at[own_rows]))
+        copies.append((grad_in.at[other_rows], input_grad_ref.at[other_rows]))
+    reads = [
+        pltpu.make_async_copy(source, stage_ref.at[i], copy_sem.at[0, i])
+        for i, (source, _) in enumerate(copies)
+    ]
+    writes = [
+        pltpu.make_async_copy(stage_ref.at[i], landing, copy_sem.at[1, i])
+        for i, (_, landing) in enumerate(copies)
+    ]
+    tiles = [slot_ref[row_rank * cap + c] for c in range(cap)]
+    olds = [
+        pltpu.make_async_copy(
+            weight_ref.at[part_rank, pl.ds(pl.multiple_of(jnp.maximum(t, 0) * BR, BR), BR)],
+            old_ref.at[c],
+            tile_sem.at[c],
+        )
+        for c, t in enumerate(tiles)
+    ]
+    for copy in olds:
+        copy.start()
+    for copy in reads:
+        copy.start()
+    params_out[...], small_first_out[...], small_second_out[...] = adam_step(
+        params_ref[...], small_ref[...], first_ref[...], second_ref[...], 0.0
+    )
+    for read, write in zip(reads, writes):
+        read.wait()
+        write.start()
+    for c, t in enumerate(tiles):
+        olds[c].wait()
+        new = adam_step(
+            old_ref[c].astype(F32), tile_grad_ref[c], tile_first_ref[0, c], tile_second_ref[0, c],
+            decay_rate,
+        )
+        live = [jnp.where(t >= 0, a, 0.0) for a in new]
+        weight_out[0, c] = live[0]
+        first_out[0, c] = live[1]
+        second_out[0, c] = live[2]
+        low_out[0, c] = live[0].astype(BF16)
+    for copy in writes:
+        copy.wait()
+
+
+def last_step(
+    slots, ranks, output_own, output_in, input_grad, weights, params, small_first, small_second,
+    small_sum, tile_grad, tile_first, tile_second
+):
+    vmem = pl.BlockSpec(memory_space=pltpu.VMEM)
+    anywhere = pl.BlockSpec(memory_space=pl.ANY)
+    smem = pl.BlockSpec(memory_space=pltpu.SMEM)
+    full = jax.ShapeDtypeStruct(input_grad.shape, F32)
+    tile = jax.ShapeDtypeStruct(tile_first.shape, F32)
+    small = jax.ShapeDtypeStruct(params.shape, F32)
+    return pl.pallas_call(
+        last_kernel,
+        in_specs=[smem, smem] + [anywhere] * 4 + [vmem] * 7,
+        out_specs=[anywhere] * 2 + [vmem] * 7,
+        out_shape=[
+            full, full, tile, tile, tile, jax.ShapeDtypeStruct(tile_first.shape, BF16), small,
+            small, small,
+        ],
+        scratch_shapes=[
+            pltpu.VMEM((16, output_own.shape[0] // 4, output_own.shape[1]), F32),
+            pltpu.VMEM(tile_grad.shape, BF16),
+            pltpu.SemaphoreType.DMA((2, 16)),
+            pltpu.SemaphoreType.DMA((tile_grad.shape[0],)),
+        ],
+        compiler_params=pltpu.CompilerParams(vmem_limit_bytes=60 << 20),
+    )(
+        slots, ranks, output_own, output_in, input_grad, weights, params, small_first, small_second,
+        small_sum, tile_grad, tile_first, tile_second
+    )
 
 
 def block_kernel(
-    filt_ref, tok_ref, mask_ref, cot_ref, stat_ref, params_ref, bias_ref, weight_ref,
-    out_ref, dres_ref, own_ref, peer_ref, small_ref, bias_grad_ref, grad_ref, *, node_total, parts, width, units, block
+    rank_ref, filt_ref, tok_ref, mask_ref, cot_ref, stat_ref, params_ref, weight_ref,
+    out_ref, dres_ref, own_ref, peer_ref, small_ref, grad_ref, *, node_total, parts, width, units, block
 ):
     i = pl.program_id(0)
 
@@ -699,7 +852,6 @@
     def _():
         grad_ref[...] = jnp.zeros_like(grad_ref)
         small_ref[...] = jnp.zeros_like(small_ref)
-        bias_grad_ref[...] = jnp.zeros_like(bias_grad_ref)
 
     part = width // parts
     unit_part = units // parts
@@ -784,14 +936,14 @@
     grad_ffn = cotangent.astype(BF16)
     ffn = jnp.zeros_like(after)
     grad_normed_two = jnp.zeros_like(after)
-    chunk = unit_part // 2
+    chunk = width
     for h in range(parts):
-        for c in range(2):
+        for c in range(unit_part // chunk):
             low = 4 * part + c * chunk
-            unit = h * unit_part + c * chunk
+            unit = 37 + (h * unit_part) // chunk + c
             fc1 = weight_ref[h, low : low + chunk]
             fc2 = weight_ref[h, low + unit_part : low + unit_part + chunk]
-            hidden = dot_last(normed_two, fc1) + bias_ref[0:1, unit : unit + chunk]
+            hidden = dot_last(normed_two, fc1) + param(unit)
             cumulative = 0.5 * (1.0 + lax.erf(hidden * 0.5**0.5))
             activation = (hidden * cumulative).astype(BF16)
             density = jnp.exp(-0.5 * hidden * hidden) * (2.0 * jnp.pi) ** (-0.5)
@@ -802,7 +954,7 @@
             grad_normed_two += dot_plain(grad_hidden, fc1)
             grad_ref[h, low : low + chunk] += dot_first(grad_hidden, normed_two)
             grad_ref[h, low + unit_part : low + unit_part + chunk] += dot_first(activation, grad_ffn)
-            bias_grad_ref[0:1, unit : unit + chunk] += col_sum(grad_hidden.astype(F32))
+            add_small(unit, col_sum(grad_hidden.astype(F32)))
     out_ref[...] = after + (ffn + param(34))
     add_small(34, col_sum(grad_ffn.astype(F32)))
 
@@ -856,38 +1008,47 @@
         peer_ref[...] = grad_ref[1 - mine].astype(BF16)
 
 
-def block_step(filtered, tokens, mask, cotangent, stat, params, bias, weights, node_total, block=256):
+def block_step(filtered, tokens, mask, cotangent, stat, params, weights, node_total, block=256):
     rows, width = filtered.shape
-    parts, units = weights.shape[0], bias.shape[1]
+    parts = weights.shape[0]
+    units = (weights.shape[1] - 4 * (width // parts)) // 2 * parts
+    blocks = rows // block
     outs = [
         jax.ShapeDtypeStruct((rows, width), F32),
         jax.ShapeDtypeStruct((rows, width), F32),
         jax.ShapeDtypeStruct(weights.shape[1:], F32),
         jax.ShapeDtypeStruct(weights.shape[1:], BF16),
         jax.ShapeDtypeStruct(params.shape, F32),
-        jax.ShapeDtypeStruct(bias.shape, F32),
     ]
-    by_rows = pl.BlockSpec((block, width), lambda i: (i, 0))
+
+    def whole(shape):
+        zeros = (0,) * len(shape)
+        return pl.BlockSpec(shape, lambda i, rank: zeros)
+
+    here = pl.BlockSpec((block, width), lambda i, rank: (i, 0))
+    chip = pl.BlockSpec((block, width), lambda i, rank: (rank[0] * blocks + i, 0))
     return pl.pallas_call(
         functools.partial(
             block_kernel, node_total=node_total, parts=parts, width=width, units=units, block=block
         ),
-        grid=(rows // block,),
-        in_specs=[
-            by_rows,
-            by_rows,
-            pl.BlockSpec((1, block), lambda i: (0, i)),
-            by_rows,
-            full_spec(stat.shape),
-            full_spec(params.shape),
-            full_spec(bias.shape),
-            full_spec(weights.shape),
-        ],
-        out_specs=[by_rows, by_rows] + [full_spec(o.shape) for o in outs[2:]],
+        grid_spec=pltpu.PrefetchScalarGridSpec(
+            num_scalar_prefetch=1,
+            grid=(blocks,),
+            in_specs=[
+                here,
+                chip,
+                pl.BlockSpec((1, block), lambda i, rank: (0, rank[0] * blocks + i)),
+                chip,
+                whole(stat.shape),
+                whole(params.shape),
+                whole(weights.shape),
+            ],
+            out_specs=[here, here] + [whole(o.shape) for o in outs[2:]],
+            scratch_shapes=[pltpu.VMEM(weights.shape, F32)],
+        ),
         out_shape=outs,
-        scratch_shapes=[pltpu.VMEM(weights.shape, F32)],
-        compiler_params=pltpu.CompilerParams(vmem_limit_bytes=58 << 20),
-    )(filtered, tokens, mask, cotangent, stat, params, bias, weights)
+        compiler_params=pltpu.CompilerParams(vmem_limit_bytes=60 << 20),
+    )(lax.axis_index("heads").reshape(1), filtered, tokens, mask, cotangent, stat, params, weights)
 
 
 def local(
@@ -901,24 +1062,16 @@
     part_rank = lax.axis_index("heads")
     rows = rows_here // parts
     node_total = rows_here * row_count
-    first = part_rank * rows
     tile_count = owners.shape[0]
     slot_cap = tile_first.shape[1]
 
-    def own(a):
-        return lax.dynamic_slice_in_dim(a, first, rows, 0)
-
     filtered, stat, near_t, extended, weights = filter_forward(
-        scene_lengths, tokens_in, neighbours, small_params, qkv_weight, proj_weight, fc1_weight,
+        scene_lengths, tokens_in, neighbours.T, small_params, qkv_weight, proj_weight, fc1_weight,
         fc2_weight, row_count, parts
     )
-    bias = small_params[37:].reshape(1, -1)
-    output, dres, own_grad, peer_grad, small_grad, bias_grad = block_step(
-        filtered, own(tokens_in), own(window_mask)[None], own(cotangent), stat, small_params, bias,
-        weights, node_total
-    )
-    output = lax.all_gather(output, "heads", axis=0, tiled=True)
-    dres_all = lax.all_gather(dres, "heads", axis=0, tiled=True)
+    output, dres, own_grad, peer_grad, small_grad = block_step(
+        filtered, tokens_in, window_mask[None], cotangent, stat, small_params, weights, node_total
+    )
 
     tile_order = jnp.arange(tile_count, dtype=jnp.int32)
     same_owner = (owners[:, None] == owners[None, :]) & (tile_order[None, :] < tile_order[:, None])
@@ -927,37 +1080,14 @@
     found = slot_of[None, :] == slot_ids[:, None]
     slot_tile = jnp.max(jnp.where(found, tile_order[None, :], -1), axis=1)
 
-    conv_back, small_sum, tile_grad = filter_backward(
-        slot_tile, extended, filtered, dres, near_t, small_params, stat, small_grad, bias_grad,
-        own_grad.reshape(tile_count, BR, width), peer_grad.reshape(tile_count, BR, width), slot_cap,
-        row_count, parts
-    )
-    input_grad = dres_all + conv_back.astype(F32)
-    small_new, small_first_new, small_second_new = adam_step(
-        small_params, small_sum, small_first, small_second, 0.0
-    )
-    own_slots = lax.dynamic_slice_in_dim(slot_tile, row_rank * slot_cap, slot_cap)
-    live = (own_slots >= 0).astype(F32)[:, None, None]
-    weight_tiles = lax.dynamic_index_in_dim(weights, part_rank, 0, keepdims=False)
-    tile_old = jnp.take(
-        weight_tiles.reshape(tile_count, BR, width), jnp.maximum(own_slots, 0), axis=0
-    ).astype(F32)
-    new_weight, new_first, new_second = adam_step(
-        tile_old, tile_grad, tile_first[0], tile_second[0], decay_rate
-    )
-    new_weight = new_weight * live
-    new_first = new_first * live
-    new_second = new_second * live
-    return (
-        output,
-        input_grad,
-        new_weight[None],
-        new_first[None],
-        new_second[None],
-        new_weight.astype(BF16)[None],
-        small_new,
-        small_first_new,
-        small_second_new,
+    input_grad, output_in, small_sum, tile_grad = filter_backward(
+        slot_tile, extended, filtered, dres, near_t, small_params, stat, small_grad,
+        own_grad.reshape(tile_count, BR, width), peer_grad.reshape(tile_count, BR, width), output,
+        slot_cap, row_count, parts
+    )
+    return last_step(
+        slot_tile, jnp.stack([row_rank, part_rank]), output, output_in, input_grad, weights,
+        small_params, small_first, small_second, small_sum, tile_grad, tile_first, tile_second
     )
 
 

time: 190 us -> 151 us (0.79)
  local copies, waits for them, and re-layouts: 26.1 us -> 0 us
  between operations: 14.2 us -> 0.85 us
  Pallas kernels: 139 us -> 147 us
  other arithmetic: 8.8 us -> 2.89 us
    unnamed x52 -> x0, local copies, waits for them, and re-layouts: 18.1 us -> none
    pallas_call x0 -> x1, Pallas kernels: none -> 8.01 us  [last_step(): pl.pallas_call(last_kernel, in_specs=[smem, smem] + [anywhere] * 4 + [vme...]
    dynamic_slice x4 -> x0, local copies, waits for them, and re-layouts: 5.68 us -> none  [the longest x1 2.87 us: local(): lax.dynamic_index_in_dim(weights, part_rank, 0, keepdims=False)]
    add x1 -> x0, other arithmetic: 4.42 us -> none  [local(): input_grad = dres_all + conv_back.astype(F32)]
    pallas_call x1, Pallas kernels: 62.9 us -> 59 us  [filter_backward(): pl.pallas_call(functools.partial(filter_back_kernel, block=block, row_cou...]
    pallas_call x1, Pallas kernels: 27.7 us -> 31.1 us  [filter_forward(): pl.pallas_call(functools.partial(filter_kernel, block=block, row_count=ro...]
    broadcast_in_dim x1 -> x0, other arithmetic: 2.39 us -> none  [local(): new_weight.astype(BF16)[None]]
    gather x1 -> x0, local copies, waits for them, and re-layouts: 2.27 us -> none  [local(): jnp.take(weight_tiles.reshape(tile_count, BR, width), jnp.maximum(own_slo...]
  transfers between devices with their start and end apart: 2 -> 0, of which waited for: 0 -> 0; matrix products, arithmetic and copies ran while one was open for 5% -> 0% of each run, Pallas kernels for 33% -> 0%
where the time goes in v3:
time: 151 us; the launch traced here: 150 us
  Pallas kernels  147 us (97%)
  other arithmetic  2.89 us (2%)
    pallas_call x1, Pallas kernels, filter_backward(): pl.pallas_call(functools.partial(filter_back_kernel, block=block, row_cou...  59 us
    pallas_call x1, Pallas kernels, block_step(): pl.pallas_call(functools.partial(block_kernel, node_total=node_total, par...  48.6 us
    pallas_call x1, Pallas kernels, filter_forward(): pl.pallas_call(functools.partial(filter_kernel, block=block, row_count=ro...  31.1 us
    pallas_call x1, Pallas kernels, last_step(): pl.pallas_call(last_kernel, in_specs=[smem, smem] + [anywhere] * 4 + [vme...  8.01 us

profile of v3, /device:TPU:0, one launch (start us, length us, event | category | flops | bytes accessed | tf_op | source)
XLA Modules:
  0.0 150.5 jit_solution(11313056197434183626)
XLA Ops:
  0.6 0.6 pad_add_fusion.rank_ref
  1.2 0.9 convert_reduce_fusion
  2.1 0.7 multiply_add_fusion
  2.8 0.7 select_reduce_fusion.slot_ref
  3.5 31.1 %shard_map.214 = (f32[1024,384]{1,0:T(8,128)}, f32[8,384]{1,0:T(8,128)}, s32[32,1024]{1,0:T(8,128)}, bf16[1280,384]{1,0:T(8,128)(2,1)}, bf16[2,2304,384]{2,1,0:T(8,128)(2,1)}) custom-call(s32[4]{0:T(128)} %lengths_ref.1, bf16[2048,384]{1,0:T(8,128)(2,1)} %tok_ref.1, s32[27,2048]{1,0:T(8,128)} %bitcast.8, f32[41,384]{1,0:T(8,128)} %params_ref.5, ...), custom_call_target="tpu_custom_call" | custom-call | tf_op jit(solution)/shard_map/pallas_call | solution.py:340
  34.7 48.6 %shard_map.215 = (f32[1024,384]{1,0:T(8,128)}, f32[1024,384]{1,0:T(8,128)}, f32[2304,384]{1,0:T(8,128)}, bf16[2304,384]{1,0:T(8,128)(2,1)}, f32[41,384]{1,0:T(8,128)}) custom-call(s32[1]{0:T(128)} %bitcast.1.rank_ref, f32[1024,384]{1,0:T(8,128)} %get-tuple-element.23.filt_ref.filt_hbm, bf16[2048,384]{1,0:T(8,128)(2,1)} %tok_ref.1, s32[1,2048]{1,0:T(1,128)} %bitcast.9, ...), custom_call_target="tpu_custom_call" | custom-call | tf_op jit(solution)/shard_map/pallas_call | solution.py:1030
  83.3 59.0 %shard_map.216 = (f32[2048,384]{1,0:T(8,128)}, f32[1024,384]{1,0:T(8,128)}, f32[41,384]{1,0:T(8,128)}, f32[14,16,384]{2,1,0:T(8,128)}) custom-call(s32[224]{0:T(256)} %select_reduce_fusion.slot_ref, bf16[1280,384]{1,0:T(8,128)(2,1)} %get-tuple-element.27.ext_hbm, f32[1024,384]{1,0:T(8,128)} %get-tuple-element.23.filt_ref.filt_hbm, ...), custom_call_target="tpu_custom_call" | custom-call | tf_op jit(solution)/shard_map/pallas_call | solution.py:690
  142.3 8.0 %shard_map.217 = (f32[2048,384]{1,0:T(8,128)}, f32[2048,384]{1,0:T(8,128)}, f32[1,14,16,384]{3,2,1,0:T(8,128)}, f32[1,14,16,384]{3,2,1,0:T(8,128)}, f32[1,14,16,...) custom-call(s32[224]{0:T(256)} %select_reduce_fusion.slot_ref, ...), custom_call_target="tpu_custom_call" | custom-call | tf_op jit(solution)/shard_map/pallas_call | solution.py:824

commit v4 on v3

--- a/solution.py
+++ b/solution.py
@@ -367,16 +367,20 @@
 
 
 def streams_of(cap, depth):
-    third = cap // 7 if depth > 2 else 0
-    counts = [(cap - 2 * third + 1) // 2, (cap - 2 * third) // 2, third, third]
-    found = []
+    seventh = cap // 7 if depth > 2 else 0
+    rest = cap - 2 * seventh
+    sizes = [
+        (0, 0, rest // 2 // 2), (1, 0, (rest - rest // 2) // 2), (2, 0, seventh),
+        (0, 1, rest // 2 - rest // 2 // 2), (1, 1, (rest - rest // 2) - (rest - rest // 2) // 2),
+        (3, 0, seventh),
+    ]
+    streams = []
     slot = 0
-    for order, count in enumerate(counts):
-        for j in range(count):
-            place = j if order < 2 else 2 * j + order - 2
-            found.append((place, order, slot))
-            slot += 1
-    return [(order, slot, place) for place, order, slot in sorted(found)]
+    for order, place, size in sizes:
+        if size:
+            streams.append((order, slot, size, place))
+            slot += size
+    return streams
 
 
 def bits_of(depth, order):
@@ -441,93 +445,96 @@
     send_to_all(lambda other: tile, landed, sum_send, sum_recv, count, parts, me)
 
     keep_at = {}
-    for i, (order, _, _) in enumerate(streams):
+    for i, (order, _, _, _) in enumerate(streams):
         keep_at[i, 0] = 0
         for t, bit in enumerate(bits_of(depth, order)):
             half = row_count >> (t + 1)
             keep_at[i, t + 1] = keep_at[i, t] + lax.rem(row_rank // (1 << bit), 2) * half
 
-    in_flight = 2
-    follower = {}
-    for i, (order, _, place) in enumerate(streams):
-        for j, (other_order, _, other_place) in enumerate(streams):
-            if min(order, 2) == min(other_order, 2) and other_place == place + in_flight:
-                follower[i] = j
-
     def give_at(i, t):
         return 2 * keep_at[i, t] + (row_count >> (t + 1)) - keep_at[i, t + 1]
 
-    def tile_at(i, p):
-        order, slot, _ = streams[i]
+    def slots_of(i):
+        return pl.ds(streams[i][1], streams[i][2])
+
+    def tile_at(i, c, p):
+        order, slot, _, _ = streams[i]
         owner = 0
         for t, bit in enumerate(bits_of(depth, order)):
             owner = owner + lax.rem(p // (1 << (depth - 1 - t)), 2) * (1 << bit)
-        return slot_ref[owner * cap + slot]
+        return slot_ref[owner * cap + slot + c]
 
     def pair_copy(i):
+        part = slots_of(i)
         return swap_copy(
-            pair_out.at[i], pair_in.at[i], pair_send.at[i], pair_recv.at[i], other_core
+            pair_out.at[part], pair_in.at[part], pair_send.at[i], pair_recv.at[i], other_core
         )
 
     def pair_start(i):
-        def body(p, carry):
-            index = tile_at(i, p)
-            value = peer_ref[jnp.maximum(index, 0)]
-            pair_out[i, p] = jnp.where(index >= 0, value, jnp.zeros_like(value))
-            return carry
-
-        lax.fori_loop(0, row_count, body, 0, unroll=8)
+        for c in range(streams[i][2]):
+
+            def body(p, carry, c=c):
+                index = tile_at(i, c, p)
+                value = peer_ref[jnp.maximum(index, 0)]
+                pair_out[streams[i][1] + c, p] = jnp.where(index >= 0, value, jnp.zeros_like(value))
+                return carry
+
+            lax.fori_loop(0, row_count, body, 0, unroll=8)
         pair_copy(i).start()
 
     def tree_copy(i, t):
-        order, _, _ = streams[i]
+        order = streams[i][0]
         half = row_count >> (t + 1)
         part = pl.ds(row_count - (row_count >> t), half)
+        here = slots_of(i)
         return swap_copy(
-            staged.at[i, part], arrived.at[i, part], tree_send.at[i, t], tree_recv.at[i, t],
+            staged.at[here, part], arrived.at[here, part], tree_send.at[i, t], tree_recv.at[i, t],
             (flip(row_rank, bits_of(depth, order)[t]), part_rank),
         )
 
     def pair_end(i):
         pair_copy(i).wait()
-
-        def value_at(p):
-            index = tile_at(i, p)
+        _, slot, size, _ = streams[i]
+
+        def value_at(c, p):
+            index = tile_at(i, c, p)
             value = own_ref[jnp.maximum(index, 0)]
-            return jnp.where(index >= 0, value, 0.0) + pair_in[i, p].astype(F32)
-
-        def give(p, carry):
-            staged[i, p] = value_at(give_at(i, 0) + p).astype(BF16)
-            return carry
-
-        def keep(p, carry):
-            sums[i, keep_at[i, 1] + p] = value_at(keep_at[i, 1] + p)
-            return carry
-
-        lax.fori_loop(0, row_count // 2, give, 0, unroll=8)
-        if streams[i][2] < in_flight:
-            tree_copy(i, 0).start()
-        lax.fori_loop(0, row_count // 2, keep, 0, unroll=8)
+            return jnp.where(index >= 0, value, 0.0) + pair_in[slot + c, p].astype(F32)
+
+        for c in range(size):
+
+            def give(p, carry, c=c):
+                staged[slot + c, p] = value_at(c, give_at(i, 0) + p).astype(BF16)
+                return carry
+
+            lax.fori_loop(0, row_count // 2, give, 0, unroll=8)
+        tree_copy(i, 0).start()
+        for c in range(size):
+
+            def keep(p, carry, c=c):
+                sums[slot + c, keep_at[i, 1] + p] = value_at(c, keep_at[i, 1] + p)
+                return carry
+
+            lax.fori_loop(0, row_count // 2, keep, 0, unroll=8)
 
     def tree_step(i, t):
         came = row_count - (row_count >> t)
         tree_copy(i, t).wait()
-        if t == 0 and i in follower:
-            tree_copy(follower[i], 0).start()
         low = keep_at[i, t + 1]
+        here = slots_of(i)
 
         def values(k, size):
-            return sums[i, pl.ds(k, size)] + arrived[i, pl.ds(came + k - low, size)].astype(F32)
+            return sums[here, pl.ds(k, size)] + arrived[here, pl.ds(came + k - low, size)].astype(F32)
 
         if t + 1 < depth:
             half = row_count >> (t + 2)
             at = row_count - (row_count >> (t + 1))
-            staged[i, at : at + half] = values(give_at(i, t + 1), half).astype(BF16)
+            staged[here, at : at + half] = values(give_at(i, t + 1), half).astype(BF16)
             tree_copy(i, t + 1).start()
             k = keep_at[i, t + 2]
-            sums[i, pl.ds(k, half)] = values(k, half)
+            sums[here, pl.ds(k, half)] = values(k, half)
         else:
-            tile_out_ref[streams[i][1]] = values(low, 1)[0]
+            tile_out_ref[here] = values(low, 1)[:, 0]
 
     loads[0].wait()
     for i in range(wide):
@@ -583,9 +590,9 @@
     group = 3
     points = TAPS // group
     schedule = {}
-    for i, (_, _, place) in enumerate(streams):
+    for i, (_, _, _, place) in enumerate(streams):
         for t in range(depth):
-            due = 2 * place + 9 * t + 8
+            due = 10 + 8 * place + 9 * t
             schedule.setdefault(min(due, blocks * points), []).append((due, t, i))
 
     def step(it, carry):
@@ -686,7 +693,7 @@
     vmem = pl.BlockSpec(memory_space=pltpu.VMEM)
     anywhere = pl.BlockSpec(memory_space=pl.ANY)
     dma = pltpu.SemaphoreType.DMA
-    of_streams = (wide, row_count, BR, width)
+    of_streams = (cap, row_count, BR, width)
     return pl.pallas_call(
         functools.partial(
             filter_back_kernel, block=block, row_count=row_count, parts=parts, cap=cap,
@@ -907,27 +914,36 @@
     def cut(a, s, g):
         return a[s * side : (s + 1) * side, g * LANES : (g + 1) * LANES]
 
-    kept = {}
-    mixture = []
-    for s in range(block // side):
-        keep = (window_q == window_k) & (mask_ref[0:1, s * side : (s + 1) * side] > 0)
-        mixed = []
-        for g in range(groups):
-            query_g = cut(query, s, g)
-            keys = stack_heads(cut(key, s, g))
-            values = stack_heads(cut(value, s, g))
-            scores = dot_last(query_g, keys)
-            probs = []
-            for j in range(heads):
-                score = jnp.where(keep, scores[:, j * side : (j + 1) * side], masked_score)
-                power = jnp.exp(score - jnp.max(score, axis=1, keepdims=True))
-                probs.append(power / jnp.sum(power, axis=1, keepdims=True))
-            probs = jnp.concatenate(probs, axis=1)
-            probs_low = probs.astype(BF16)
-            mixed.append(dot_plain(probs_low, values))
-            kept[s, g] = (query_g, keys, values, probs, probs_low)
-        mixture.append(jnp.concatenate(mixed, axis=1))
-    mixture = jnp.concatenate(mixture, axis=0).astype(BF16)
+    sides = block // side
+    pairs = [(s, g) for s in range(sides) for g in range(groups)]
+
+    def join(pieces):
+        return jnp.concatenate(
+            [
+                jnp.concatenate(pieces[s * groups : (s + 1) * groups], axis=1)
+                for s in range(sides)
+            ],
+            axis=0,
+        )
+
+    keeps = [
+        (window_q == window_k) & (mask_ref[0:1, s * side : (s + 1) * side] > 0)
+        for s in range(sides)
+    ]
+    queries = [cut(query, s, g) for s, g in pairs]
+    keys = [stack_heads(cut(key, s, g)) for s, g in pairs]
+    values = [stack_heads(cut(value, s, g)) for s, g in pairs]
+    scores = [dot_last(a, b) for a, b in zip(queries, keys)]
+    probs = []
+    for (s, _), score_all in zip(pairs, scores):
+        here = []
+        for j in range(heads):
+            score = jnp.where(keeps[s], score_all[:, j * side : (j + 1) * side], masked_score)
+            power = jnp.exp(score - jnp.max(score, axis=1, keepdims=True))
+            here.append(power * (1.0 / jnp.sum(power, axis=1, keepdims=True)))
+        probs.append(jnp.concatenate(here, axis=1))
+    probs_low = [p.astype(BF16) for p in probs]
+    mixture = join([dot_plain(p, v) for p, v in zip(probs_low, values)]).astype(BF16)
     after = resid + (dot_plain(mixture, proj_rows()) + param(33))
     unit_two, factor_two = layer_norm(after)
     normed_two = (unit_two * param(31) + param(32)).astype(BF16)
@@ -936,14 +952,17 @@
     grad_ffn = cotangent.astype(BF16)
     ffn = jnp.zeros_like(after)
     grad_normed_two = jnp.zeros_like(after)
-    chunk = width
+    chunk = unit_part
     for h in range(parts):
         for c in range(unit_part // chunk):
             low = 4 * part + c * chunk
-            unit = 37 + (h * unit_part) // chunk + c
+            unit = 37 + (h * unit_part + c * chunk) // width
+            bias_rows = range(unit, unit + chunk // width)
             fc1 = weight_ref[h, low : low + chunk]
             fc2 = weight_ref[h, low + unit_part : low + unit_part + chunk]
-            hidden = dot_last(normed_two, fc1) + param(unit)
+            hidden = dot_last(normed_two, fc1) + jnp.concatenate(
+                [param(r) for r in bias_rows], axis=1
+            )
             cumulative = 0.5 * (1.0 + lax.erf(hidden * 0.5**0.5))
             activation = (hidden * cumulative).astype(BF16)
             density = jnp.exp(-0.5 * hidden * hidden) * (2.0 * jnp.pi) ** (-0.5)
@@ -954,7 +973,9 @@
             grad_normed_two += dot_plain(grad_hidden, fc1)
             grad_ref[h, low : low + chunk] += dot_first(grad_hidden, normed_two)
             grad_ref[h, low + unit_part : low + unit_part + chunk] += dot_first(activation, grad_ffn)
-            add_small(unit, col_sum(grad_hidden.astype(F32)))
+            bias_sum = col_sum(grad_hidden.astype(F32))
+            for j, r in enumerate(bias_rows):
+                add_small(r, bias_sum[:, j * width : (j + 1) * width])
     out_ref[...] = after + (ffn + param(34))
     add_small(34, col_sum(grad_ffn.astype(F32)))
 
@@ -966,27 +987,20 @@
     add_small(33, col_sum(grad_branch.astype(F32)))
     grad_mixture = dot_last(grad_branch, proj_rows()).astype(BF16)
 
-    grads = ([], [], [])
-    for s in range(block // side):
-        here = ([], [], [])
-        for g in range(groups):
-            query_g, keys, values, probs, probs_low = kept[s, g]
-            grad_mix = cut(grad_mixture, s, g)
-            grad_probs = dot_last(grad_mix, values)
-            grad_scores = []
-            for j in range(heads):
-                prob = probs[:, j * side : (j + 1) * side]
-                term = prob * grad_probs[:, j * side : (j + 1) * side]
-                grad_scores.append(
-                    (term - prob * jnp.sum(term, axis=1, keepdims=True)).astype(BF16)
-                )
-            grad_scores = jnp.concatenate(grad_scores, axis=1)
-            here[0].append(dot_plain(grad_scores, keys))
-            here[1].append(pick_heads(dot_first(grad_scores, query_g)))
-            here[2].append(pick_heads(dot_first(probs_low, grad_mix)))
-        for kind in range(3):
-            grads[kind].append(jnp.concatenate(here[kind], axis=1))
-    grad_qkv = [jnp.concatenate(kind, axis=0).astype(BF16) for kind in grads]
+    grad_mix = [cut(grad_mixture, s, g) for s, g in pairs]
+    grad_probs = [dot_last(a, v) for a, v in zip(grad_mix, values)]
+    grad_values = [pick_heads(dot_first(p, a)) for p, a in zip(probs_low, grad_mix)]
+    grad_scores = []
+    for prob_all, grad_all in zip(probs, grad_probs):
+        here = []
+        for j in range(heads):
+            prob = prob_all[:, j * side : (j + 1) * side]
+            term = prob * grad_all[:, j * side : (j + 1) * side]
+            here.append((term - prob * jnp.sum(term, axis=1, keepdims=True)).astype(BF16))
+        grad_scores.append(jnp.concatenate(here, axis=1))
+    grad_queries = [dot_plain(a, k) for a, k in zip(grad_scores, keys)]
+    grad_keys = [pick_heads(dot_first(a, q)) for a, q in zip(grad_scores, queries)]
+    grad_qkv = [join(kind).astype(BF16) for kind in (grad_queries, grad_keys, grad_values)]
     grad_normed_one = jnp.zeros_like(resid)
     for j in range(3):
         grad_normed_one += dot_plain(grad_qkv[j], qkv_rows(j))
@@ -1008,7 +1022,7 @@
         peer_ref[...] = grad_ref[1 - mine].astype(BF16)
 
 
-def block_step(filtered, tokens, mask, cotangent, stat, params, weights, node_total, block=256):
+def block_step(filtered, tokens, mask, cotangent, stat, params, weights, node_total, block=512):
     rows, width = filtered.shape
     parts = weights.shape[0]
     units = (weights.shape[1] - 4 * (width // parts)) // 2 * parts

time: 151 us -> 130 us (0.86)
  Pallas kernels: 147 us -> 126 us
    pallas_call x1, Pallas kernels: 48.6 us -> 32.6 us  [block_step(): pl.pallas_call(functools.partial(block_kernel, node_total=node_total, par...]
    pallas_call x1, Pallas kernels: 59 us -> 54.1 us  [filter_backward(): pl.pallas_call(functools.partial(filter_back_kernel, block=block, row_cou...]
where the time goes in v4:
time: 130 us
  Pallas kernels  126 us (97%)
  other arithmetic  2.89 us (2%)
    pallas_call x1, Pallas kernels, filter_backward(): pl.pallas_call(functools.partial(filter_back_kernel, block=block, row_cou...  54.1 us
    pallas_call x1, Pallas kernels, block_step(): pl.pallas_call(functools.partial(block_kernel, node_total=node_total, par...  32.6 us
    pallas_call x1, Pallas kernels, filter_forward(): pl.pallas_call(functools.partial(filter_kernel, block=block, row_count=ro...  31.1 us
    pallas_call x1, Pallas kernels, last_step(): pl.pallas_call(last_kernel, in_specs=[smem, smem] + [anywhere] * 4 + [vme...  8.01 us

profile of v4, /device:TPU:0, one launch (start us, length us, event | category | flops | bytes accessed | tf_op | source)
XLA Modules:
  0.0 129.6 jit_solution(4682939152618564549)
XLA Ops:
  0.6 0.6 pad_add_fusion.rank_ref
  1.2 0.9 convert_reduce_fusion
  2.1 0.7 multiply_add_fusion
  2.8 0.7 select_reduce_fusion.slot_ref
  3.5 31.1 %shard_map.214 = (f32[1024,384]{1,0:T(8,128)}, f32[8,384]{1,0:T(8,128)}, s32[32,1024]{1,0:T(8,128)}, bf16[1280,384]{1,0:T(8,128)(2,1)}, bf16[2,2304,384]{2,1,0:T(8,128)(2,1)}) custom-call(s32[4]{0:T(128)} %lengths_ref.1, bf16[2048,384]{1,0:T(8,128)(2,1)} %tok_ref.1, s32[27,2048]{1,0:T(8,128)} %bitcast.8, f32[41,384]{1,0:T(8,128)} %params_ref.5, ...), custom_call_target="tpu_custom_call" | custom-call | tf_op jit(solution)/shard_map/pallas_call | solution.py:340
  34.7 32.6 %shard_map.215 = (f32[1024,384]{1,0:T(8,128)}, f32[1024,384]{1,0:T(8,128)}, f32[2304,384]{1,0:T(8,128)}, bf16[2304,384]{1,0:T(8,128)(2,1)}, f32[41,384]{1,0:T(8,128)}) custom-call(s32[1]{0:T(128)} %bitcast.1.rank_ref, f32[1024,384]{1,0:T(8,128)} %get-tuple-element.23.filt_ref.filt_hbm, bf16[2048,384]{1,0:T(8,128)(2,1)} %tok_ref.1, s32[1,2048]{1,0:T(1,128)} %bitcast.9, ...), custom_call_target="tpu_custom_call" | custom-call | tf_op jit(solution)/shard_map/pallas_call | solution.py:1044
  67.3 54.1 %shard_map.216 = (f32[2048,384]{1,0:T(8,128)}, f32[1024,384]{1,0:T(8,128)}, f32[41,384]{1,0:T(8,128)}, f32[14,16,384]{2,1,0:T(8,128)}) custom-call(s32[224]{0:T(256)} %select_reduce_fusion.slot_ref, bf16[1280,384]{1,0:T(8,128)(2,1)} %get-tuple-element.27.ext_hbm, f32[1024,384]{1,0:T(8,128)} %get-tuple-element.23.filt_ref.filt_hbm, ...), custom_call_target="tpu_custom_call" | custom-call | tf_op jit(solution)/shard_map/pallas_call | solution.py:697
  121.4 8.0 %shard_map.217 = (f32[2048,384]{1,0:T(8,128)}, f32[2048,384]{1,0:T(8,128)}, f32[1,14,16,384]{3,2,1,0:T(8,128)}, f32[1,14,16,384]{3,2,1,0:T(8,128)}, f32[1,14,16,...) custom-call(s32[224]{0:T(256)} %select_reduce_fusion.slot_ref, ...), custom_call_target="tpu_custom_call" | custom-call | tf_op jit(solution)/shard_map/pallas_call | solution.py:831

commit v5 on v4

v5 whole, which is shorter than its diff:
```python
import functools

import jax
import jax.numpy as jnp
from jax import lax
from jax.experimental import pallas as pl
from jax.experimental.pallas import tpu as pltpu
from jax.sharding import PartitionSpec as P

HEAD_DIM = 32
WIN = 32
HALO = 128
BR = 16
STEP = 3
TAPS = 27
LANES = 128

norm_eps = 1e-05
adam_rate = 0.05
beta_one = 0.5
beta_two = 0.5
adam_eps = 1e-08
decay_rate = 0.05
masked_score = -1e30

F32 = jnp.float32
BF16 = jnp.bfloat16


def adam_step(weight, gradient, first_moment, second_moment, decay_factor):
    first_new = beta_one * first_moment + (1.0 - beta_one) * gradient
    second_new = beta_two * second_moment + (1.0 - beta_two) * gradient * gradient
    first_hat = first_new / (1.0 - beta_one**STEP)
    second_hat = second_new / (1.0 - beta_two**STEP)
    weight_new = weight - adam_rate * (
        first_hat / (jnp.sqrt(second_hat) + adam_eps) + decay_factor * weight
    )
    return (weight_new, first_new, second_new)


def dot_plain(a, b):
    return jnp.dot(a, b, preferred_element_type=F32)


def dot_last(a, b):
    return lax.dot_general(a, b, (((1,), (1,)), ((), ())), preferred_element_type=F32)


def dot_first(a, b):
    return lax.dot_general(a, b, (((0,), (0,)), ((), ())), preferred_element_type=F32)


def col_sum(v):
    return jnp.sum(v, axis=0, keepdims=True)


def layer_norm(v):
    centre = v - jnp.mean(v, axis=1, keepdims=True)
    factor = lax.rsqrt(jnp.mean(centre * centre, axis=1, keepdims=True) + norm_eps)
    return centre * factor, factor


def norm_back(upstream, unit_part, factor, gain):
    scaled = upstream * gain
    return factor * (
        scaled
        - jnp.mean(scaled, axis=1, keepdims=True)
        - unit_part * jnp.mean(scaled * unit_part, axis=1, keepdims=True)
    )


def full_spec(shape):
    zeros = (0,) * len(shape)
    return pl.BlockSpec(shape, lambda i: zeros)


MESH = pl.DeviceIdType.MESH


def device_of(index, parts):
    return (index // parts, lax.rem(index, parts))


def greet_all(count, parts, me):
    barrier = pltpu.get_barrier_semaphore()

    def greet(j, carry):
        pl.semaphore_signal(
            barrier, inc=1, device_id=device_of(lax.rem(me + j, count), parts), device_id_type=MESH
        )
        return carry

    lax.fori_loop(1, count, greet, 0)


def await_all(count):
    pl.semaphore_wait(pltpu.get_barrier_semaphore(), count - 1)


def swap_copy(source, landing, send_sem, recv_sem, device):
    return pltpu.make_async_remote_copy(
        src_ref=source, dst_ref=landing, send_sem=send_sem, recv_sem=recv_sem,
        device_id=device, device_id_type=MESH,
    )


def send_to_all(source_of, landing, send_sem, recv_sem, count, parts, me):
    def send(j, carry):
        other = lax.rem(me + j, count)
        swap_copy(
            source_of(other), landing.at[count - j], send_sem.at[j], recv_sem.at[count - j],
            device_of(other, parts),
        ).start()
        return carry

    lax.fori_loop(1, count, send, 0)


def await_from_all(source, landing, send_sem, recv_sem, count, parts, me):
    def wait(j, carry):
        swap_copy(
            source, landing.at[count - j], send_sem.at[j], recv_sem.at[count - j],
            device_of(lax.rem(me + j, count), parts),
        ).wait()
        return carry

    lax.fori_loop(1, count, wait, 0)


def add_landed(own, landing, count):
    return lax.fori_loop(1, count, lambda j, total: total + landing[j], own)


def to_tile(tile_ref, rows):
    tile_ref[...] = jnp.zeros_like(tile_ref)
    groups = rows[0].shape[1] // LANES
    for r, row in enumerate(rows):
        for g in range(groups):
            at = r * groups + g
            tile_ref[at : at + 1, :] = row[:, g * LANES : (g + 1) * LANES]


def from_tile(tile, row, groups):
    at = row * groups
    return jnp.concatenate([tile[at + g : at + g + 1, :] for g in range(groups)], axis=1)


def streams_of(cap, depth):
    seventh = cap // 7 if depth > 2 else 0
    rest = cap - 2 * seventh
    sizes = [
        (0, 0, rest // 2 // 2), (1, 0, (rest - rest // 2) // 2), (2, 0, seventh),
        (0, 1, rest // 2 - rest // 2 // 2), (1, 1, (rest - rest // 2) - (rest - rest // 2) // 2),
        (3, 0, seventh),
    ]
    streams = []
    slot = 0
    for order, place, size in sizes:
        if size:
            streams.append((order, slot, size, place))
            slot += size
    return streams


def bits_of(depth, order):
    bits = list(range(depth))
    if order == 1 and depth > 1:
        bits[:2] = [1, 0]
    if order == 2:
        bits[:3] = [2, 0, 1]
    if order == 3:
        bits[:3] = [2, 1, 0]
    return bits


def flip(rank, bit):
    weight = 1 << bit
    return rank + weight - 2 * weight * lax.rem(rank // weight, 2)


def step_kernel(
    lengths_ref, slot_ref, tokens_hbm, near_hbm, cot_hbm, qkv_hbm, proj_hbm, fc1_hbm, fc2_hbm,
    tile_first_hbm, tile_second_hbm, mask_ref, params_ref, small_first_ref, small_second_ref,
    output_ref, input_grad_ref, weight_out, first_out, second_out, low_out, params_out,
    small_first_out, small_second_out,
    near_in, near_t, ext_ref, filt_ref, stat_ref, stack_ref, cot_ref, stack_grad, small_ref,
    total_ref, grad_ref, rim_ref, rim_in, pair_in, staged, arrived, sums, tile_sum, tile_first_ref,
    tile_second_ref, tile, landed, back_tile, back_landed, flat, flat_in, part_sum, flat_all,
    local_sem, side_sem, weight_sem, stat_send, stat_recv, back_send, back_recv, pair_send,
    pair_recv, tree_send, tree_recv, rim_sem, flat_send, flat_recv, all_send, all_recv, out_sem,
    *, filter_block, row_block, back_block, row_count, parts, cap, scenes
):
    row_rank = lax.axis_index("rows")
    part_rank = lax.axis_index("heads")
    count = row_count * parts
    me = row_rank * parts + part_rank
    other_core = (row_rank, 1 - part_rank)
    rows_here, width = tokens_hbm.shape
    rows = rows_here // parts
    first = part_rank * rows
    node_total = rows_here * row_count
    groups = width // LANES
    part = width // parts
    unit_part = fc1_hbm.shape[0] * BR
    depth = row_count.bit_length() - 1
    streams = streams_of(cap, depth)
    wide = len(streams)
    small_rows = params_ref.shape[0]
    scale = HEAD_DIM**-0.5
    greet_all(count, parts, me)

    own_copy = pltpu.make_async_copy(
        tokens_hbm.at[pl.ds(first, rows)], ext_ref.at[pl.ds(HALO, rows)], local_sem.at[0]
    )
    near_copy = pltpu.make_async_copy(
        near_hbm.at[:, pl.ds(pl.multiple_of(first, LANES), rows)], near_in, local_sem.at[1]
    )
    late_copies = [
        pltpu.make_async_copy(cot_hbm.at[pl.ds(first, rows)], cot_ref, local_sem.at[3]),
        pltpu.make_async_copy(tile_first_hbm, tile_first_ref, local_sem.at[4]),
        pltpu.make_async_copy(tile_second_hbm, tile_second_ref, local_sem.at[5]),
    ]
    own_copy.start()
    near_copy.start()
    low_side = ext_ref.at[pl.ds(0, HALO)]
    high_side = ext_ref.at[pl.ds(rows + HALO, HALO)]

    @pl.when(part_rank == 0)
    def _():
        pltpu.make_async_copy(tokens_hbm.at[pl.ds(rows, HALO)], high_side, local_sem.at[2]).start()

    @pl.when(part_rank == 1)
    def _():
        pltpu.make_async_copy(
            tokens_hbm.at[pl.ds(rows - HALO, HALO)], low_side, local_sem.at[2]
        ).start()

    @pl.when(me == 0)
    def _():
        ext_ref[0:HALO, :] = jnp.zeros((HALO, width), BF16)

    @pl.when(me == count - 1)
    def _():
        ext_ref[rows + HALO :, :] = jnp.zeros((HALO, width), BF16)

    pieces = []
    low = 0
    for ref in (qkv_hbm, proj_hbm, fc1_hbm, fc2_hbm):
        pieces.append((ref, low, ref.shape[0]))
        low += ref.shape[0]

    def own_weight(i):
        ref, at, size = pieces[i]
        return pltpu.make_async_copy(
            ref, stack_ref.at[part_rank, pl.ds(at, size)], weight_sem.at[0, i]
        )

    def sent_weight(i):
        _, at, size = pieces[i]
        here = stack_ref.at[part_rank, pl.ds(at, size)]
        return swap_copy(here, here, weight_sem.at[1, i], weight_sem.at[2, i], other_core)

    for i in range(len(pieces)):
        own_weight(i).start()
    for copy in late_copies:
        copy.start()

    def side_up():
        return swap_copy(
            tokens_hbm.at[pl.ds(rows_here - HALO, HALO)], low_side, side_sem.at[0], side_sem.at[1],
            (jnp.minimum(row_rank + 1, row_count - 1), part_rank),
        )

    def side_down():
        return swap_copy(
            tokens_hbm.at[pl.ds(0, HALO)], high_side, side_sem.at[0], side_sem.at[1],
            (jnp.maximum(row_rank - 1, 0), part_rank),
        )

    stat_ref[...] = jnp.zeros_like(stat_ref)
    stack_grad[...] = jnp.zeros_like(stack_grad)
    small_ref[...] = jnp.zeros_like(small_ref)
    total_ref[...] = jnp.zeros_like(total_ref)
    ends = []
    reached = 0
    for s in range(scenes):
        reached = reached + lengths_ref[s]
        ends.append(reached * WIN)
    near_copy.wait()
    own_copy.wait()

    block = filter_block
    blocks = rows // block
    span = block + 2 * HALO

    def filter_step(it, carry):
        @pl.when(it == 2)
        def _():
            await_all(count)

            @pl.when((part_rank == 0) & (row_rank < row_count - 1))
            def _():
                side_up().start()

            @pl.when((part_rank == 1) & (row_rank > 0))
            def _():
                side_down().start()

            for i in range(len(pieces)):
                own_weight(i).wait()
                sent_weight(i).start()

        @pl.when(it == blocks - 2)
        def _():
            pltpu.make_async_copy(
                tokens_hbm.at[pl.ds(0, HALO)], low_side, local_sem.at[2]
            ).wait()

            @pl.when((part_rank == 0) & (row_rank < row_count - 1))
            def _():
                side_up().wait_send()

            @pl.when((part_rank == 0) & (row_rank > 0))
            def _():
                side_up().wait_recv()

            @pl.when((part_rank == 1) & (row_rank > 0))
            def _():
                side_down().wait_send()

            @pl.when((part_rank == 1) & (row_rank < row_count - 1))
            def _():
                side_down().wait_recv()

        b = lax.rem(it + 1, blocks)
        base = pl.multiple_of(b * block, block)
        window = ext_ref[pl.ds(base, span), :]
        near = near_in[:, pl.ds(base, block)]
        lane = lax.broadcasted_iota(jnp.int32, (1, block), 1)
        own_row = row_rank * rows_here + first + base + lane
        scene_low = jnp.zeros_like(own_row)
        scene_high = jnp.full_like(own_row, node_total)
        for end in ends:
            passed = own_row >= end
            scene_low = jnp.maximum(scene_low, jnp.where(passed, end, 0))
            scene_high = jnp.minimum(scene_high, jnp.where(passed, node_total, end))
        target = own_row + near
        usable = (near >= -HALO) & (target >= scene_low) & (target < scene_high)
        place_t = jnp.where(usable, near + lane + HALO, -8 * HALO)
        near_t[0:TAPS, pl.ds(base, block)] = place_t
        place = jnp.transpose(
            jnp.concatenate([place_t, jnp.zeros((LANES - TAPS, block), jnp.int32)], axis=0)
        )
        column = lax.broadcasted_iota(jnp.int32, (block, span), 1)
        total = jnp.zeros((block, width), F32)
        group = 3
        for k0 in range(0, TAPS, group):
            hot = jnp.concatenate(
                [
                    (place[:, k : k + 1] == column).astype(F32).astype(BF16)
                    for k in range(k0, k0 + group)
                ],
                axis=0,
            )
            picked = dot_plain(hot, window)
            for j in range(group):
                total += picked[j * block : (j + 1) * block] * params_ref[k0 + j : k0 + j + 1, :]
        filt_ref[pl.ds(base, block), :] = total
        stat_ref[0:1, :] += col_sum(total)
        stat_ref[1:2, :] += col_sum(total * total)
        return carry

    lax.fori_loop(0, blocks, filter_step, 0)

    to_tile(tile, [stat_ref[0:1], stat_ref[1:2]])
    send_to_all(lambda other: tile, landed, stat_send, stat_recv, count, parts, me)
    for i in range(len(pieces)):
        sent_weight(i).wait()
    late_copies[0].wait()
    await_from_all(tile, landed, stat_send, stat_recv, count, parts, me)
    stat = add_landed(tile[...], landed, count)
    centre = from_tile(stat, 0, groups) / node_total
    inv_std = lax.rsqrt(from_tile(stat, 1, groups) / node_total - centre * centre + norm_eps)
    stat_ref[0:1, :] = centre
    stat_ref[1:2, :] = inv_std

    def weight_part(h, low, size):
        return stack_ref[h, low // BR : (low + size) // BR].reshape(size, width)

    def weight_rows(low, size):
        return jnp.concatenate([weight_part(h, low, size) for h in range(parts)], axis=0)

    def qkv_rows(j):
        return weight_rows(j * part, part)

    def proj_rows():
        return weight_rows(3 * part, part)

    def add_part(h, low, value):
        size = value.shape[0]
        stack_grad[h, low // BR : (low + size) // BR] += value.reshape(size // BR, BR, width)

    def add_grad(low, value):
        for h in range(parts):
            add_part(h, low, value[h * part : (h + 1) * part])

    def param(row):
        return params_ref[row : row + 1, :]

    def add_small(row, value):
        small_ref[row : row + 1, :] += value

    def out_copy(ref, sem, low, size):
        here = ref.at[pl.ds(pl.multiple_of(first + low, LANES), size)]
        return swap_copy(here, here, out_sem.at[0, sem], out_sem.at[1, sem], other_core)

    def row_step(it, carry):
        block = row_block
        base = pl.multiple_of(it * block, block)
        block_rows = pl.ds(base, block)
        there = pl.ds(pl.multiple_of(first + base, LANES), block)
        mask_at = (first + base) // LANES
        bn_norm = (filt_ref[block_rows, :] - stat_ref[0:1]) * stat_ref[1:2]
        resid = ext_ref[pl.ds(pl.multiple_of(base + HALO, HALO), block), :].astype(F32) + (
            bn_norm * param(27) + param(28)
        )
        unit_one, factor_one = layer_norm(resid)
        normed_one = (unit_one * param(29) + param(30)).astype(BF16)
        query = ((dot_last(normed_one, qkv_rows(0)) + param(35)) * scale).astype(BF16)
        key = (dot_last(normed_one, qkv_rows(1)) * scale).astype(BF16)
        value = ((dot_last(normed_one, qkv_rows(2)) + param(36)) * scale).astype(BF16)

        side = LANES
        heads = LANES // HEAD_DIM
        lane_head = lax.broadcasted_iota(jnp.int32, (side, LANES), 1) // HEAD_DIM
        window_q = lax.broadcasted_iota(jnp.int32, (side, side), 0) // WIN
        window_k = lax.broadcasted_iota(jnp.int32, (side, side), 1) // WIN

        def stack_heads(a):
            return jnp.concatenate(
                [jnp.where(lane_head == j, a, jnp.zeros_like(a)) for j in range(heads)], axis=0
            )

        def pick_heads(a):
            picked = a[:side]
            for j in range(1, heads):
                picked = jnp.where(lane_head == j, a[j * side : (j + 1) * side], picked)
            return picked

        def cut(a, s, g):
            return a[s * side : (s + 1) * side, g * LANES : (g + 1) * LANES]

        sides = block // side
        pairs = [(s, g) for s in range(sides) for g in range(groups)]

        def join(pieces):
            return jnp.concatenate(
                [
                    jnp.concatenate(pieces[s * groups : (s + 1) * groups], axis=1)
                    for s in range(sides)
                ],
                axis=0,
            )

        keeps = [
            (window_q == window_k) & (mask_ref[pl.ds(mask_at + s, 1), :] > 0)
            for s in range(sides)
        ]
        queries = [cut(query, s, g) for s, g in pairs]
        keys = [stack_heads(cut(key, s, g)) for s, g in pairs]
        values = [stack_heads(cut(value, s, g)) for s, g in pairs]
        scores = [dot_last(a, b) for a, b in zip(queries, keys)]
        probs = []
        for (s, _), score_all in zip(pairs, scores):
            here = []
            for j in range(heads):
                score = jnp.where(keeps[s], score_all[:, j * side : (j + 1) * side], masked_score)
                power = jnp.exp(score - jnp.max(score, axis=1, keepdims=True))
                here.append(power * (1.0 / jnp.sum(power, axis=1, keepdims=True)))
            probs.append(jnp.concatenate(here, axis=1))
        probs_low = [p.astype(BF16) for p in probs]
        mixture = join([dot_plain(p, v) for p, v in zip(probs_low, values)]).astype(BF16)
        after = resid + (dot_plain(mixture, proj_rows()) + param(33))
        unit_two, factor_two = layer_norm(after)
        normed_two = (unit_two * param(31) + param(32)).astype(BF16)

        cotangent = cot_ref[block_rows, :]
        grad_ffn = cotangent.astype(BF16)
        ffn = jnp.zeros_like(after)
        grad_normed_two = jnp.zeros_like(after)
        chunk = unit_part
        for h in range(parts):
            for c in range(unit_part // chunk):
                low = 4 * part + c * chunk
                unit = 37 + (h * unit_part + c * chunk) // width
                bias_rows = range(unit, unit + chunk // width)
                fc1 = weight_part(h, low, chunk)
                fc2 = weight_part(h, low + unit_part, chunk)
                hidden = dot_last(normed_two, fc1) + jnp.concatenate(
                    [param(r) for r in bias_rows], axis=1
                )
                cumulative = 0.5 * (1.0 + lax.erf(hidden * 0.5**0.5))
                activation = (hidden * cumulative).astype(BF16)
                density = jnp.exp(-0.5 * hidden * hidden) * (2.0 * jnp.pi) ** (-0.5)
                ffn += dot_plain(activation, fc2)
                grad_hidden = (
                    dot_last(grad_ffn, fc2) * (cumulative + hidden * density)
                ).astype(BF16)
                grad_normed_two += dot_plain(grad_hidden, fc1)
                add_part(h, low, dot_first(grad_hidden, normed_two))
                add_part(h, low + unit_part, dot_first(activation, grad_ffn))
                bias_sum = col_sum(grad_hidden.astype(F32))
                for j, r in enumerate(bias_rows):
                    add_small(r, bias_sum[:, j * width : (j + 1) * width])
        output_ref[there, :] = after + (ffn + param(34))
        add_small(34, col_sum(grad_ffn.astype(F32)))

        grad_after = cotangent + norm_back(grad_normed_two, unit_two, factor_two, param(31))
        add_small(31, col_sum(grad_normed_two * unit_two))
        add_small(32, col_sum(grad_normed_two))
        grad_branch = grad_after.astype(BF16)
        add_grad(3 * part, dot_first(mixture, grad_branch))
        add_small(33, col_sum(grad_branch.astype(F32)))
        grad_mixture = dot_last(grad_branch, proj_rows()).astype(BF16)

        grad_mix = [cut(grad_mixture, s, g) for s, g in pairs]
        grad_probs = [dot_last(a, v) for a, v in zip(grad_mix, values)]
        grad_values = [pick_heads(dot_first(p, a)) for p, a in zip(probs_low, grad_mix)]
        grad_scores = []
        for prob_all, grad_all in zip(probs, grad_probs):
            here = []
            for j in range(heads):
                prob = prob_all[:, j * side : (j + 1) * side]
                term = prob * grad_all[:, j * side : (j + 1) * side]
                here.append((term - prob * jnp.sum(term, axis=1, keepdims=True)).astype(BF16))
            grad_scores.append(jnp.concatenate(here, axis=1))
        grad_queries = [dot_plain(a, k) for a, k in zip(grad_scores, keys)]
        grad_keys = [pick_heads(dot_first(a, q)) for a, q in zip(grad_scores, queries)]
        grad_qkv = [join(kind).astype(BF16) for kind in (grad_queries, grad_keys, grad_values)]
        grad_normed_one = jnp.zeros_like(resid)
        for j in range(3):
            grad_normed_one += dot_plain(grad_qkv[j], qkv_rows(j))
            add_grad(j * part, scale * dot_first(grad_qkv[j], normed_one))
        grad_normed_one = scale * grad_normed_one
        add_small(35, scale * col_sum(grad_qkv[0].astype(F32)))
        add_small(36, scale * col_sum(grad_qkv[2].astype(F32)))
        dres = grad_after + norm_back(grad_normed_one, unit_one, factor_one, param(29))
        add_small(29, col_sum(grad_normed_one * unit_one))
        add_small(30, col_sum(grad_normed_one))
        add_small(27, col_sum(dres * bn_norm))
        add_small(28, col_sum(dres))
        input_grad_ref[there, :] = dres
        for s in range(rows // block):

            @pl.when(it == s)
            def _(s=s):
                out_copy(output_ref, s, s * block, block).start()

        return carry

    lax.fori_loop(0, rows // row_block, row_step, 0)

    to_tile(back_tile, [small_ref[27:28], small_ref[28:29]])
    send_to_all(lambda other: back_tile, back_landed, back_send, back_recv, count, parts, me)
    keep_at = {}
    for i, (order, _, _, _) in enumerate(streams):
        keep_at[i, 0] = 0
        for t, bit in enumerate(bits_of(depth, order)):
            half = row_count >> (t + 1)
            keep_at[i, t + 1] = keep_at[i, t] + lax.rem(row_rank // (1 << bit), 2) * half

    def give_at(i, t):
        return 2 * keep_at[i, t] + (row_count >> (t + 1)) - keep_at[i, t + 1]

    def slots_of(i):
        return pl.ds(streams[i][1], streams[i][2])

    def tile_at(i, c, p):
        order, slot, _, _ = streams[i]
        owner = 0
        for t, bit in enumerate(bits_of(depth, order)):
            owner = owner + lax.rem(p // (1 << (depth - 1 - t)), 2) * (1 << bit)
        return slot_ref[owner * cap + slot + c]

    def pair_copy(i):
        part = slots_of(i)
        return swap_copy(
            staged.at[part], pair_in.at[part], pair_send.at[i], pair_recv.at[i], other_core
        )

    def pair_start(i):
        for c in range(streams[i][2]):

            def body(p, carry, c=c):
                index = tile_at(i, c, p)
                value = stack_grad[1 - part_rank, jnp.maximum(index, 0)].astype(BF16)
                staged[streams[i][1] + c, p] = jnp.where(index >= 0, value, jnp.zeros_like(value))
                return carry

            lax.fori_loop(0, row_count, body, 0, unroll=8)
        pair_copy(i).start()

    def tree_copy(i, t):
        order = streams[i][0]
        half = row_count >> (t + 1)
        part = pl.ds(row_count - (row_count >> t), half)
        here = slots_of(i)
        return swap_copy(
            staged.at[here, part], arrived.at[here, part], tree_send.at[i, t], tree_recv.at[i, t],
            (flip(row_rank, bits_of(depth, order)[t]), part_rank),
        )

    def pair_end(i):
        pair_copy(i).wait()
        _, slot, size, _ = streams[i]

        def value_at(c, p):
            index = tile_at(i, c, p)
            value = stack_grad[part_rank, jnp.maximum(index, 0)]
            return jnp.where(index >= 0, value, 0.0) + pair_in[slot + c, p].astype(F32)

        for c in range(size):

            def give(p, carry, c=c):
                staged[slot + c, p] = value_at(c, give_at(i, 0) + p).astype(BF16)
                return carry

            lax.fori_loop(0, row_count // 2, give, 0, unroll=8)
        tree_copy(i, 0).start()
        for c in range(size):

            def keep(p, carry, c=c):
                sums[slot + c, keep_at[i, 1] + p] = value_at(c, keep_at[i, 1] + p)
                return carry

            lax.fori_loop(0, row_count // 2, keep, 0, unroll=8)

    def tree_step(i, t):
        came = row_count - (row_count >> t)
        tree_copy(i, t).wait()
        low = keep_at[i, t + 1]
        here = slots_of(i)

        def values(k, size):
            return sums[here, pl.ds(k, size)] + arrived[here, pl.ds(came + k - low, size)].astype(F32)

        if t + 1 < depth:
            half = row_count >> (t + 2)
            at = row_count - (row_count >> (t + 1))
            staged[here, at : at + half] = values(give_at(i, t + 1), half).astype(BF16)
            tree_copy(i, t + 1).start()
            k = keep_at[i, t + 2]
            sums[here, pl.ds(k, half)] = values(k, half)
        else:
            tile_sum[here] = values(low, 1)[:, 0]

    for i in range(wide):
        pair_start(i)
    for i in range(wide):
        pair_end(i)
    own_rows = pl.ds(pl.multiple_of(first, LANES), rows)
    await_from_all(back_tile, back_landed, back_send, back_recv, count, parts, me)
    back = add_landed(back_tile[...], back_landed, count)
    gain_mean = from_tile(back, 0, groups) * (1.0 / node_total)
    shift_mean = from_tile(back, 1, groups) * (1.0 / node_total)
    factor = params_ref[27:28] * inv_std
    grad_ref[...] = (
        factor
        * (
            input_grad_ref[own_rows, :]
            - shift_mean
            - (filt_ref[...] - centre) * inv_std * gain_mean
        )
    ).astype(BF16)

    block = back_block
    blocks = rows // block
    span = block + 2 * HALO
    has_before = me > 0
    has_after = me < count - 1

    def rim_low():
        return swap_copy(
            rim_ref.at[0], rim_in.at[1], rim_sem.at[0, 0], rim_sem.at[1, 1],
            device_of(jnp.maximum(me - 1, 0), parts),
        )

    def rim_high():
        return swap_copy(
            rim_ref.at[1], rim_in.at[0], rim_sem.at[0, 1], rim_sem.at[1, 0],
            device_of(jnp.minimum(me + 1, count - 1), parts),
        )

    def finish_rows(low, size):
        input_grad_ref[pl.ds(pl.multiple_of(first + low, LANES), size), :] += total_ref[
            HALO + low : HALO + low + size
        ]

    late = rows - block - HALO
    out_first = rows // row_block

    group = 3
    points = TAPS // group
    schedule = {}
    for i, (_, _, _, place) in enumerate(streams):
        for t in range(depth):
            due = 10 + 8 * place + 9 * t
            schedule.setdefault(min(due, blocks * points), []).append((due, t, i))

    def back_step(it, carry):
        b = lax.rem(it * (blocks - 1), blocks)
        base = pl.multiple_of(b * block, block)
        window = pl.ds(base, span)
        place = near_t[0:TAPS, pl.ds(base, block)]
        place = place + lax.broadcasted_iota(jnp.int32, place.shape, 1) // LANES * LANES
        row = lax.broadcasted_iota(jnp.int32, (span, block), 0)
        grad = grad_ref[pl.ds(base, block), :]
        for point in range(points):
            total = total_ref[window, :]
            tokens = ext_ref[window, :].astype(F32)
            for k in range(point * group, (point + 1) * group):
                hot = (place[k : k + 1, :] == row).astype(F32).astype(BF16)
                spread = dot_plain(hot, grad)
                total += spread * params_ref[k : k + 1, :]
                small_ref[k : k + 1, :] += col_sum(spread * tokens)
            total_ref[window, :] = total
            for s in range(blocks):
                if s * points + point in schedule:

                    @pl.when(it == s)
                    def _(s=s, point=point):
                        for _, t, i in sorted(schedule[s * points + point]):
                            tree_step(i, t)

        @pl.when(it == 1)
        def _():
            rim_ref[0] = total_ref[0:HALO].astype(BF16)
            rim_ref[1] = total_ref[rows + HALO : rows + 2 * HALO].astype(BF16)

            @pl.when(has_before)
            def _():
                rim_low().start()

            @pl.when(has_after)
            def _():
                rim_high().start()

        @pl.when(it == 2)
        def _():
            @pl.when(has_before)
            def _():
                rim_low().wait_send()
                rim_high().wait_recv()
                total_ref[HALO : 2 * HALO] += rim_in[0].astype(F32)

            @pl.when(has_after)
            def _():
                rim_high().wait_send()
                rim_low().wait_recv()
                total_ref[rows : rows + HALO] += rim_in[1].astype(F32)

            finish_rows(late, rows - late)
            out_copy(input_grad_ref, out_first, late, rows - late).start()

        return carry

    lax.fori_loop(0, blocks, back_step, 0)

    flat[...] = jnp.zeros_like(flat)
    for r in range(small_rows):
        row = small_ref[r : r + 1, :]
        for g in range(groups):
            at = r * groups + g
            flat[at // 8, at % 8 : at % 8 + 1, :] = row[:, g * LANES : (g + 1) * LANES]
    send_to_all(lambda other: flat.at[other], flat_in, flat_send, flat_recv, count, parts, me)
    finish_rows(0, late)
    out_copy(input_grad_ref, out_first + 1, 0, late).start()
    await_from_all(flat.at[0], flat_in, flat_send, flat_recv, count, parts, me)
    part_sum[...] = add_landed(flat[me], flat_in, count)
    send_to_all(lambda other: part_sum, flat_all, all_send, all_recv, count, parts, me)
    for _, t, i in sorted(schedule.get(blocks * points, [])):
        tree_step(i, t)
    late_copies[1].wait()
    late_copies[2].wait()
    for c in range(cap):
        index = slot_ref[row_rank * cap + c]
        new = adam_step(
            stack_ref[part_rank, jnp.maximum(index, 0)].astype(F32), tile_sum[c], tile_first_ref[0, c],
            tile_second_ref[0, c], decay_rate,
        )
        live = [jnp.where(index >= 0, a, 0.0) for a in new]
        weight_out[0, c] = live[0]
        first_out[0, c] = live[1]
        second_out[0, c] = live[2]
        low_out[0, c] = live[0].astype(BF16)
    await_from_all(part_sum, flat_all, all_send, all_recv, count, parts, me)
    flat_all[0] = part_sum[...]
    for r in range(small_rows):
        for g in range(groups):
            at = r * groups + g
            tile_from = lax.rem(at // 8 - me + count, count)
            small_ref[r : r + 1, g * LANES : (g + 1) * LANES] = flat_all[
                tile_from, at % 8 : at % 8 + 1, :
            ]
    params_out[...], small_first_out[...], small_second_out[...] = adam_step(
        params_ref[...], small_ref[...], small_first_ref[...], small_second_ref[...], 0.0
    )
    for s in range(out_first):
        out_copy(output_ref, s, s * row_block, row_block).wait()
    out_copy(input_grad_ref, out_first, late, rows - late).wait()
    out_copy(input_grad_ref, out_first + 1, 0, late).wait()


def local(
    tokens_in, neighbours, scene_lengths, window_mask, small_params, qkv_weight, proj_weight,
    fc1_weight, fc2_weight, cotangent, owners, small_first, small_second, tile_first, tile_second
):
    rows_here, width = tokens_in.shape
    row_count = lax.axis_size("rows")
    parts = lax.axis_size("heads")
    count = row_count * parts
    rows = rows_here // parts
    tile_count = owners.shape[0]
    cap = tile_first.shape[1]
    depth = row_count.bit_length() - 1
    wide = len(streams_of(cap, depth))
    filter_block, row_block, back_block = 128, 512, 256

    tile_order = jnp.arange(tile_count, dtype=jnp.int32)
    same_owner = (owners[:, None] == owners[None, :]) & (tile_order[None, :] < tile_order[:, None])
    slot_of = owners * cap + jnp.sum(same_owner.astype(jnp.int32), axis=1)
    slot_ids = jnp.arange(row_count * cap, dtype=jnp.int32)
    found = slot_of[None, :] == slot_ids[:, None]
    slot_tile = jnp.max(jnp.where(found, tile_order[None, :], -1), axis=1)

    def by_tile(weight):
        return weight.reshape(-1, BR, width)

    vmem = pl.BlockSpec(memory_space=pltpu.VMEM)
    anywhere = pl.BlockSpec(memory_space=pl.ANY)
    smem = pl.BlockSpec(memory_space=pltpu.SMEM)
    dma = pltpu.SemaphoreType.DMA
    full = jax.ShapeDtypeStruct((rows_here, width), F32)
    tiles = jax.ShapeDtypeStruct(tile_first.shape, F32)
    small = jax.ShapeDtypeStruct(small_params.shape, F32)
    by_slot = (cap, row_count, BR, width)
    exchange = [pltpu.VMEM((8, LANES), F32), pltpu.VMEM((count, 8, LANES), F32)]
    return pl.pallas_call(
        functools.partial(
            step_kernel, filter_block=filter_block, row_block=row_block, back_block=back_block,
            row_count=row_count, parts=parts, cap=cap, scenes=scene_lengths.shape[0],
        ),
        in_specs=[smem] * 2 + [anywhere] * 9 + [vmem] * 4,
        out_specs=[vmem] * 9,
        out_shape=[
            full, full, tiles, tiles, tiles, jax.ShapeDtypeStruct(tile_first.shape, BF16), small,
            small, small,
        ],
        scratch_shapes=[
            pltpu.VMEM((TAPS, rows), jnp.int32),
            pltpu.VMEM((32, rows), jnp.int32),
            pltpu.VMEM((rows + 2 * HALO, width), BF16),
            pltpu.VMEM((rows, width), F32),
            pltpu.VMEM((8, width), F32),
            pltpu.VMEM((parts, tile_count, BR, width), BF16),
            pltpu.VMEM((rows, width), F32),
            pltpu.VMEM((parts, tile_count, BR, width), F32),
            pltpu.VMEM(small_params.shape, F32),
            pltpu.VMEM((rows + 2 * HALO, width), F32),
            pltpu.VMEM((rows, width), BF16),
            pltpu.VMEM((2, HALO, width), BF16),
            pltpu.VMEM((2, HALO, width), BF16),
            pltpu.VMEM(by_slot, BF16),
            pltpu.VMEM(by_slot, BF16),
            pltpu.VMEM(by_slot, BF16),
            pltpu.VMEM(by_slot, F32),
            pltpu.VMEM((cap, BR, width), F32),
            pltpu.VMEM(tile_first.shape, F32),
            pltpu.VMEM(tile_first.shape, F32),
        ]
        + exchange
        + exchange
        + [exchange[1]] * 2
        + exchange
        + [
            dma((6,)),
            dma((2,)),
            dma((3, 4)),
            dma((count,)),
            dma((count,)),
            dma((count,)),
            dma((count,)),
            dma((wide,)),
            dma((wide,)),
            dma((wide, depth)),
            dma((wide, depth)),
            dma((2, 2)),
            dma((count,)),
            dma((count,)),
            dma((count,)),
            dma((count,)),
            dma((2, rows // row_block + 2)),
        ],
        compiler_params=pltpu.CompilerParams(
            collective_id=0, has_side_effects=True, vmem_limit_bytes=62 << 20
        ),
    )(
        scene_lengths, slot_tile, tokens_in, neighbours.T, cotangent, by_tile(qkv_weight),
        by_tile(proj_weight), by_tile(fc1_weight), by_tile(fc2_weight), tile_first, tile_second, window_mask.reshape(-1, LANES),
        small_params, small_first, small_second,
    )


def solution(mesh):
    return jax.shard_map(
        local,
        mesh=mesh,
        in_specs=(
            P("rows", None),
            P("rows", None),
            P(),
            P("rows"),
            P(),
            P(None, "heads", None),
            P("heads", None),
            P("heads", None),
            P("heads", None),
            P("rows", None),
            P(),
            P(),
            P(),
            P("heads", "rows", None, None),
            P("heads", "rows", None, None),
        ),
        out_specs=(
            P("rows", None),
            P("rows", None),
            P("heads", "rows", None, None),
            P("heads", "rows", None, None),
            P("heads", "rows", None, None),
            P("heads", "rows", None, None),
            P(),
            P(),
            P(),
        ),
        check_vma=False,
    )
```

time: 130 us -> 120 us (0.923)
  Pallas kernels: 126 us -> 107 us
  local copies, waits for them, and re-layouts: 0 us -> 10.4 us
    pallas_call x4 -> x1, Pallas kernels: 126 us -> 107 us  [local(): pl.pallas_call(functools.partial(step_kernel, filter_block=filter_block,...]
    unnamed x0 -> x25, local copies, waits for them, and re-layouts: none -> 10.4 us
where the time goes in v5:
time: 120 us
  Pallas kernels  107 us (89%)
  local copies, waits for them, and re-layouts  10.4 us (9%)
  other arithmetic  2.3 us (2%)
    pallas_call x1, Pallas kernels, local(): pl.pallas_call(functools.partial(step_kernel, filter_block=filter_block,...  107 us
    unnamed x25, local copies, waits for them, and re-layouts  10.4 us

profile of v5, /device:TPU:0, one launch (start us, length us, event | category | flops | bytes accessed | tf_op | source)
XLA Modules:
  0.0 119.9 jit_solution(15750294894063576461)
XLA Ops:
  0.6 0.9 convert_reduce_fusion
  1.6 0.7 multiply_add_fusion
  2.3 0.7 select_reduce_fusion.slot_ref
  2.9 106.5 %shard_map.214 = (f32[2048,384]{1,0:T(8,128)}, f32[2048,384]{1,0:T(8,128)}, f32[1,14,16,384]{3,2,1,0:T(8,128)}, f32[1,14,16,384]{3,2,1,0:T(8,128)}, f32[1,14,16,...) custom-call(s32[4]{0:T(128)} %lengths_ref.1, ...), custom_call_target="tpu_custom_call" | custom-call | tf_op jit(solution)/shard_map/pallas_call | solution.py:848
  109.5 0.0 copy-start
  109.5 3.9 %copy.33 = f32[2048,384]{1,0:T(8,128)} copy(f32[2048,384]{1,0:T(8,128)} %get-tuple-element.18) | data formatting | bytes 6291456
  113.4 0.0 copy-done
  113.4 0.0 copy-start.3
  113.4 0.0 copy-start.2
  113.4 0.0 copy-start.1
  113.4 0.0 copy-start.4
  113.4 0.0 copy-start.7
  113.4 0.0 copy-start.6
  113.4 0.0 copy-start.5
  113.4 1.7 %copy.34 = f32[2048,384]{1,0:T(8,128)} copy(f32[2048,384]{1,0:T(8,128)S(1)} %copy-done) | data formatting | bytes 6291456
  115.1 0.0 copy-done.3
  115.1 0.7 copy.35
  115.8 0.0 copy-done.2
  115.8 0.7 copy.36
  116.6 0.0 copy-done.1
  116.6 0.7 copy.37
  117.3 0.0 copy-done.4
  117.3 0.7 copy.38
  118.0 0.0 copy-done.7
  118.0 0.6 copy.39
  118.6 0.0 copy-done.6
  118.6 0.6 copy.40
  119.3 0.0 copy-done.5
  119.3 0.6 copy.41
Async XLA Ops:
  109.5 3.9 %copy-start = (f32[2048,384]{1,0:T(8,128)S(1)}, f32[2048,384]{1,0:T(8,128)}, u32[]{:S(2)}) copy-start(f32[2048,384]{1,0:T(8,128)} %get-tuple-element.19) | copy-start | bytes 9437188
  113.4 1.7 %copy-start.3 = (f32[1,14,16,384]{3,2,1,0:T(8,128)S(1)}, f32[1,14,16,384]{3,2,1,0:T(8,128)}, u32[]{:S(2)}) copy-start(f32[1,14,16,384]{3,2,1,0:T(8,128)} %get-tuple-element.20) | copy-start | bytes 1032196
  113.4 2.5 %copy-start.2 = (f32[1,14,16,384]{3,2,1,0:T(8,128)S(1)}, f32[1,14,16,384]{3,2,1,0:T(8,128)}, u32[]{:S(2)}) copy-start(f32[1,14,16,384]{3,2,1,0:T(8,128)} %get-tuple-element.21) | copy-start | bytes 1032196
  113.4 3.2 %copy-start.1 = (f32[1,14,16,384]{3,2,1,0:T(8,128)S(1)}, f32[1,14,16,384]{3,2,1,0:T(8,128)}, u32[]{:S(2)}) copy-start(f32[1,14,16,384]{3,2,1,0:T(8,128)} %get-tuple-element.22) | copy-start | bytes 1032196
  113.4 3.9 %copy-start.4 = (bf16[1,14,16,384]{3,2,1,0:T(8,128)(2,1)S(1)}, bf16[1,14,16,384]{3,2,1,0:T(8,128)(2,1)}, u32[]{:S(2)}) copy-start(bf16[1,14,16,384]{3,2,1,0:T(8,128)(2,1)} %get-tuple-element.23) | copy-start | bytes 516100
  113.4 4.6 %copy-start.7 = (f32[41,384]{1,0:T(8,128)S(1)}, f32[41,384]{1,0:T(8,128)}, u32[]{:S(2)}) copy-start(f32[41,384]{1,0:T(8,128)} %get-tuple-element.24) | copy-start | bytes 188932
  113.4 5.2 %copy-start.6 = (f32[41,384]{1,0:T(8,128)S(1)}, f32[41,384]{1,0:T(8,128)}, u32[]{:S(2)}) copy-start(f32[41,384]{1,0:T(8,128)} %get-tuple-element.25) | copy-start | bytes 188932
  113.4 5.8 %copy-start.5 = (f32[41,384]{1,0:T(8,128)S(1)}, f32[41,384]{1,0:T(8,128)}, u32[]{:S(2)}) copy-start(f32[41,384]{1,0:T(8,128)} %get-tuple-element.26) | copy-start | bytes 188932

commit v6 on v5

--- a/solution.py
+++ b/solution.py
@@ -181,13 +181,13 @@
 def step_kernel(
     lengths_ref, slot_ref, tokens_hbm, near_hbm, cot_hbm, qkv_hbm, proj_hbm, fc1_hbm, fc2_hbm,
     tile_first_hbm, tile_second_hbm, mask_ref, params_ref, small_first_ref, small_second_ref,
-    output_ref, input_grad_ref, weight_out, first_out, second_out, low_out, params_out,
+    output_hbm, input_grad_hbm, weight_out, first_out, second_out, low_out, params_out,
     small_first_out, small_second_out,
-    near_in, near_t, ext_ref, filt_ref, stat_ref, stack_ref, cot_ref, stack_grad, small_ref,
-    total_ref, grad_ref, rim_ref, rim_in, pair_in, staged, arrived, sums, tile_sum, tile_first_ref,
-    tile_second_ref, tile, landed, back_tile, back_landed, flat, flat_in, part_sum, flat_all,
+    output_ref, input_grad_ref, near_in, near_t, ext_ref, filt_ref, stat_ref, stack_ref, cot_ref, stack_grad, small_ref,
+    total_ref, grad_ref, rim_ref, rim_in, pair_out, pair_in, staged, arrived, sums, tile_sum, tile_first_ref,
+    tile_second_ref, tile, landed, back_tile, back_landed, flat, part_sum,
     local_sem, side_sem, weight_sem, stat_send, stat_recv, back_send, back_recv, pair_send,
-    pair_recv, tree_send, tree_recv, rim_sem, flat_send, flat_recv, all_send, all_recv, out_sem,
+    pair_recv, tree_send, tree_recv, rim_sem, flat_send, flat_recv, all_send, all_recv, out_sem, leave_sem,
     *, filter_block, row_block, back_block, row_count, parts, cap, scenes
 ):
     row_rank = lax.axis_index("rows")
@@ -413,6 +413,28 @@
     def out_copy(ref, sem, low, size):
         here = ref.at[pl.ds(pl.multiple_of(first + low, LANES), size)]
         return swap_copy(here, here, out_sem.at[0, sem], out_sem.at[1, sem], other_core)
+
+    early = 4 * part // BR
+    tile_count = stack_ref.shape[1]
+
+    def pair_copy(i):
+        tiles = pl.ds(0, early) if i == 0 else pl.ds(early, tile_count - early)
+        return swap_copy(
+            pair_out.at[tiles], pair_in.at[tiles], pair_send.at[i], pair_recv.at[i], other_core
+        )
+
+    def pair_start(i):
+        low, high = (0, early) if i == 0 else (early, tile_count)
+        pair_out[low:high] = stack_grad[1 - part_rank, low:high].astype(BF16)
+        pair_copy(i).start()
+
+    def leave(ref, hbm, sem, rank, low, size):
+        there = pl.ds(pl.multiple_of(rank * rows + low, LANES), size)
+        return pltpu.make_async_copy(ref.at[there], hbm.at[there], leave_sem.at[sem])
+
+    def leave_output(s, own):
+        rank = part_rank if own else 1 - part_rank
+        return leave(output_ref, output_hbm, 2 * s + own, rank, s * row_block, row_block)
 
     def row_step(it, carry):
         block = row_block
@@ -515,6 +537,11 @@
         output_ref[there, :] = after + (ffn + param(34))
         add_small(34, col_sum(grad_ffn.astype(F32)))
 
+        @pl.when(it == rows // row_block - 1)
+        def _():
+            pair_start(1)
+
+
         grad_after = cotangent + norm_back(grad_normed_two, unit_two, factor_two, param(31))
         add_small(31, col_sum(grad_normed_two * unit_two))
         add_small(32, col_sum(grad_normed_two))
@@ -555,11 +582,13 @@
             @pl.when(it == s)
             def _(s=s):
                 out_copy(output_ref, s, s * block, block).start()
+                leave_output(s, 1).start()
 
         return carry
 
     lax.fori_loop(0, rows // row_block, row_step, 0)
 
+    pair_start(0)
     to_tile(back_tile, [small_ref[27:28], small_ref[28:29]])
     send_to_all(lambda other: back_tile, back_landed, back_send, back_recv, count, parts, me)
     keep_at = {}
@@ -582,24 +611,6 @@
             owner = owner + lax.rem(p // (1 << (depth - 1 - t)), 2) * (1 << bit)
         return slot_ref[owner * cap + slot + c]
 
-    def pair_copy(i):
-        part = slots_of(i)
-        return swap_copy(
-            staged.at[part], pair_in.at[part], pair_send.at[i], pair_recv.at[i], other_core
-        )
-
-    def pair_start(i):
-        for c in range(streams[i][2]):
-
-            def body(p, carry, c=c):
-                index = tile_at(i, c, p)
-                value = stack_grad[1 - part_rank, jnp.maximum(index, 0)].astype(BF16)
-                staged[streams[i][1] + c, p] = jnp.where(index >= 0, value, jnp.zeros_like(value))
-                return carry
-
-            lax.fori_loop(0, row_count, body, 0, unroll=8)
-        pair_copy(i).start()
-
     def tree_copy(i, t):
         order = streams[i][0]
         half = row_count >> (t + 1)
@@ -610,14 +621,14 @@
             (flip(row_rank, bits_of(depth, order)[t]), part_rank),
         )
 
-    def pair_end(i):
-        pair_copy(i).wait()
+    def tree_first(i):
         _, slot, size, _ = streams[i]
 
         def value_at(c, p):
             index = tile_at(i, c, p)
-            value = stack_grad[part_rank, jnp.maximum(index, 0)]
-            return jnp.where(index >= 0, value, 0.0) + pair_in[slot + c, p].astype(F32)
+            at = jnp.maximum(index, 0)
+            value = stack_grad[part_rank, at] + pair_in[at].astype(F32)
+            return jnp.where(index >= 0, value, 0.0)
 
         for c in range(size):
 
@@ -654,10 +665,10 @@
         else:
             tile_sum[here] = values(low, 1)[:, 0]
 
+    pair_copy(1).wait()
+    pair_copy(0).wait()
     for i in range(wide):
-        pair_start(i)
-    for i in range(wide):
-        pair_end(i)
+        tree_first(i)
     own_rows = pl.ds(pl.multiple_of(first, LANES), rows)
     await_from_all(back_tile, back_landed, back_send, back_recv, count, parts, me)
     back = add_landed(back_tile[...], back_landed, count)
@@ -698,6 +709,14 @@
 
     late = rows - block - HALO
     out_first = rows // row_block
+
+    def leave_grad(i, own):
+        low, size = ((late, rows - late), (0, late))[i]
+        rank = part_rank if own else 1 - part_rank
+        return leave(
+            input_grad_ref, input_grad_hbm, 2 * out_first + 2 * i + own, rank, low, size
+        )
+
 
     group = 3
     points = TAPS // group
@@ -761,11 +780,13 @@
 
             finish_rows(late, rows - late)
             out_copy(input_grad_ref, out_first, late, rows - late).start()
+            leave_grad(0, 1).start()
 
         return carry
 
     lax.fori_loop(0, blocks, back_step, 0)
 
+    flat_in, flat_all = landed, back_landed
     flat[...] = jnp.zeros_like(flat)
     for r in range(small_rows):
         row = small_ref[r : r + 1, :]
@@ -775,6 +796,12 @@
     send_to_all(lambda other: flat.at[other], flat_in, flat_send, flat_recv, count, parts, me)
     finish_rows(0, late)
     out_copy(input_grad_ref, out_first + 1, 0, late).start()
+    leave_grad(1, 1).start()
+    for s in range(out_first):
+        out_copy(output_ref, s, s * row_block, row_block).wait()
+        leave_output(s, 0).start()
+    out_copy(input_grad_ref, out_first, late, rows - late).wait()
+    leave_grad(0, 0).start()
     await_from_all(flat.at[0], flat_in, flat_send, flat_recv, count, parts, me)
     part_sum[...] = add_landed(flat[me], flat_in, count)
     send_to_all(lambda other: part_sum, flat_all, all_send, all_recv, count, parts, me)
@@ -802,13 +829,54 @@
             small_ref[r : r + 1, g * LANES : (g + 1) * LANES] = flat_all[
                 tile_from, at % 8 : at % 8 + 1, :
             ]
+    out_copy(input_grad_ref, out_first + 1, 0, late).wait()
+    leave_grad(1, 0).start()
     params_out[...], small_first_out[...], small_second_out[...] = adam_step(
         params_ref[...], small_ref[...], small_first_ref[...], small_second_ref[...], 0.0
     )
     for s in range(out_first):
-        out_copy(output_ref, s, s * row_block, row_block).wait()
-    out_copy(input_grad_ref, out_first, late, rows - late).wait()
-    out_copy(input_grad_ref, out_first + 1, 0, late).wait()
+        leave_output(s, 0).wait()
+        leave_output(s, 1).wait()
+    leave_grad(0, 0).wait()
+    leave_grad(0, 1).wait()
+    leave_grad(1, 0).wait()
+    leave_grad(1, 1).wait()
+
+
+def hand_on_kernel(*refs, cuts):
+    count = len(cuts)
+    sources, landings, stages = refs[:count], refs[count : 2 * count], refs[2 * count : 3 * count]
+    sem = refs[3 * count]
+    reads, writes = [], []
+    for source, landing, stage, cut in zip(sources, landings, stages, cuts):
+        size = source.shape[0] // cut
+        for c in range(cut):
+            part = pl.ds(c * size, size)
+            i = len(reads)
+            reads.append(pltpu.make_async_copy(source.at[part], stage.at[part], sem.at[0, i]))
+            writes.append(pltpu.make_async_copy(stage.at[part], landing.at[part], sem.at[1, i]))
+    for read in reads:
+        read.start()
+    for read, write in zip(reads, writes):
+        read.wait()
+        write.start()
+    for write in writes:
+        write.wait()
+
+
+def hand_on(arrays):
+    cuts = [4 if a.shape[0] % 4 == 0 and a.size > 1 << 19 else 1 for a in arrays]
+    shapes = [jax.ShapeDtypeStruct(a.shape, a.dtype) for a in arrays]
+    anywhere = pl.BlockSpec(memory_space=pl.ANY)
+    return pl.pallas_call(
+        functools.partial(hand_on_kernel, cuts=cuts),
+        in_specs=[anywhere] * len(arrays),
+        out_specs=[anywhere] * len(arrays),
+        out_shape=shapes,
+        scratch_shapes=[pltpu.VMEM(a.shape, a.dtype) for a in arrays]
+        + [pltpu.SemaphoreType.DMA((2, sum(cuts)))],
+        compiler_params=pltpu.CompilerParams(vmem_limit_bytes=60 << 20),
+    )(*arrays)
 
 
 def local(
@@ -845,18 +913,20 @@
     small = jax.ShapeDtypeStruct(small_params.shape, F32)
     by_slot = (cap, row_count, BR, width)
     exchange = [pltpu.VMEM((8, LANES), F32), pltpu.VMEM((count, 8, LANES), F32)]
-    return pl.pallas_call(
+    results = pl.pallas_call(
         functools.partial(
             step_kernel, filter_block=filter_block, row_block=row_block, back_block=back_block,
             row_count=row_count, parts=parts, cap=cap, scenes=scene_lengths.shape[0],
         ),
         in_specs=[smem] * 2 + [anywhere] * 9 + [vmem] * 4,
-        out_specs=[vmem] * 9,
+        out_specs=[anywhere] * 2 + [vmem] * 7,
         out_shape=[
             full, full, tiles, tiles, tiles, jax.ShapeDtypeStruct(tile_first.shape, BF16), small,
             small, small,
         ],
         scratch_shapes=[
+            pltpu.VMEM((rows_here, width), F32),
+            pltpu.VMEM((rows_here, width), F32),
             pltpu.VMEM((TAPS, rows), jnp.int32),
             pltpu.VMEM((32, rows), jnp.int32),
             pltpu.VMEM((rows + 2 * HALO, width), BF16),
@@ -870,7 +940,8 @@
             pltpu.VMEM((rows, width), BF16),
             pltpu.VMEM((2, HALO, width), BF16),
             pltpu.VMEM((2, HALO, width), BF16),
-            pltpu.VMEM(by_slot, BF16),
+            pltpu.VMEM((tile_count, BR, width), BF16),
+            pltpu.VMEM((tile_count, BR, width), BF16),
             pltpu.VMEM(by_slot, BF16),
             pltpu.VMEM(by_slot, BF16),
             pltpu.VMEM(by_slot, F32),
@@ -880,8 +951,7 @@
         ]
         + exchange
         + exchange
-        + [exchange[1]] * 2
-        + exchange
+        + [exchange[1], exchange[0]]
         + [
             dma((6,)),
             dma((2,)),
@@ -890,8 +960,8 @@
             dma((count,)),
             dma((count,)),
             dma((count,)),
-            dma((wide,)),
-            dma((wide,)),
+            dma((2,)),
+            dma((2,)),
             dma((wide, depth)),
             dma((wide, depth)),
             dma((2, 2)),
@@ -900,6 +970,7 @@
             dma((count,)),
             dma((count,)),
             dma((2, rows // row_block + 2)),
+            dma((2 * (rows // row_block) + 4,)),
         ],
         compiler_params=pltpu.CompilerParams(
             collective_id=0, has_side_effects=True, vmem_limit_bytes=62 << 20
@@ -909,6 +980,7 @@
         by_tile(proj_weight), by_tile(fc1_weight), by_tile(fc2_weight), tile_first, tile_second, window_mask.reshape(-1, LANES),
         small_params, small_first, small_second,
     )
+    return hand_on(results)
 
 
 def solution(mesh):

time: 120 us -> 114 us (0.950)
  local copies, waits for them, and re-layouts: 10.4 us -> 0 us
  Pallas kernels: 107 us -> 110 us
    unnamed x25 -> x0, local copies, waits for them, and re-layouts: 10.4 us -> none
    pallas_call x0 -> x1, Pallas kernels: none -> 6.04 us  [hand_on(): pl.pallas_call(functools.partial(hand_on_kernel, cuts=cuts), in_specs=[an...]
    pallas_call x1, Pallas kernels: 107 us -> 104 us  [local(): pl.pallas_call(functools.partial(step_kernel, filter_block=filter_block,...]
where the time goes in v6:
time: 114 us
  Pallas kernels  110 us (96%)
  other arithmetic  2.3 us (2%)
    pallas_call x1, Pallas kernels, local(): pl.pallas_call(functools.partial(step_kernel, filter_block=filter_block,...  104 us
    pallas_call x1, Pallas kernels, hand_on(): pl.pallas_call(functools.partial(hand_on_kernel, cuts=cuts), in_specs=[an...  6.04 us

profile of v6, /device:TPU:0, one launch (start us, length us, event | category | flops | bytes accessed | tf_op | source)
XLA Modules:
  0.0 113.6 jit_solution(12112554629329320398)
XLA Ops:
  0.6 0.9 convert_reduce_fusion
  1.6 0.7 multiply_add_fusion
  2.3 0.7 select_reduce_fusion.slot_ref
  2.9 104.4 %shard_map.214 = (f32[2048,384]{1,0:T(8,128)}, f32[2048,384]{1,0:T(8,128)}, f32[1,14,16,384]{3,2,1,0:T(8,128)}, f32[1,14,16,384]{3,2,1,0:T(8,128)}, f32[1,14,16,...) custom-call(s32[4]{0:T(128)} %lengths_ref.1, ...), custom_call_target="tpu_custom_call" | custom-call | tf_op jit(solution)/shard_map/pallas_call | solution.py:916
  107.4 6.0 %shard_map.215 = (f32[2048,384]{1,0:T(8,128)}, f32[2048,384]{1,0:T(8,128)}, f32[1,14,16,384]{3,2,1,0:T(8,128)}, f32[1,14,16,384]{3,2,1,0:T(8,128)}, f32[1,14,16,...) custom-call(f32[2048,384]{1,0:T(8,128)} %get-tuple-element.18.refs_0, ...), custom_call_target="tpu_custom_call" | custom-call | tf_op jit(solution)/shard_map/pallas_call | solution.py:871

commit v7 on v6

--- a/solution.py
+++ b/solution.py
@@ -185,7 +185,7 @@
     small_first_out, small_second_out,
     output_ref, input_grad_ref, near_in, near_t, ext_ref, filt_ref, stat_ref, stack_ref, cot_ref, stack_grad, small_ref,
     total_ref, grad_ref, rim_ref, rim_in, pair_out, pair_in, staged, arrived, sums, tile_sum, tile_first_ref,
-    tile_second_ref, tile, landed, back_tile, back_landed, flat, part_sum,
+    tile_second_ref, tile, landed, back_tile, back_landed, small_sum,
     local_sem, side_sem, weight_sem, stat_send, stat_recv, back_send, back_recv, pair_send,
     pair_recv, tree_send, tree_recv, rim_sem, flat_send, flat_recv, all_send, all_recv, out_sem, leave_sem,
     *, filter_block, row_block, back_block, row_count, parts, cap, scenes
@@ -786,14 +786,38 @@
 
     lax.fori_loop(0, blocks, back_step, 0)
 
-    flat_in, flat_all = landed, back_landed
-    flat[...] = jnp.zeros_like(flat)
-    for r in range(small_rows):
-        row = small_ref[r : r + 1, :]
-        for g in range(groups):
-            at = r * groups + g
-            flat[at // 8, at % 8 : at % 8 + 1, :] = row[:, g * LANES : (g + 1) * LANES]
-    send_to_all(lambda other: flat.at[other], flat_in, flat_send, flat_recv, count, parts, me)
+    small_tiles = [(q, g) for q in range(small_ref.shape[0] // 8) for g in range(groups)]
+    hosts = [k * count // len(small_tiles) for k in range(len(small_tiles))]
+
+    def small_at(ref, k):
+        q, g = small_tiles[k]
+        return ref.at[q * 8 : q * 8 + 8, g * LANES : (g + 1) * LANES]
+
+    def to_host(k):
+        host = hosts[k]
+        slot = lax.rem(me - host + count, count)
+        return swap_copy(
+            small_at(small_ref, k), landed.at[slot], flat_send.at[k], flat_recv.at[slot],
+            (host // parts, host % parts),
+        )
+
+    def at_host(k, j):
+        return swap_copy(
+            small_at(small_ref, k), landed.at[j], flat_send.at[k], flat_recv.at[j], other_core
+        )
+
+    def from_host(k, j):
+        return swap_copy(
+            small_at(small_sum, k), small_at(small_sum, k), all_send.at[j], all_recv.at[k],
+            device_of(lax.rem(me + j, count), parts),
+        )
+
+    for k, host in enumerate(hosts):
+
+        @pl.when(me != host)
+        def _(k=k):
+            to_host(k).start()
+
     finish_rows(0, late)
     out_copy(input_grad_ref, out_first + 1, 0, late).start()
     leave_grad(1, 1).start()
@@ -802,9 +826,24 @@
         leave_output(s, 0).start()
     out_copy(input_grad_ref, out_first, late, rows - late).wait()
     leave_grad(0, 0).start()
-    await_from_all(flat.at[0], flat_in, flat_send, flat_recv, count, parts, me)
-    part_sum[...] = add_landed(flat[me], flat_in, count)
-    send_to_all(lambda other: part_sum, flat_all, all_send, all_recv, count, parts, me)
+    for k, host in enumerate(hosts):
+
+        @pl.when(me == host)
+        def _(k=k):
+            def wait(j, carry):
+                at_host(k, j).wait_recv()
+                return carry
+
+            lax.fori_loop(1, count, wait, 0)
+            total = small_at(small_ref, k)[...]
+            small_at(small_sum, k)[...] = add_landed(total, landed, count)
+
+            def send(j, carry):
+                from_host(k, j).start()
+                return carry
+
+            lax.fori_loop(1, count, send, 0)
+
     for _, t, i in sorted(schedule.get(blocks * points, [])):
         tree_step(i, t)
     late_copies[1].wait()
@@ -820,19 +859,25 @@
         first_out[0, c] = live[1]
         second_out[0, c] = live[2]
         low_out[0, c] = live[0].astype(BF16)
-    await_from_all(part_sum, flat_all, all_send, all_recv, count, parts, me)
-    flat_all[0] = part_sum[...]
-    for r in range(small_rows):
-        for g in range(groups):
-            at = r * groups + g
-            tile_from = lax.rem(at // 8 - me + count, count)
-            small_ref[r : r + 1, g * LANES : (g + 1) * LANES] = flat_all[
-                tile_from, at % 8 : at % 8 + 1, :
-            ]
+    for k, host in enumerate(hosts):
+
+        @pl.when(me != host)
+        def _(k=k):
+            to_host(k).wait_send()
+            from_host(k, 1).wait_recv()
+
+        @pl.when(me == host)
+        def _(k=k):
+            def sent(j, carry):
+                from_host(k, j).wait_send()
+                return carry
+
+            lax.fori_loop(1, count, sent, 0)
+
     out_copy(input_grad_ref, out_first + 1, 0, late).wait()
     leave_grad(1, 0).start()
     params_out[...], small_first_out[...], small_second_out[...] = adam_step(
-        params_ref[...], small_ref[...], small_first_ref[...], small_second_ref[...], 0.0
+        params_ref[...], small_sum[:small_rows, :], small_first_ref[...], small_second_ref[...], 0.0
     )
     for s in range(out_first):
         leave_output(s, 0).wait()
@@ -890,6 +935,7 @@
     rows = rows_here // parts
     tile_count = owners.shape[0]
     cap = tile_first.shape[1]
+    small_pad = (small_params.shape[0] + 7) // 8 * 8
     depth = row_count.bit_length() - 1
     wide = len(streams_of(cap, depth))
     filter_block, row_block, back_block = 128, 512, 256
@@ -912,6 +958,7 @@
     tiles = jax.ShapeDtypeStruct(tile_first.shape, F32)
     small = jax.ShapeDtypeStruct(small_params.shape, F32)
     by_slot = (cap, row_count, BR, width)
+    small_count = small_pad // 8 * (width // LANES)
     exchange = [pltpu.VMEM((8, LANES), F32), pltpu.VMEM((count, 8, LANES), F32)]
     results = pl.pallas_call(
         functools.partial(
@@ -935,7 +982,7 @@
             pltpu.VMEM((parts, tile_count, BR, width), BF16),
             pltpu.VMEM((rows, width), F32),
             pltpu.VMEM((parts, tile_count, BR, width), F32),
-            pltpu.VMEM(small_params.shape, F32),
+            pltpu.VMEM((small_pad, width), F32),
             pltpu.VMEM((rows + 2 * HALO, width), F32),
             pltpu.VMEM((rows, width), BF16),
             pltpu.VMEM((2, HALO, width), BF16),
@@ -951,7 +998,7 @@
         ]
         + exchange
         + exchange
-        + [exchange[1], exchange[0]]
+        + [pltpu.VMEM((small_pad, width), F32)]
         + [
             dma((6,)),
             dma((2,)),
@@ -965,10 +1012,10 @@
             dma((wide, depth)),
             dma((wide, depth)),
             dma((2, 2)),
+            dma((small_count,)),
             dma((count,)),
             dma((count,)),
-            dma((count,)),
-            dma((count,)),
+            dma((small_count,)),
             dma((2, rows // row_block + 2)),
             dma((2 * (rows // row_block) + 4,)),
         ],

time: 114 us -> 112 us (0.982)
    pallas_call x1, Pallas kernels: 104 us -> 103 us  [local(): pl.pallas_call(functools.partial(step_kernel, filter_block=filter_block,...]
where the time goes in v7:
time: 112 us
  Pallas kernels  109 us (97%)
  other arithmetic  2.3 us (2%)
    pallas_call x1, Pallas kernels, local(): pl.pallas_call(functools.partial(step_kernel, filter_block=filter_block,...  103 us
    pallas_call x1, Pallas kernels, hand_on(): pl.pallas_call(functools.partial(hand_on_kernel, cuts=cuts), in_specs=[an...  6.04 us

profile of v7, /device:TPU:0, one launch (start us, length us, event | category | flops | bytes accessed | tf_op | source)
XLA Modules:
  0.0 111.7 jit_solution(12327300365467595515)
XLA Ops:
  0.6 0.9 convert_reduce_fusion
  1.6 0.7 multiply_add_fusion
  2.3 0.7 select_reduce_fusion.slot_ref
  2.9 102.5 %shard_map.214 = (f32[2048,384]{1,0:T(8,128)}, f32[2048,384]{1,0:T(8,128)}, f32[1,14,16,384]{3,2,1,0:T(8,128)}, f32[1,14,16,384]{3,2,1,0:T(8,128)}, f32[1,14,16,...) custom-call(s32[4]{0:T(128)} %lengths_ref.1, ...), custom_call_target="tpu_custom_call" | custom-call | tf_op jit(solution)/shard_map/pallas_call | solution.py:963
  105.5 6.0 %shard_map.215 = (f32[2048,384]{1,0:T(8,128)}, f32[2048,384]{1,0:T(8,128)}, f32[1,14,16,384]{3,2,1,0:T(8,128)}, f32[1,14,16,384]{3,2,1,0:T(8,128)}, f32[1,14,16,...) custom-call(f32[2048,384]{1,0:T(8,128)} %get-tuple-element.18.refs_0, ...), custom_call_target="tpu_custom_call" | custom-call | tf_op jit(solution)/shard_map/pallas_call | solution.py:916

commit v8 on v7

--- a/solution.py
+++ b/solution.py
@@ -910,7 +910,7 @@
 
 
 def hand_on(arrays):
-    cuts = [4 if a.shape[0] % 4 == 0 and a.size > 1 << 19 else 1 for a in arrays]
+    cuts = [8 if a.shape[0] % 64 == 0 and a.size > 1 << 19 else 1 for a in arrays]
     shapes = [jax.ShapeDtypeStruct(a.shape, a.dtype) for a in arrays]
     anywhere = pl.BlockSpec(memory_space=pl.ANY)
     return pl.pallas_call(

time: 112 us -> 112 us (level)
  no operation moved by 1% of the time
where the time goes in v8:
time: 112 us
  Pallas kernels  109 us (97%)
  other arithmetic  2.3 us (2%)
    pallas_call x1, Pallas kernels, local(): pl.pallas_call(functools.partial(step_kernel, filter_block=filter_block,...  103 us
    pallas_call x1, Pallas kernels, hand_on(): pl.pallas_call(functools.partial(hand_on_kernel, cuts=cuts), in_specs=[an...  6.12 us

profile of v8, /device:TPU:0, one launch (start us, length us, event | category | flops | bytes accessed | tf_op | source)
XLA Modules:
  0.0 111.8 jit_solution(7738362560503409548)
XLA Ops:
  0.6 0.9 convert_reduce_fusion
  1.6 0.7 multiply_add_fusion
  2.3 0.7 select_reduce_fusion.slot_ref
  2.9 102.5 %shard_map.214 = (f32[2048,384]{1,0:T(8,128)}, f32[2048,384]{1,0:T(8,128)}, f32[1,14,16,384]{3,2,1,0:T(8,128)}, f32[1,14,16,384]{3,2,1,0:T(8,128)}, f32[1,14,16,...) custom-call(s32[4]{0:T(128)} %lengths_ref.1, ...), custom_call_target="tpu_custom_call" | custom-call | tf_op jit(solution)/shard_map/pallas_call | solution.py:963
  105.5 6.1 %shard_map.215 = (f32[2048,384]{1,0:T(8,128)}, f32[2048,384]{1,0:T(8,128)}, f32[1,14,16,384]{3,2,1,0:T(8,128)}, f32[1,14,16,384]{3,2,1,0:T(8,128)}, f32[1,14,16,...) custom-call(f32[2048,384]{1,0:T(8,128)} %get-tuple-element.18.refs_0, ...), custom_call_target="tpu_custom_call" | custom-call | tf_op jit(solution)/shard_map/pallas_call | solution.py:916
